TPU v7x, 32 devices: a whole 2x2x4 slice. The times are simulated.
32 devices in a mesh: dp: 2 (over x), expert: 16 (over z, y, core).
Axes of the slice: x: 2, y: 2, z: 4, core: 2. Of those that a mesh axis runs over, the one named last changes fastest.
Arguments:
- tokens: bfloat16 [4096, 1024], P(('dp', 'expert')), may hold values from -6 to 6
- cotangent: bfloat16 [4096, 1024], P(('dp', 'expert')), may hold values from -4 to 4
- expert_ids: int32 [4096, 8], P(('dp', 'expert')), may hold values from 0 to 15, all different within a row; in each aligned block of 128 rows (0 to 127, 128 to 255, ...) at most 72 rows name the same one
- gate_probs: bfloat16 [4096, 8], P(('dp', 'expert')), may hold values from 0.049804688 to 0.29882812
- w_gate: bfloat16 [16, 1024, 384], P('expert'), may hold values from -0.1875 to 0.1875
- w_up: bfloat16 [16, 1024, 384], P('expert'), may hold values from -0.1875 to 0.1875
- w_down: bfloat16 [16, 384, 1024], P('expert'), may hold values from -0.3125 to 0.3125
Outputs:
- grad_tokens: bfloat16 [4096, 1024], P(('dp', 'expert'))
- grad_probs: bfloat16 [4096, 8], P(('dp', 'expert'))
- grad_w_gate: bfloat16 [16, 1024, 384], P('expert', 'dp')
- grad_w_up: bfloat16 [16, 1024, 384], P('expert', 'dp')
- grad_w_down: bfloat16 [16, 384, 1024], P('expert', 'dp')
Inputs may be any that keep to these rules, and one draw needn't show every extreme that they name: `expert_ids`: each row names 8 different experts. Among the rows of one device no expert is named more than 72 times, and in some device's rows some expert is named exactly 72 times.
All inputs are finite; a program needn't handle non-finite values.
Results may differ from a plain program's by a relative error of at most 0.014.
Values may be sent and summed in bfloat16 or wider, within the bound.
No kernel may reach another device: no remote copies, remote signals or barrier semaphores. Data moves between devices by JAX's collectives and lax.ppermute only.
A program may use at most 64 MiB of HBM per device.

v0:
```python
import jax
import jax.numpy as jnp
from jax import lax
from jax.sharding import PartitionSpec as P


def silu_parts(gate):
    sig = jax.nn.sigmoid(gate)
    return (gate * sig, sig + gate * sig * (1.0 - sig))


def on_device(tokens, cotangent, expert_ids, gate_probs, w_gate, w_up, w_down):
    tok_dev, width = tokens.shape
    topk = expert_ids.shape[1]
    local = w_gate.shape[0]
    experts = local * lax.axis_size("expert")
    most = min(tok_dev, tok_dev * topk * 9 // (8 * experts))
    assigns = tok_dev * topk
    flat_ids = expert_ids.reshape(assigns)
    onehot = (flat_ids[:, None] == jnp.arange(experts, dtype=jnp.int32)[None, :]).astype(jnp.int32)
    ranks = jnp.cumsum(onehot, axis=0) - 1
    slots = jnp.sum(ranks * onehot, axis=1)
    target = flat_ids * most + slots
    filled = (
        jnp.full((experts * most,), assigns, jnp.int32)
        .at[target]
        .set(jnp.arange(assigns, dtype=jnp.int32))
    )
    rows_tok = filled // topk
    zero_row = jnp.zeros((1, width), jnp.bfloat16)
    x_slots = jnp.concatenate([tokens, zero_row], axis=0)[rows_tok].reshape(experts, most, width)
    dy_slots = jnp.concatenate([cotangent, zero_row], axis=0)[rows_tok].reshape(
        experts, most, width
    )
    p_flat = jnp.concatenate([gate_probs.reshape(assigns), jnp.zeros((1,), jnp.bfloat16)], axis=0)
    p_slots = p_flat[filled].reshape(experts, most)
    x_recv = lax.all_to_all(x_slots, "expert", split_axis=0, concat_axis=1, tiled=True)
    dy_recv, p_recv = (
        lax.all_to_all(dy_slots, "expert", split_axis=0, concat_axis=1, tiled=True),
        lax.all_to_all(p_slots, "expert", split_axis=0, concat_axis=1, tiled=True),
    )
    prob = p_recv.astype(jnp.float32)[:, :, None]
    gate = jnp.einsum("erd,edf->erf", x_recv, w_gate, preferred_element_type=jnp.float32)
    up = jnp.einsum("erd,edf->erf", x_recv, w_up, preferred_element_type=jnp.float32)
    act, dact = silu_parts(gate)
    hidden = (act * up).astype(jnp.bfloat16)
    scaled = (prob * dy_recv.astype(jnp.float32)).astype(jnp.bfloat16)
    grad_down_part = jnp.einsum("erf,erd->efd", hidden, scaled, preferred_element_type=jnp.float32)
    dz = jnp.einsum("erd,efd->erf", dy_recv, w_down, preferred_element_type=jnp.float32)
    gate_grad = jnp.sum(dz * hidden.astype(jnp.float32), axis=2).astype(jnp.bfloat16)
    dh = prob * dz
    d_gate = (dh * up * dact).astype(jnp.bfloat16)
    d_up = (dh * act).astype(jnp.bfloat16)
    row_grad = (
        jnp.einsum("erf,edf->erd", d_gate, w_gate, preferred_element_type=jnp.float32)
        + jnp.einsum("erf,edf->erd", d_up, w_up, preferred_element_type=jnp.float32)
    ).astype(jnp.bfloat16)
    back_rows, back_probs = (
        lax.all_to_all(row_grad, "expert", split_axis=1, concat_axis=0, tiled=True),
        lax.all_to_all(gate_grad, "expert", split_axis=1, concat_axis=0, tiled=True),
    )
    grad_gate_part = jnp.einsum("erd,erf->edf", x_recv, d_gate, preferred_element_type=jnp.float32)
    grad_up_part = jnp.einsum("erd,erf->edf", x_recv, d_up, preferred_element_type=jnp.float32)
    summed_gate, summed_up, summed_down = (
        lax.psum_scatter(
            grad_gate_part.astype(jnp.bfloat16), "dp", scatter_dimension=1, tiled=True
        ).astype(jnp.float32),
        lax.psum_scatter(
            grad_up_part.astype(jnp.bfloat16), "dp", scatter_dimension=1, tiled=True
        ).astype(jnp.float32),
        lax.psum_scatter(
            grad_down_part.astype(jnp.bfloat16), "dp", scatter_dimension=1, tiled=True
        ).astype(jnp.float32),
    )
    picked = back_rows.reshape(experts * most, width)[target].reshape(tok_dev, topk, width)
    grad_tokens = jnp.sum(picked.astype(jnp.float32), axis=1).astype(jnp.bfloat16)
    grad_probs = back_probs.reshape(experts * most)[target].reshape(tok_dev, topk)
    return (
        grad_tokens,
        grad_probs,
        summed_gate.astype(jnp.bfloat16),
        summed_up.astype(jnp.bfloat16),
        summed_down.astype(jnp.bfloat16),
    )


def solution(mesh):
    return jax.shard_map(
        on_device,
        mesh=mesh,
        in_specs=(
            P(("dp", "expert"), None),
            P(("dp", "expert"), None),
            P(("dp", "expert"), None),
            P(("dp", "expert"), None),
            P("expert", None, None),
            P("expert", None, None),
            P("expert", None, None),
        ),
        out_specs=(
            P(("dp", "expert"), None),
            P(("dp", "expert"), None),
            P("expert", "dp", None),
            P("expert", "dp", None),
            P("expert", "dp", None),
        ),
        check_vma=False,
    )
```

profile of v0, /device:TPU:13, one launch (start us, length us, event | category | flops | bytes accessed | tf_op | source)
XLA Modules:
  0.0 292.8 jit_solution(4287309075161056809)
XLA Ops:
  7.2 0.0 copy-start
  7.2 0.8 broadcast_multiply_fusion
  7.9 0.8 copy.32
  8.7 0.1 eq.29
  8.8 0.1 eq.25
  8.9 0.8 copy.30
  9.7 0.1 reshape.225
  9.8 0.1 copy.31
  9.9 0.1 mul.74
  10.0 4.5 %reduce-window.6 = s32[16,8,128]{2,1,0:T(8,128)S(1)} reduce-window(s32[16,8,128]{2,1,0:T(8,128)S(1)} %fusion.20, s32[]{:T(128)} %constant.17.clone.1), window={size=1x1x128 pad=0_0x0_0x127_0}, to_apply=%region_0.0 | reduce-window | flops 2080768 | bytes 131076 | tf_op jit(solution)/shard_map/reduce-window
  14.6 0.1 slice.18
  14.6 0.1 copy.34
  14.8 0.1 copy.35
  14.9 0.1 add_add_fusion
  15.0 4.3 %scatter_custom_fusion = s32[1152]{0:T(1024)S(1)} fusion(s32[1024]{0:T(1024)S(1)} %bitcast.73, s32[1024]{0:T(1024)S(1)} %iota.11, s32[]{:T(128)} %constant.13.clone.1), kind=kCustom, calls=%fused_computation.56 | custom fusion | bytes 4612 | tf_op jit(solution)/shard_map/scatter | solution.py:27
  19.4 7.3 %gather_fusion = bf16[1152]{0:T(1024)(128)(2,1)S(1)} fusion(bf16[1025]{0:T(1024)(128)(2,1)S(1)} %pad_maximum_fusion, s32[2048]{0:T(1024)S(1)} %get-tuple-element.27), kind=kCustom, calls=%fused_computation | custom fusion | bytes 9216 | tf_op jit(solution)/shard_map/gather | solution.py:36
  26.7 0.7 all_to_all.20
  27.4 6.6 %all-to-all-start = ((bf16[16,1,72]{2,1,0:T(2,128)(2,1)}), bf16[16,1,72]{2,1,0:T(2,128)(2,1)S(1)}, u32[]{:S(2)}, u32[]{:S(2)}) async-start(bf16[16,1,72]{2,1,0:T(2,128)(2,1)} %all_to_all.20), calls=%async_computation | async-start | bytes 16384 | tf_op jit(solution)/shard_map/all_to_all | solution.py:40
  33.9 0.0 copy-done.6
  34.0 5.0 %gather_fusion.2 = bf16[1152,1024]{1,0:T(8,128)(2,1)} fusion(bf16[129,1024]{1,0:T(8,128)(2,1)S(1)} %concatenate.11, s32[2048]{0:T(1024)S(1)} %get-tuple-element.26), kind=kCustom, calls=%fused_computation.2 | custom fusion | bytes 4723200 | tf_op jit(solution)/shard_map/gather | solution.py:31
  39.0 0.0 all-to-all-done
  39.0 6.0 %all-to-all-start.2 = ((bf16[16,72,1024]{2,1,0:T(8,128)(2,1)}), bf16[16,72,1024]{2,1,0:T(8,128)(2,1)S(1)}, u32[]{:S(2)}, u32[]{:S(2)}) async-start(bf16[16,72,1024]{2,1,0:T(8,128)(2,1)} %bitcast.7), calls=%async_computation.2 | async-start | bytes 4718592 | tf_op jit(solution)/shard_map/all_to_all | solution.py:37
  45.0 1.0 concatenate.10
  46.0 5.0 %gather_fusion.1 = bf16[1152,1024]{1,0:T(8,128)(2,1)} fusion(bf16[129,1024]{1,0:T(8,128)(2,1)S(1)} %concatenate.10, s32[2048]{0:T(1024)S(1)} %get-tuple-element.26), kind=kCustom, calls=%fused_computation.1 | custom fusion | bytes 4723200 | tf_op jit(solution)/shard_map/gather | solution.py:32
  51.0 47.1 %all-to-all-done.2 = bf16[16,72,1024]{2,1,0:T(8,128)(2,1)S(1)} async-done(((bf16[16,72,1024]{2,1,0:T(8,128)(2,1)}), bf16[16,72,1024]{2,1,0:T(8,128)(2,1)S(1)}, u32[]{:S(2)}, u32[]{:S(2)}) %all-to-all-start.2) | async-done | bytes 2359328 | tf_op jit(solution)/shard_map/all_to_all | solution.py:37
  98.0 4.9 %all-to-all-start.1 = ((bf16[16,72,1024]{2,1,0:T(8,128)(2,1)}), bf16[16,72,1024]{2,1,0:T(8,128)(2,1)}, u32[]{:S(2)}, u32[]{:S(2)}) async-start(bf16[16,72,1024]{2,1,0:T(8,128)(2,1)} %bitcast.4), calls=%async_computation.1 | async-start | bytes 4718592 | tf_op jit(solution)/shard_map/all_to_all | solution.py:39
  103.0 0.0 reduce-scatter.8.cloned.1.call-start
  103.0 0.1 reshape.238
  103.1 0.0 copy-done
  103.1 0.0 copy-start.4
  103.1 2.5 fusion.11
  105.6 0.0 copy-done.1
  105.6 0.0 copy-done.4
  105.6 2.5 fusion.14
  108.2 47.9 %all-to-all-done.1 = bf16[16,72,1024]{2,1,0:T(8,128)(2,1)} async-done(((bf16[16,72,1024]{2,1,0:T(8,128)(2,1)}), bf16[16,72,1024]{2,1,0:T(8,128)(2,1)}, u32[]{:S(2)}, u32[]{:S(2)}) %all-to-all-start.1) | async-done | bytes 2359328 | tf_op jit(solution)/shard_map/all_to_all | solution.py:39
  156.1 4.7 %multiply_reduce_fusion = (bf16[1152]{0:T(1024)(128)(2,1)S(1)}, bf16[1152,384]{0,1:T(8,128)(2,1)S(1)}, bf16[1152,384]{0,1:T(8,128)(2,1)S(1)}, bf16[1152,384]{0,1:T(8,128)(2,1)S(1)}) fusion(f32[1152,384]{0,1:T(8,128)} %fusion.14, f32[1152,384]{0,1:T(8,128)} %fusion.11, f32[1152]{0:T(1024)S(1)} %reshape.238, bf16[1152,1024]{1,0:T(8,128)(2,1)} %bitcast.5, ...), kind=kOutput, calls=%fused_computation.14 | convolution fusion | flops 913931136 | bytes 9345792 | tf_op jit(solution)/shard_map/erd,efd->erf/dot_general | solution.py:49
  160.9 4.6 %fusion.7 = bf16[1,384,1024]{2,1,0:T(8,128)(2,1)} fusion(bf16[1152,384]{0,1:T(8,128)(2,1)S(1)} %get-tuple-element.21, bf16[1152,1024]{1,0:T(8,128)(2,1)} %bitcast.5, f32[1152]{0:T(1024)S(1)} %reshape.238), kind=kOutput, calls=%fused_computation.24 | convolution fusion | flops 909901824 | bytes 4035072 | tf_op jit(solution)/shard_map/erf,erd->efd/dot_general | solution.py:48
  165.4 0.0 reduce-scatter.8.cloned.1.call-update
  165.5 0.7 convert_element_type.120
  166.2 4.9 %all-to-all-start.4 = ((bf16[1,16,72]{2,0,1:T(2,128)(2,1)}), bf16[1,16,72]{2,0,1:T(2,128)(2,1)S(1)}, u32[]{:S(2)}, u32[]{:S(2)}) async-start(bf16[1,16,72]{2,0,1:T(2,128)(2,1)} %convert_element_type.120), calls=%async_computation.4 | async-start | bytes 16384 | tf_op jit(solution)/shard_map/all_to_all | solution.py:60
  171.1 0.0 copy-start.5
  171.1 1.4 fusion.9
  172.6 1.5 fusion.1
  174.0 16.4 %copy.46 = bf16[1,1152,1024]{2,0,1:T(2,128)(2,1)} copy(bf16[1,1152,1024]{2,1,0:T(8,128)(2,1)S(1)} %fusion.1) | data formatting | bytes 4718592 | tf_op jit(solution)/shard_map/convert_element_type | solution.py:57
  190.5 0.5 broadcast.132
  191.0 14.2 %reduce.8 = bf16[1152,1024]{1,0:T(8,128)(2,1)S(1)} reduce(bf16[1152,1,1024]{2,1,0:T(2,128)(2,1)} %bitcast.64, bf16[]{:T(256)} %broadcast.132), dimensions={1}, to_apply=%bitcast.61.reduce_sub_computation | reduce | bytes 4718594
  205.2 2.8 reshape.300
  207.9 0.0 all-to-all-done.4
  208.0 6.0 %all-to-all-start.3 = ((bf16[16,2,36864]{2,1,0:T(2,128)(2,1)}), bf16[16,2,36864]{2,1,0:T(2,128)(2,1)S(1)}, u32[]{:S(2)}, u32[]{:S(2)}) async-start(bf16[16,2,36864]{2,1,0:T(2,128)(2,1)} %reshape.300), calls=%async_computation.3 | async-start | bytes 4718592 | tf_op jit(solution)/shard_map/all_to_all | solution.py:59
  214.0 0.0 reduce-scatter.6.cloned.1.call-start
  214.0 4.3 %fusion.6 = bf16[1,1024,384]{2,1,0:T(8,128)(2,1)} fusion(bf16[1152,1024]{1,0:T(8,128)(2,1)} %bitcast.68, bf16[1152,384]{0,1:T(8,128)(2,1)} %copy-done.3), kind=kOutput, calls=%fused_computation.23 | convolution fusion | flops 906362880 | bytes 4030464 | tf_op jit(solution)/shard_map/erd,erf->edf/dot_general | solution.py:63
  218.3 0.0 reduce-scatter.6.cloned.1.call-update
  218.3 0.3 reduce-scatter.4.cloned.1.call-start
  218.6 4.4 %fusion.5 = bf16[1,1024,384]{2,1,0:T(8,128)(2,1)} fusion(bf16[1152,1024]{1,0:T(8,128)(2,1)} %bitcast.69, bf16[1152,384]{0,1:T(8,128)(2,1)} %copy-done.2), kind=kOutput, calls=%fused_computation.22 | convolution fusion | flops 906362880 | bytes 4030464 | tf_op jit(solution)/shard_map/erd,erf->edf/dot_general | solution.py:62
  223.0 0.0 reduce-scatter.4.cloned.1.call-update
  223.0 0.1 reshape.236
  223.1 6.8 %gather_fusion.4 = bf16[1024]{0:T(1024)(128)(2,1)S(1)} fusion(bf16[1152]{0:T(1024)(128)(2,1)S(1)} %reshape.236, s32[1024]{0:T(1024)S(1)} %broadcast_clamp_fusion), kind=kCustom, calls=%fused_computation.4 | custom fusion | bytes 8192 | tf_op jit(solution)/shard_map/gather | solution.py:77
  229.9 0.1 reshape.237
  230.0 0.7 copy.39
  230.7 36.3 %all-to-all-done.3 = bf16[16,2,36864]{2,1,0:T(2,128)(2,1)S(1)} async-done(((bf16[16,2,36864]{2,1,0:T(2,128)(2,1)}), bf16[16,2,36864]{2,1,0:T(2,128)(2,1)S(1)}, u32[]{:S(2)}, u32[]{:S(2)}) %all-to-all-start.3) | async-done | bytes 2359328 | tf_op jit(solution)/shard_map/all_to_all | solution.py:59
  267.0 6.9 %reshape.301 = bf16[1152,1,1024]{2,1,0:T(2,128)(2,1)} reshape(bf16[16,2,36864]{2,1,0:T(2,128)(2,1)S(1)} %all-to-all-done.3) | data formatting | bytes 4718592
  274.0 3.3 %copy.45 = bf16[1,1152,1024]{2,1,0:T(8,128)(2,1)S(1)} copy(bf16[1,1152,1024]{2,0,1:T(2,128)(2,1)} %bitcast.65) | data formatting | bytes 4718592
  277.2 5.4 %gather_fusion.3 = bf16[1024,1024]{1,0:T(8,128)(2,1)} fusion(bf16[1152,1024]{1,0:T(8,128)(2,1)S(1)} %bitcast.63, s32[1024]{0:T(1024)S(1)} %broadcast_clamp_fusion), kind=kCustom, calls=%fused_computation.3 | custom fusion | bytes 4198400 | tf_op jit(solution)/shard_map/gather | solution.py:75
  282.6 3.7 %bitcast_reduce_fusion = bf16[128,1024]{1,0:T(8,128)(2,1)} fusion(bf16[1024,1024]{1,0:T(8,128)(2,1)} %gather_fusion.3), kind=kLoop, calls=%fused_computation.13 | loop fusion | flops 917504 | bytes 2359296 | tf_op jit(solution)/shard_map/reduce_sum | solution.py:76
  (23 shorter events, 0.2 us)
Async XLA Ops:
  7.2 96.0 %copy-start = (bf16[1,1024,384]{2,1,0:T(8,128)(2,1)S(1)}, bf16[1,1024,384]{2,1,0:T(8,128)(2,1)}, u32[]{:S(2)}) copy-start(bf16[1,1024,384]{2,1,0:T(8,128)(2,1)} %param.11) | copy-start | bytes 2359300
  14.6 19.3 %copy-start.6 = (bf16[128,1024]{1,0:T(8,128)(2,1)S(1)}, bf16[128,1024]{1,0:T(8,128)(2,1)}, u32[]{:S(2)}) copy-start(bf16[128,1024]{1,0:T(8,128)(2,1)} %param.7) | copy-start | bytes 786436
  27.4 11.6 %all-to-all-start = ((bf16[16,1,72]{2,1,0:T(2,128)(2,1)}), bf16[16,1,72]{2,1,0:T(2,128)(2,1)S(1)}, u32[]{:S(2)}, u32[]{:S(2)}) async-start(bf16[16,1,72]{2,1,0:T(2,128)(2,1)} %all_to_all.20), calls=%async_computation | async-start | bytes 16384 | tf_op jit(solution)/shard_map/all_to_all | solution.py:40
  39.0 59.1 %all-to-all-start.2 = ((bf16[16,72,1024]{2,1,0:T(8,128)(2,1)}), bf16[16,72,1024]{2,1,0:T(8,128)(2,1)S(1)}, u32[]{:S(2)}, u32[]{:S(2)}) async-start(bf16[16,72,1024]{2,1,0:T(8,128)(2,1)} %bitcast.7), calls=%async_computation.2 | async-start | bytes 4718592 | tf_op jit(solution)/shard_map/all_to_all | solution.py:37
  98.0 7.6 %copy-start.1 = (bf16[16,72,1024]{2,1,0:T(8,128)(2,1)}, bf16[16,72,1024]{2,1,0:T(8,128)(2,1)S(1)}, u32[]{:S(2)}) copy-start(bf16[16,72,1024]{2,1,0:T(8,128)(2,1)S(1)} %all-to-all-done.2) | copy-start | bytes 7077892
  98.0 58.1 %all-to-all-start.1 = ((bf16[16,72,1024]{2,1,0:T(8,128)(2,1)}), bf16[16,72,1024]{2,1,0:T(8,128)(2,1)}, u32[]{:S(2)}, u32[]{:S(2)}) async-start(bf16[16,72,1024]{2,1,0:T(8,128)(2,1)} %bitcast.4), calls=%async_computation.1 | async-start | bytes 4718592 | tf_op jit(solution)/shard_map/all_to_all | solution.py:39
  103.0 183.3 %reduce-scatter.8.cloned.1.call-start = ((), (), s32[]{:S(2)}) async-start(), calls=%async_computation.10 | async-start | bytes 1179648 | tf_op jit(solution)/shard_map/reduce_scatter | solution.py:71
  103.1 2.5 copy-start.4
  160.8 10.2 %copy-start.2 = (bf16[1152,384]{0,1:T(8,128)(2,1)}, bf16[1152,384]{0,1:T(8,128)(2,1)S(1)}, u32[]{:S(2)}) copy-start(bf16[1152,384]{0,1:T(8,128)(2,1)S(1)} %get-tuple-element.22) | copy-start | bytes 2654212
  160.9 11.7 %copy-start.3 = (bf16[1152,384]{0,1:T(8,128)(2,1)}, bf16[1152,384]{0,1:T(8,128)(2,1)S(1)}, u32[]{:S(2)}) copy-start(bf16[1152,384]{0,1:T(8,128)(2,1)S(1)} %get-tuple-element.23) | copy-start | bytes 2654212
  166.2 41.8 %all-to-all-start.4 = ((bf16[1,16,72]{2,0,1:T(2,128)(2,1)}), bf16[1,16,72]{2,0,1:T(2,128)(2,1)S(1)}, u32[]{:S(2)}, u32[]{:S(2)}) async-start(bf16[1,16,72]{2,0,1:T(2,128)(2,1)} %convert_element_type.120), calls=%async_computation.4 | async-start | bytes 16384 | tf_op jit(solution)/shard_map/all_to_all | solution.py:60
  171.1 1.5 copy-start.5
  208.0 59.1 %all-to-all-start.3 = ((bf16[16,2,36864]{2,1,0:T(2,128)(2,1)}), bf16[16,2,36864]{2,1,0:T(2,128)(2,1)S(1)}, u32[]{:S(2)}, u32[]{:S(2)}) async-start(bf16[16,2,36864]{2,1,0:T(2,128)(2,1)} %reshape.300), calls=%async_computation.3 | async-start | bytes 4718592 | tf_op jit(solution)/shard_map/all_to_all | solution.py:59
  214.0 72.3 %reduce-scatter.6.cloned.1.call-start = ((), (), s32[]{:S(2)}) async-start(), calls=%async_computation.9 | async-start | bytes 1179648 | tf_op jit(solution)/shard_map/reduce_scatter | solution.py:68
  218.3 68.0 %reduce-scatter.4.cloned.1.call-start = ((), (), s32[]{:S(2)}) async-start(), calls=%async_computation.8 | async-start | bytes 1179648 | tf_op jit(solution)/shard_map/reduce_scatter | solution.py:65
Sparse Core Ops, SparseCore 0:
  165.6 16.8 reduce-scatter.7
  218.4 17.9 reduce-scatter.5
  239.3 17.4 reduce-scatter.3
where the time goes:
time: 293 us
  waiting for transfers between devices  131 us (45%)
  local copies, waits for them, and re-layouts  69.4 us (24%)
  starting transfers between devices  28.7 us (10%)
  matrix products  25.9 us (9%)
  other arithmetic  23.4 us (8%)
  between operations  14 us (5%)
    all_to_all x1, waiting for transfers between devices, on_device(): lax.all_to_all(dy_slots, 'expert', split_axis=0, concat_axis=1, tiled=True)  47.9 us
    all_to_all x1, waiting for transfers between devices, on_device(): lax.all_to_all(x_slots, 'expert', split_axis=0, concat_axis=1, tiled=True)  47.1 us
    all_to_all x1, waiting for transfers between devices, on_device(): lax.all_to_all(row_grad, 'expert', split_axis=1, concat_axis=0, tiled=True)  36.3 us
    convert_element_type x1, local copies, waits for them, and re-layouts, on_device(): row_grad = (jnp.einsum('erf,edf->erd', d_gate, w_gate, preferred_element_...  16.4 us
    unnamed x21, local copies, waits for them, and re-layouts  15.8 us
    unnamed x1, other arithmetic  14.2 us
    gather x1, local copies, waits for them, and re-layouts, on_device(): p_slots = p_flat[filled].reshape(experts, most)  7.27 us
    gather x1, local copies, waits for them, and re-layouts, on_device(): back_probs.reshape(experts * most)[target].reshape(tok_dev, topk)  6.8 us
  transfers between devices with their start and end apart: 8, of which 3 were waited for; matrix products, arithmetic and copies ran while one was open for 30% of the time, Pallas kernels for 0%

commit v1 on v0

v1 whole, which is shorter than its diff:
```python
import functools

import jax
import jax.numpy as jnp
from jax import lax
from jax.experimental import pallas as pl
from jax.experimental.pallas import tpu as pltpu
from jax.sharding import PartitionSpec as P

BF16, F32 = jnp.bfloat16, jnp.float32
ROWS, LANES = 16, 128
VMEM = pl.BlockSpec(memory_space=pltpu.VMEM)
SMEM = pl.BlockSpec(memory_space=pltpu.SMEM)
PARAMS = pltpu.CompilerParams(vmem_limit_bytes=48 * 1024 * 1024)


def iota(shape, dim):
    return lax.broadcasted_iota(jnp.int32, shape, dim)


def nt(a, b):
    return lax.dot_general(a, b, (((1,), (1,)), ((), ())), preferred_element_type=F32)


def put_tiles(ref, first, value):
    rows, width = value.shape
    across = width // LANES
    for i in range(rows // ROWS):
        for j in range(across):
            ref[first + i * across + j] = value[
                i * ROWS : (i + 1) * ROWS, j * LANES : (j + 1) * LANES
            ]


def take_tiles(ref, first, dst, row, rows, width):
    across = width // LANES
    for i in range(rows // ROWS):
        for j in range(across):
            dst[row + i * ROWS : row + (i + 1) * ROWS, j * LANES : (j + 1) * LANES] = ref[
                first + i * across + j
            ]


def pack_kernel(tok_ref, cot_ref, ids_ref, prob_ref, a_ref, b_ref):
    tok_dev, width = tok_ref.shape
    half = tok_dev // 2
    block = half * width // (ROWS * LANES)
    ids, prob = ids_ref[...], prob_ref[...].astype(F32)
    for i in range(a_ref.shape[0] - 2 * block):
        expert = iota((ROWS, tok_dev), 0) + i * ROWS
        dense = jnp.zeros((ROWS, tok_dev), F32)
        for k in range(ids.shape[0]):
            dense += jnp.where(ids[k : k + 1] == expert, prob[k : k + 1], 0.0)
        a_ref[2 * block + i] = dense.astype(BF16)
        b_ref[2 * block + i] = dense.astype(BF16)
    for n, ref in enumerate((a_ref, b_ref)):
        put_tiles(ref, 0, tok_ref[n * half : (n + 1) * half])
        put_tiles(ref, block, cot_ref[n * half : (n + 1) * half])


def expert_kernel(
    me_ref,
    c0_ref,
    c1_ref,
    c2_ref,
    c3_ref,
    wg_ref,
    wu_ref,
    wd_ref,
    r0_ref,
    r1_ref,
    r2_ref,
    r3_ref,
    xt_ref,
    ht_ref,
    dgu_ref,
    sc_ref,
    x_ref,
    dy_ref,
):
    width, ff = wg_ref.shape
    chunks, grads = (c0_ref, c1_ref, c2_ref, c3_ref), (r0_ref, r1_ref, r2_ref, r3_ref)
    half = x_ref.shape[0] // 4
    block = half * width // (ROWS * LANES)
    me = me_ref[0]
    probs, eyes = [], []
    for n, ref in enumerate(chunks):
        take_tiles(ref, 0, x_ref, n * half, half, width)
        take_tiles(ref, block, dy_ref, n * half, half, width)
        row = jnp.zeros((1, LANES), F32)
        for i in range(ref.shape[0] - 2 * block):
            mine = iota((ROWS, LANES), 0) + i * ROWS == me
            row += jnp.sum(
                jnp.where(mine, ref[2 * block + i].astype(F32), 0.0), axis=0, keepdims=True
            )
        eye = iota((half, LANES), 0) + (n % 2) * half == iota((half, LANES), 1)
        probs.append(jnp.sum(jnp.where(eye, row, 0.0), axis=1, keepdims=True))
        eyes.append(eye)
    prob = jnp.concatenate(probs, axis=0)
    x, dy = x_ref[...], dy_ref[...]
    gate = jnp.dot(x, wg_ref[...], preferred_element_type=F32)
    up = jnp.dot(x, wu_ref[...], preferred_element_type=F32)
    dz = nt(dy, wd_ref[...])
    sig = jax.nn.sigmoid(gate)
    act, dact = gate * sig, sig + gate * sig * (1.0 - sig)
    hidden = (act * up).astype(BF16)
    gate_grad = jnp.sum(dz * hidden.astype(F32), axis=1, keepdims=True)
    dh = prob * dz
    d_gate = (dh * up * dact).astype(BF16)
    d_up = (dh * act).astype(BF16)
    rows = nt(d_gate, wg_ref[...]) + nt(d_up, wu_ref[...])
    for n, ref in enumerate(grads):
        put_tiles(ref, 0, rows[n * half : (n + 1) * half].astype(BF16))
        row = jnp.sum(
            jnp.where(eyes[n], gate_grad[n * half : (n + 1) * half], 0.0), axis=0, keepdims=True
        )
        for i in range(ref.shape[0] - block):
            mine = iota((ROWS, LANES), 0) + i * ROWS == me
            ref[block + i] = jnp.where(mine, row, 0.0).astype(BF16)
    dgu_ref[:, :ff] = d_gate
    dgu_ref[:, ff:] = d_up
    sc_ref[...] = (prob * dy.astype(F32)).astype(BF16)
    xt_ref[...] = x.T
    ht_ref[...] = hidden.T


def weight_kernel(groups, start, final, *refs):
    refs = refs[1:]
    in_w, in_d = (refs[:2]) if start else (None, None)
    refs = refs[2:] if start else refs
    total_w = in_w[...] if start else None
    total_d = in_d[...] if start else None
    for g in range(groups):
        xt, ht, dgu, sc = refs[4 * g : 4 * g + 4]
        w = jnp.dot(xt[...], dgu[...], preferred_element_type=F32)
        d = jnp.dot(ht[...], sc[...], preferred_element_type=F32)
        total_w = w if total_w is None else total_w + w
        total_d = d if total_d is None else total_d + d
    outs = refs[4 * groups :]
    if final:
        ff = outs[0].shape[1]
        outs[0][...] = total_w[:, :ff].astype(BF16)
        outs[1][...] = total_w[:, ff:].astype(BF16)
        outs[2][...] = total_d.astype(BF16)
    else:
        outs[0][...] = total_w
        outs[1][...] = total_d


def weight_sums(totals, groups, width, ff, part=None, parts=1, final=False):
    steps = 4 // parts
    tile_w, tile_d = width // 4, ff // 4
    first = jnp.zeros((1,), jnp.int32) if part is None else (part * steps).astype(jnp.int32)[None]
    row = lambda i, s: (s[0] + i, 0)
    whole = lambda i, s: (0, 0)
    out_row = lambda i, s: (i, 0)
    specs, args = [], []
    if totals is not None:
        specs += [pl.BlockSpec((tile_w, 2 * ff), row), pl.BlockSpec((tile_d, width), row)]
        args += list(totals)
    for xt, ht, dgu, sc in groups:
        k = xt.shape[1]
        specs += [
            pl.BlockSpec((tile_w, k), row),
            pl.BlockSpec((tile_d, k), row),
            pl.BlockSpec((k, 2 * ff), whole),
            pl.BlockSpec((k, width), whole),
        ]
        args += [xt, ht, dgu, sc]
    if final:
        blocks = ((tile_w, ff), (tile_w, ff), (tile_d, width))
        kind = BF16
    else:
        blocks = ((tile_w, 2 * ff), (tile_d, width))
        kind = F32
    rows = sum(g[0].shape[1] for g in groups)
    return pl.pallas_call(
        functools.partial(weight_kernel, len(groups), totals is not None, final),
        out_shape=tuple(jax.ShapeDtypeStruct((r * steps, c), kind) for r, c in blocks),
        grid_spec=pltpu.PrefetchScalarGridSpec(
            num_scalar_prefetch=1,
            grid=(steps,),
            in_specs=specs,
            out_specs=tuple(pl.BlockSpec(b, out_row) for b in blocks),
        ),
        compiler_params=PARAMS,
        cost_estimate=pl.CostEstimate(
            flops=6 * rows * width * ff // parts, bytes_accessed=8 * 2**20 // parts, transcendentals=0
        ),
        name="weight_sums",
    )(first, *args)


def home_kernel(count, ids_ref, *refs):
    out_ref, prob_ref = refs[2 * count :]
    tok_dev, width = out_ref.shape
    half = tok_dev // 2
    block = half * width // (ROWS * LANES)
    across = width // LANES
    sums = []
    for n in range(2):
        total = refs[n * count][...].astype(F32)
        for ref in refs[n * count + 1 : (n + 1) * count]:
            total += ref[...].astype(F32)
        for i in range(half // ROWS):
            for j in range(across):
                out_ref[
                    n * half + i * ROWS : n * half + (i + 1) * ROWS, j * LANES : (j + 1) * LANES
                ] = total[i * across + j].astype(BF16)
        sums.append(total[block:])
    by_expert = sums[0] + sums[1]
    ids = ids_ref[...]
    for k in range(ids.shape[0]):
        row = jnp.zeros((1, tok_dev), F32)
        for i in range(by_expert.shape[0]):
            expert = iota((ROWS, tok_dev), 0) + i * ROWS
            row += jnp.sum(
                jnp.where(ids[k : k + 1] == expert, by_expert[i], 0.0), axis=0, keepdims=True
            )
        prob_ref[k : k + 1] = row


def on_device(tokens, cotangent, expert_ids, gate_probs, w_gate, w_up, w_down):
    tok_dev, width = tokens.shape
    ff = w_gate.shape[2]
    half = tok_dev // 2
    devices = lax.axis_size("expert")
    groups = lax.axis_size("dp")
    experts = devices * w_gate.shape[0]
    block = half * width // (ROWS * LANES)
    extra = experts // ROWS

    chips = devices // 2
    ring = list(range(0, chips, 2)) + list(range(1, chips, 2))[::-1]
    hop = {
        d: [
            (2 * ring[i] + c, 2 * ring[(i + d) % chips] + c)
            for i in range(chips)
            for c in range(2)
        ]
        for d in (1, -1)
    }
    right = lambda v: lax.ppermute(v, "expert", hop[1])
    left = lambda v: lax.ppermute(v, "expert", hop[-1])
    swap = lambda v: lax.ppermute(v, "expert", [(i, i ^ 1) for i in range(devices)])
    full, odd = (chips - 1) // 2, chips % 2 == 0

    me = lax.axis_index("expert").astype(jnp.int32)[None]
    ids_t, probs_t = expert_ids.T, gate_probs.T
    wg, wu, wd = w_gate[0], w_up[0], w_down[0]

    chunk = jax.ShapeDtypeStruct((2 * block + extra, ROWS, LANES), BF16)
    a0, b0 = pl.pallas_call(
        pack_kernel,
        out_shape=(chunk, chunk),
        in_specs=[VMEM] * 4,
        out_specs=(VMEM, VMEM),
        compiler_params=PARAMS,
        name="pack",
    )(tokens, cotangent, ids_t, probs_t)

    grad = jax.ShapeDtypeStruct((block + extra, ROWS, LANES), BF16)

    def expert(first, second):
        rows = 4 * half
        outs = pl.pallas_call(
            expert_kernel,
            out_shape=(grad,) * 4
            + (
                jax.ShapeDtypeStruct((width, rows), BF16),
                jax.ShapeDtypeStruct((ff, rows), BF16),
                jax.ShapeDtypeStruct((rows, 2 * ff), BF16),
                jax.ShapeDtypeStruct((rows, width), BF16),
            ),
            in_specs=[SMEM] + [VMEM] * 7,
            out_specs=(VMEM,) * 8,
            scratch_shapes=[pltpu.VMEM((rows, width), BF16), pltpu.VMEM((rows, width), BF16)],
            compiler_params=PARAMS,
            cost_estimate=pl.CostEstimate(
                flops=10 * rows * width * ff, bytes_accessed=6 * 2**20, transcendentals=rows * ff
            ),
            name="expert",
        )(me, first, second, swap(first), swap(second), wg, wu, wd)
        mine = ((outs[0], swap(outs[2])), (outs[1], swap(outs[3])))
        return mine, outs[4:]

    home, group0 = expert(a0, b0)
    ra = la = a0
    rb = lb = b0
    local = {}
    group = {}
    for s in range(1, full + 1):
        ra, lb = right(ra), left(lb)
        (local["ra", s], local["lb", s]), group[s, 0] = expert(ra, lb)
        la, rb = left(la), right(rb)
        (local["la", s], local["rb", s]), group[s, 1] = expert(la, rb)
    if odd:
        ra, lb = right(ra), left(lb)
        (local["ra", full + 1], local["lb", full + 1]), group[full + 1, 0] = expert(ra, lb)

    order = [group0] + list(group.values())
    totals = None
    at = 0
    for n in range(0, len(order) - 2, 2):
        totals = weight_sums(totals, order[n : n + 2], width, ff)
        at = n + 2
    rest = order[at:]
    if groups == 2:
        here = lax.axis_index("dp")
        send = weight_sums(totals, rest, width, ff, 1 - here, 2, True)
        got = [lax.ppermute(v, "dp", [(0, 1), (1, 0)]) for v in send]
        keep = weight_sums(totals, rest, width, ff, here, 2, True)
        grads = [(a.astype(F32) + b.astype(F32)).astype(BF16) for a, b in zip(keep, got)]
    else:
        parts = weight_sums(totals, rest, width, ff, final=True)
        grads = [lax.psum_scatter(v, "dp", scatter_dimension=0, tiled=True) for v in parts]

    def add(*terms):
        return sum(t.astype(F32) for t in terms).astype(BF16)

    def back(name, first, move):
        moving = add(*local[name, first])
        for s in range(first - 1, 0, -1):
            moving = add(move(moving), *local[name, s])
        return move(moving)

    last = full + 1 if odd else full
    came_ra, came_lb = back("ra", last, left), back("lb", last, right)
    came_rb, came_la = back("rb", full, left), back("la", full, right)
    grad_tokens, grad_probs = pl.pallas_call(
        functools.partial(home_kernel, 4),
        out_shape=(
            jax.ShapeDtypeStruct((tok_dev, width), BF16),
            jax.ShapeDtypeStruct(ids_t.shape, F32),
        ),
        in_specs=[VMEM] * 9,
        out_specs=(VMEM, VMEM),
        compiler_params=PARAMS,
        name="home",
    )(ids_t, *home[0], came_ra, came_la, *home[1], came_rb, came_lb)
    return (
        grad_tokens,
        grad_probs.T.astype(BF16),
        grads[0][None],
        grads[1][None],
        grads[2][None],
    )


def solution(mesh):
    return jax.shard_map(
        on_device,
        mesh=mesh,
        in_specs=(
            P(("dp", "expert"), None),
            P(("dp", "expert"), None),
            P(("dp", "expert"), None),
            P(("dp", "expert"), None),
            P("expert", None, None),
            P("expert", None, None),
            P("expert", None, None),
        ),
        out_specs=(
            P(("dp", "expert"), None),
            P(("dp", "expert"), None),
            P("expert", "dp", None),
            P("expert", "dp", None),
            P("expert", "dp", None),
        ),
        check_vma=False,
    )
```

time: 293 us -> 165 us (0.56)
  the two profiles are of different devices: /device:TPU:13 before, /device:TPU:0 now
where the time goes in v1:
time: 165 us; the launch traced here: 164 us
  waiting for transfers between devices  52.7 us (32%)
  starting transfers between devices  43.7 us (26%)
  Pallas kernels  38 us (23%)
  local copies, waits for them, and re-layouts  24.6 us (15%)
  other arithmetic  3.89 us (2%)
    ppermute x14, starting transfers between devices, on_device(): right = lambda v: lax.ppermute(v, 'expert', hop[1])  25.2 us
    unnamed x90, local copies, waits for them, and re-layouts  24.6 us
    ppermute x14, waiting for transfers between devices, on_device(): left = lambda v: lax.ppermute(v, 'expert', hop[-1])  23.4 us
    ppermute x14, waiting for transfers between devices, on_device(): right = lambda v: lax.ppermute(v, 'expert', hop[1])  19.1 us
    pallas_call x5, Pallas kernels, weight_sums(): pl.pallas_call(functools.partial(weight_kernel, len(groups), totals is no...  18.6 us
    pallas_call x8, Pallas kernels, expert(): pl.pallas_call(expert_kernel, out_shape=(grad,) * 4 + (jax.ShapeDtypeStru...  18.4 us
    ppermute x14, starting transfers between devices, on_device(): left = lambda v: lax.ppermute(v, 'expert', hop[-1])  7.6 us
    ppermute x3, waiting for transfers between devices, on_device(): got = [lax.ppermute(v, 'dp', [(0, 1), (1, 0)]) for v in send]  6.78 us
  transfers between devices with their start and end apart: 63, of which 23 were waited for; matrix products, arithmetic and copies ran while one was open for 2% of the time, Pallas kernels for 23%

profile of v1, /device:TPU:0, one launch (start us, length us, event | category | flops | bytes accessed | tf_op | source)
XLA Modules:
  0.0 164.0 jit_solution(7094714828516215854)
XLA Ops:
  0.6 0.9 copy-done.2
  1.6 0.9 copy-done.3
  4.0 3.1 %collective-permute-start.3 = (bf16[65,16,128]{2,1,0:T(8,128)(2,1)S(1)}, bf16[65,16,128]{2,1,0:T(8,128)(2,1)S(1)}, u32[]{:S(2)}, u32[]{:S(2)}) collective-permute-start(bf16[65,16,128]{2,1,0:T(8,128)(2,1)S(1)} %get-tuple-element.85.c0_ref), channel_id=1, source_target_pairs={{0,4},{1,5},{4,8},{5,9},{8,12},{9,13},{12,14},{13,15},{14,10},{15,... | collective-permute-start | bytes 798728 | tf_op jit(solution)/shard_map/ppermute | solution.py:243
  7.6 2.0 %collective-permute-start.27 = (bf16[65,16,128]{2,1,0:T(8,128)(2,1)S(1)}, bf16[65,16,128]{2,1,0:T(8,128)(2,1)S(1)}, u32[]{:S(2)}, u32[]{:S(2)}) collective-permute-start(bf16[65,16,128]{2,1,0:T(8,128)(2,1)S(1)} %get-tuple-element.85.c0_ref), channel_id=1, source_target_pairs={{0,2},{1,3},{4,0},{5,1},{8,4},{9,5},{12,8},{13,9},{14,12},{15,13},... | collective-permute-start | bytes 798728 | tf_op jit(solution)/shard_map/ppermute | solution.py:244
  10.2 3.2 %collective-permute-done.3.c0_ref = bf16[65,16,128]{2,1,0:T(8,128)(2,1)S(1)} collective-permute-done((bf16[65,16,128]{2,1,0:T(8,128)(2,1)S(1)}, bf16[65,16,128]{2,1,0:T(8,128)(2,1)S(1)}, u32[]{:S(2)}, u32[]{:S(2)}) %collective-permute-start.3) | collective-permute-done | bytes 266272 | tf_op jit(solution)/shard_map/ppermute | solution.py:243
  13.4 1.8 %collective-permute-start.30 = (bf16[65,16,128]{2,1,0:T(8,128)(2,1)S(1)}, bf16[65,16,128]{2,1,0:T(8,128)(2,1)}, u32[]{:S(2)}, u32[]{:S(2)}) collective-permute-start(bf16[65,16,128]{2,1,0:T(8,128)(2,1)S(1)} %get-tuple-element.86.c1_ref), channel_id=1, source_target_pairs={{0,4},{1,5},{4,8},{5,9},{8,12},{9,13},{12,14},{13,15},{14,10},{15,... | collective-permute-start | bytes 798728 | tf_op jit(solution)/shard_map/ppermute | solution.py:243
  18.3 1.6 collective-permute-start.4
  23.7 1.9 %collective-permute-start.28 = (bf16[65,16,128]{2,1,0:T(8,128)(2,1)S(1)}, bf16[65,16,128]{2,1,0:T(8,128)(2,1)S(1)}, u32[]{:S(2)}, u32[]{:S(2)}) collective-permute-start(bf16[65,16,128]{2,1,0:T(8,128)(2,1)S(1)} %collective-permute-done.27.c0_ref), channel_id=1, source_target_pairs={{0,2},{1,3},{4,0},{5,1},{8,4},{9,5},{12,8},{13,9},{14,12},{15,13},... | collective-permute-start | bytes 798728 | tf_op jit(solution)/shard_map/ppermute | solution.py:244
  25.6 1.1 collective-permute-done.4.c0_ref
  26.7 1.5 collective-permute-start.31
  28.2 1.8 %collective-permute-done.8.c1_ref = bf16[65,16,128]{2,1,0:T(8,128)(2,1)} collective-permute-done((bf16[65,16,128]{2,1,0:T(8,128)(2,1)S(1)}, bf16[65,16,128]{2,1,0:T(8,128)(2,1)}, u32[]{:S(2)}, u32[]{:S(2)}) %collective-permute-start.8) | collective-permute-done | bytes 266272 | tf_op jit(solution)/shard_map/ppermute | solution.py:244
  31.9 1.6 collective-permute-start.5
  33.5 1.1 copy-done.7
  34.7 1.1 copy-done.9
  35.8 1.1 copy-done.11
  36.9 0.9 copy-done.20
  37.9 0.9 copy-done.22
  38.8 0.9 copy-done.30
  39.8 0.9 copy-done.34
  40.8 2.5 %expert.8 = (bf16[33,16,128]{2,1,0:T(8,128)(2,1)S(1)}, bf16[33,16,128]{2,1,0:T(8,128)(2,1)S(1)}, bf16[33,16,128]{2,1,0:T(8,128)(2,1)}, bf16[33,16,128]{2,1,0:T(8...) custom-call(s32[1]{0:T(128)} %bitcast.1.me_ref, ...), custom_call_target="tpu_custom_call" | custom-call | flops 1006632960 | bytes 6291456 | tf_op jit(solution)/shard_map/expert/pallas_call | solution.py:266
  44.4 1.6 collective-permute-start.32
  46.0 0.9 copy-done.32
  46.9 1.9 %expert.12 = (bf16[33,16,128]{2,1,0:T(8,128)(2,1)S(1)}, bf16[33,16,128]{2,1,0:T(8,128)(2,1)S(1)}, bf16[33,16,128]{2,1,0:T(8,128)(2,1)S(1)}, bf16[33,16,128]{2,1,...) custom-call(s32[1]{0:T(128)} %bitcast.1.me_ref, ...), custom_call_target="tpu_custom_call" | custom-call | flops 1006632960 | bytes 6291456 | tf_op jit(solution)/shard_map/expert/pallas_call | solution.py:266
  51.1 1.0 copy-done.14
  52.0 2.8 %expert.15 = (bf16[33,16,128]{2,1,0:T(8,128)(2,1)S(1)}, bf16[33,16,128]{2,1,0:T(8,128)(2,1)S(1)}, bf16[33,16,128]{2,1,0:T(8,128)(2,1)S(1)}, bf16[33,16,128]{2,1,...) custom-call(s32[1]{0:T(128)} %bitcast.1.me_ref, ...), custom_call_target="tpu_custom_call" | custom-call | flops 1006632960 | bytes 6291456 | tf_op jit(solution)/shard_map/expert/pallas_call | solution.py:266
  55.5 3.3 %weight_sums.5 = (f32[1024,768]{1,0:T(8,128)}, f32[384,1024]{1,0:T(8,128)S(1)}) custom-call(s32[1]{0:T(128)} %constant.13.clone.1.refs_0_, bf16[1024,256]{1,0:T(8,128)(2,1)S(1)} %get-tuple-element.121.refs_1_, bf16[384,256]{1,0:T(8,128)(2,1)S(1)} %get-tuple-element.122.refs_2_, bf16[256,768]{1,0:T(8,128)(2,1)S(1)} %get-tuple-element.123.refs_3_, ...), custom_call_target="tpu_custom_call" | custom-call | flops 1207959552 | bytes 8388608 | tf_op jit(solution)/shard_map/weight_sums/pallas_call | solution.py:177
  58.8 1.3 copy-done
  60.6 3.0 %expert.11 = (bf16[33,16,128]{2,1,0:T(8,128)(2,1)S(1)}, bf16[33,16,128]{2,1,0:T(8,128)(2,1)S(1)}, bf16[33,16,128]{2,1,0:T(8,128)(2,1)S(1)}, bf16[33,16,128]{2,1,...) custom-call(s32[1]{0:T(128)} %bitcast.1.me_ref, ...), custom_call_target="tpu_custom_call" | custom-call | flops 1006632960 | bytes 6291456 | tf_op jit(solution)/shard_map/expert/pallas_call | solution.py:266
  64.2 2.8 %expert.14 = (bf16[33,16,128]{2,1,0:T(8,128)(2,1)S(1)}, bf16[33,16,128]{2,1,0:T(8,128)(2,1)S(1)}, bf16[33,16,128]{2,1,0:T(8,128)(2,1)S(1)}, bf16[33,16,128]{2,1,...) custom-call(s32[1]{0:T(128)} %bitcast.1.me_ref, ...), custom_call_target="tpu_custom_call" | custom-call | flops 1006632960 | bytes 6291456 | tf_op jit(solution)/shard_map/expert/pallas_call | solution.py:266
  67.0 5.4 %weight_sums.6 = (f32[1024,768]{1,0:T(8,128)}, f32[384,1024]{1,0:T(8,128)S(1)}) custom-call(s32[1]{0:T(128)} %constant.13.clone.1.refs_0_, f32[1024,768]{1,0:T(8,128)} %get-tuple-element.129.refs_1_, f32[384,1024]{1,0:T(8,128)} %copy-done, bf16[1024,256]{1,0:T(8,128)(2,1)S(1)} %get-tuple-element.131.refs_3_, ...), custom_call_target="tpu_custom_call" | custom-call | flops 1207959552 | bytes 8388608 | tf_op jit(solution)/shard_map/weight_sums/pallas_call | solution.py:177
  72.5 1.3 copy-done.1
  73.7 1.6 collective-permute-start.6
  75.8 1.9 %expert.13 = (bf16[33,16,128]{2,1,0:T(8,128)(2,1)S(1)}, bf16[33,16,128]{2,1,0:T(8,128)(2,1)S(1)}, bf16[33,16,128]{2,1,0:T(8,128)(2,1)S(1)}, bf16[33,16,128]{2,1,...) custom-call(s32[1]{0:T(128)} %bitcast.1.me_ref, ...), custom_call_target="tpu_custom_call" | custom-call | flops 1006632960 | bytes 6291456 | tf_op jit(solution)/shard_map/expert/pallas_call | solution.py:266
  78.2 1.8 %expert.10 = (bf16[33,16,128]{2,1,0:T(8,128)(2,1)S(1)}, bf16[33,16,128]{2,1,0:T(8,128)(2,1)S(1)}, bf16[33,16,128]{2,1,0:T(8,128)(2,1)S(1)}, bf16[33,16,128]{2,1,...) custom-call(s32[1]{0:T(128)} %bitcast.1.me_ref, ...), custom_call_target="tpu_custom_call" | custom-call | flops 1006632960 | bytes 6291456 | tf_op jit(solution)/shard_map/expert/pallas_call | solution.py:266
  80.1 5.5 %weight_sums.7 = (f32[1024,768]{1,0:T(8,128)}, f32[384,1024]{1,0:T(8,128)S(1)}) custom-call(s32[1]{0:T(128)} %constant.13.clone.1.refs_0_, f32[1024,768]{1,0:T(8,128)} %get-tuple-element.139.refs_1_, f32[384,1024]{1,0:T(8,128)} %copy-done.1, bf16[1024,256]{1,0:T(8,128)(2,1)S(1)} %get-tuple-element.141.refs_3_, ...), custom_call_target="tpu_custom_call" | custom-call | flops 1207959552 | bytes 8388608 | tf_op jit(solution)/shard_map/weight_sums/pallas_call | solution.py:177
  87.8 1.9 %expert.9 = (bf16[33,16,128]{2,1,0:T(8,128)(2,1)S(1)}, bf16[33,16,128]{2,1,0:T(8,128)(2,1)S(1)}, bf16[33,16,128]{2,1,0:T(8,128)(2,1)S(1)}, bf16[33,16,128]{2,1,0...) custom-call(s32[1]{0:T(128)} %bitcast.1.me_ref, ...), custom_call_target="tpu_custom_call" | custom-call | flops 1006632960 | bytes 6291456 | tf_op jit(solution)/shard_map/expert/pallas_call | solution.py:266
  89.6 2.2 %weight_sums.8 = (bf16[512,384]{1,0:T(8,128)(2,1)S(1)}, bf16[512,384]{1,0:T(8,128)(2,1)S(1)}, bf16[192,1024]{1,0:T(8,128)(2,1)S(1)}) custom-call(s32[1]{0:T(128)} %bitcast.7.refs_0_, f32[1024,768]{1,0:T(8,128)} %get-tuple-element.149.refs_1_, f32[384,1024]{1,0:T(8,128)S(1)} %get-tuple-element.150.refs_2_, bf16[1024,256]{1,0:T(8,128)(2,1)S(1)} %get-tuple-element.151.refs_3_, ...), custom_call_target="tpu_custom_call" | custom-call | flops 603979776 | bytes 4194304 | tf_op jit(solution)/shard_map/weight_sums/pallas_call | solution.py:177
  91.9 2.3 %weight_sums.9 = (bf16[512,384]{1,0:T(8,128)(2,1)S(1)}, bf16[512,384]{1,0:T(8,128)(2,1)S(1)}, bf16[192,1024]{1,0:T(8,128)(2,1)S(1)}) custom-call(s32[1]{0:T(128)} %bitcast.8.refs_0_, f32[1024,768]{1,0:T(8,128)} %get-tuple-element.149.refs_1_, f32[384,1024]{1,0:T(8,128)S(1)} %get-tuple-element.150.refs_2_, bf16[1024,256]{1,0:T(8,128)(2,1)S(1)} %get-tuple-element.151.refs_3_, ...), custom_call_target="tpu_custom_call" | custom-call | flops 603979776 | bytes 4194304 | tf_op jit(solution)/shard_map/weight_sums/pallas_call | solution.py:177
  94.5 1.8 %collective-permute-start.36 = (bf16[33,16,128]{2,1,0:T(8,128)(2,1)S(1)}, bf16[33,16,128]{2,1,0:T(8,128)(2,1)S(1)}, u32[]{:S(2)}, u32[]{:S(2)}) collective-permute-start(bf16[33,16,128]{2,1,0:T(8,128)(2,1)S(1)} %add_convert_fusion.12), channel_id=1, source_target_pairs={{0,4},{1,5},{4,8},{5,9},{8,12},{9,13},{12,14},{13,15},{14,10},{15,... | collective-permute-start | bytes 405512 | tf_op jit(solution)/shard_map/ppermute | solution.py:243
  96.5 3.7 %collective-permute-done.36 = bf16[33,16,128]{2,1,0:T(8,128)(2,1)S(1)} collective-permute-done((bf16[33,16,128]{2,1,0:T(8,128)(2,1)S(1)}, bf16[33,16,128]{2,1,0:T(8,128)(2,1)S(1)}, u32[]{:S(2)}, u32[]{:S(2)}) %collective-permute-start.36) | collective-permute-done | bytes 135200 | tf_op jit(solution)/shard_map/ppermute | solution.py:243
  100.3 1.3 collective-permute-done.52
  101.8 1.2 collective-permute-done.13
  103.2 5.6 %collective-permute-done.49 = bf16[33,16,128]{2,1,0:T(8,128)(2,1)S(1)} collective-permute-done((bf16[33,16,128]{2,1,0:T(8,128)(2,1)S(1)}, bf16[33,16,128]{2,1,0:T(8,128)(2,1)S(1)}, u32[]{:S(2)}, u32[]{:S(2)}) %collective-permute-start.49) | collective-permute-done | bytes 135200 | tf_op jit(solution)/shard_map/ppermute | solution.py:244
  108.8 1.7 %collective-permute-start.40 = (bf16[33,16,128]{2,1,0:T(8,128)(2,1)S(1)}, bf16[33,16,128]{2,1,0:T(8,128)(2,1)S(1)}, u32[]{:S(2)}, u32[]{:S(2)}) collective-permute-start(bf16[33,16,128]{2,1,0:T(8,128)(2,1)S(1)} %add_convert_fusion.11), channel_id=1, source_target_pairs={{0,4},{1,5},{4,8},{5,9},{8,12},{9,13},{12,14},{13,15},{14,10},{15,... | collective-permute-start | bytes 405512 | tf_op jit(solution)/shard_map/ppermute | solution.py:243
  110.7 3.1 %collective-permute-done.40 = bf16[33,16,128]{2,1,0:T(8,128)(2,1)S(1)} collective-permute-done((bf16[33,16,128]{2,1,0:T(8,128)(2,1)S(1)}, bf16[33,16,128]{2,1,0:T(8,128)(2,1)S(1)}, u32[]{:S(2)}, u32[]{:S(2)}) %collective-permute-start.40) | collective-permute-done | bytes 135200 | tf_op jit(solution)/shard_map/ppermute | solution.py:243
  113.8 1.7 %collective-permute-start.53 = (bf16[33,16,128]{2,1,0:T(8,128)(2,1)S(1)}, bf16[33,16,128]{2,1,0:T(8,128)(2,1)S(1)}, u32[]{:S(2)}, u32[]{:S(2)}) collective-permute-start(bf16[33,16,128]{2,1,0:T(8,128)(2,1)S(1)} %add_convert_fusion.6), channel_id=1, source_target_pairs={{0,4},{1,5},{4,8},{5,9},{8,12},{9,13},{12,14},{13,15},{14,10},{15,... | collective-permute-start | bytes 405512 | tf_op jit(solution)/shard_map/ppermute | solution.py:243
  115.6 1.5 collective-permute-start.62
  117.1 1.7 %collective-permute-done.53 = bf16[33,16,128]{2,1,0:T(8,128)(2,1)S(1)} collective-permute-done((bf16[33,16,128]{2,1,0:T(8,128)(2,1)S(1)}, bf16[33,16,128]{2,1,0:T(8,128)(2,1)S(1)}, u32[]{:S(2)}, u32[]{:S(2)}) %collective-permute-start.53) | collective-permute-done | bytes 135200 | tf_op jit(solution)/shard_map/ppermute | solution.py:243
  119.1 4.8 %collective-permute-done.14 = bf16[33,16,128]{2,1,0:T(8,128)(2,1)S(1)} collective-permute-done((bf16[33,16,128]{2,1,0:T(8,128)(2,1)S(1)}, bf16[33,16,128]{2,1,0:T(8,128)(2,1)S(1)}, u32[]{:S(2)}, u32[]{:S(2)}) %collective-permute-start.14) | collective-permute-done | bytes 135200 | tf_op jit(solution)/shard_map/ppermute | solution.py:244
  123.8 1.4 collective-permute-start.61
  125.3 0.9 collective-permute-done.62
  126.3 0.9 fusion.2
  127.2 5.8 %collective-permute-done.61 = bf16[512,384]{1,0:T(8,128)(2,1)S(1)} collective-permute-done((bf16[512,384]{1,0:T(8,128)(2,1)S(1)}, bf16[512,384]{1,0:T(8,128)(2,1)S(1)}, u32[]{:S(2)}, u32[]{:S(2)}) %collective-permute-start.61) | collective-permute-done | bytes 393248 | tf_op jit(solution)/shard_map/ppermute | solution.py:311
  133.0 1.6 collective-permute-start.55
  135.5 2.6 %collective-permute-done.55 = bf16[33,16,128]{2,1,0:T(8,128)(2,1)S(1)} collective-permute-done((bf16[33,16,128]{2,1,0:T(8,128)(2,1)S(1)}, bf16[33,16,128]{2,1,0:T(8,128)(2,1)S(1)}, u32[]{:S(2)}, u32[]{:S(2)}) %collective-permute-start.55) | collective-permute-done | bytes 135200 | tf_op jit(solution)/shard_map/ppermute | solution.py:243
  138.7 4.3 %collective-permute-done.18 = bf16[33,16,128]{2,1,0:T(8,128)(2,1)S(1)} collective-permute-done((bf16[33,16,128]{2,1,0:T(8,128)(2,1)S(1)}, bf16[33,16,128]{2,1,0:T(8,128)(2,1)S(1)}, u32[]{:S(2)}, u32[]{:S(2)}) %collective-permute-start.18) | collective-permute-done | bytes 135200 | tf_op jit(solution)/shard_map/ppermute | solution.py:244
  143.0 1.6 collective-permute-start.57
  144.7 1.6 collective-permute-start.60
  146.3 1.8 %collective-permute-done.57 = bf16[33,16,128]{2,1,0:T(8,128)(2,1)S(1)} collective-permute-done((bf16[33,16,128]{2,1,0:T(8,128)(2,1)S(1)}, bf16[33,16,128]{2,1,0:T(8,128)(2,1)S(1)}, u32[]{:S(2)}, u32[]{:S(2)}) %collective-permute-start.57) | collective-permute-done | bytes 135200 | tf_op jit(solution)/shard_map/ppermute | solution.py:243
  149.3 4.2 %collective-permute-done.22 = bf16[33,16,128]{2,1,0:T(8,128)(2,1)S(1)} collective-permute-done((bf16[33,16,128]{2,1,0:T(8,128)(2,1)S(1)}, bf16[33,16,128]{2,1,0:T(8,128)(2,1)S(1)}, u32[]{:S(2)}, u32[]{:S(2)}) %collective-permute-start.22) | collective-permute-done | bytes 135200 | tf_op jit(solution)/shard_map/ppermute | solution.py:244
  153.5 1.8 %collective-permute-start.44 = (bf16[33,16,128]{2,1,0:T(8,128)(2,1)S(1)}, bf16[33,16,128]{2,1,0:T(8,128)(2,1)S(1)}, u32[]{:S(2)}, u32[]{:S(2)}) collective-permute-start(bf16[33,16,128]{2,1,0:T(8,128)(2,1)S(1)} %add_convert_fusion.10), channel_id=1, source_target_pairs={{0,4},{1,5},{4,8},{5,9},{8,12},{9,13},{12,14},{13,15},{14,10},{15,... | collective-permute-start | bytes 405512 | tf_op jit(solution)/shard_map/ppermute | solution.py:243
  155.3 2.2 %collective-permute-start.59 = (bf16[33,16,128]{2,1,0:T(8,128)(2,1)S(1)}, bf16[33,16,128]{2,1,0:T(8,128)(2,1)S(1)}, u32[]{:S(2)}, u32[]{:S(2)}) collective-permute-start(bf16[33,16,128]{2,1,0:T(8,128)(2,1)S(1)} %add_convert_fusion.3), channel_id=1, source_target_pairs={{0,4},{1,5},{4,8},{5,9},{8,12},{9,13},{12,14},{13,15},{14,10},{15,... | collective-permute-start | bytes 405512 | tf_op jit(solution)/shard_map/ppermute | solution.py:243
  158.5 1.9 %collective-permute-done.59.refs_7_ = bf16[33,16,128]{2,1,0:T(8,128)(2,1)S(1)} collective-permute-done((bf16[33,16,128]{2,1,0:T(8,128)(2,1)S(1)}, bf16[33,16,128]{2,1,0:T(8,128)(2,1)S(1)}, u32[]{:S(2)}, u32[]{:S(2)}) %collective-permute-start.59) | collective-permute-done | bytes 135200 | tf_op jit(solution)/shard_map/ppermute | solution.py:243
  160.4 2.2 %collective-permute-done.26.refs_2_ = bf16[33,16,128]{2,1,0:T(8,128)(2,1)S(1)} collective-permute-done((bf16[33,16,128]{2,1,0:T(8,128)(2,1)S(1)}, bf16[33,16,128]{2,1,0:T(8,128)(2,1)S(1)}, u32[]{:S(2)}, u32[]{:S(2)}) %collective-permute-start.26) | collective-permute-done | bytes 135200 | tf_op jit(solution)/shard_map/ppermute | solution.py:244
  (185 shorter events, 26.7 us)
Async XLA Ops:
  4.0 9.4 %collective-permute-start.3 = (bf16[65,16,128]{2,1,0:T(8,128)(2,1)S(1)}, bf16[65,16,128]{2,1,0:T(8,128)(2,1)S(1)}, u32[]{:S(2)}, u32[]{:S(2)}) collective-permute-start(bf16[65,16,128]{2,1,0:T(8,128)(2,1)S(1)} %get-tuple-element.85.c0_ref), channel_id=1, source_target_pairs={{0,4},{1,5},{4,8},{5,9},{8,12},{9,13},{12,14},{13,15},{14,10},{15,... | collective-permute-start | bytes 798728 | tf_op jit(solution)/shard_map/ppermute | solution.py:243
  7.1 9.3 %collective-permute-start.7 = (bf16[65,16,128]{2,1,0:T(8,128)(2,1)S(1)}, bf16[65,16,128]{2,1,0:T(8,128)(2,1)S(1)}, u32[]{:S(2)}, u32[]{:S(2)}) collective-permute-start(bf16[65,16,128]{2,1,0:T(8,128)(2,1)S(1)} %get-tuple-element.86.c1_ref), channel_id=1, source_target_pairs={{0,2},{1,3},{4,0},{5,1},{8,4},{9,5},{12,8},{13,9},{14,12},{15,13},... | collective-permute-start | bytes 798728 | tf_op jit(solution)/shard_map/ppermute | solution.py:244
  7.1 9.3 %collective-permute-start = (bf16[65,16,128]{2,1,0:T(8,128)(2,1)S(1)}, bf16[65,16,128]{2,1,0:T(8,128)(2,1)S(1)}, u32[]{:S(2)}, u32[]{:S(2)}) collective-permute-start(bf16[65,16,128]{2,1,0:T(8,128)(2,1)S(1)} %get-tuple-element.85.c0_ref), channel_id=1, source_target_pairs={{0,1},{1,0},{2,3},{3,2},{4,5},{5,4},{6,7},{7,6},{8,9},{9,8},{10,11... | collective-permute-start | bytes 798728 | tf_op jit(solution)/shard_map/ppermute | solution.py:245
  7.1 10.5 %collective-permute-start.1 = (bf16[65,16,128]{2,1,0:T(8,128)(2,1)S(1)}, bf16[65,16,128]{2,1,0:T(8,128)(2,1)S(1)}, u32[]{:S(2)}, u32[]{:S(2)}) collective-permute-start(bf16[65,16,128]{2,1,0:T(8,128)(2,1)S(1)} %get-tuple-element.86.c1_ref), channel_id=1, source_target_pairs={{0,1},{1,0},{2,3},{3,2},{4,5},{5,4},{6,7},{7,6},{8,9},{9,8},{10,11... | collective-permute-start | bytes 798728 | tf_op jit(solution)/shard_map/ppermute | solution.py:245
  7.6 13.0 %collective-permute-start.27 = (bf16[65,16,128]{2,1,0:T(8,128)(2,1)S(1)}, bf16[65,16,128]{2,1,0:T(8,128)(2,1)S(1)}, u32[]{:S(2)}, u32[]{:S(2)}) collective-permute-start(bf16[65,16,128]{2,1,0:T(8,128)(2,1)S(1)} %get-tuple-element.85.c0_ref), channel_id=1, source_target_pairs={{0,2},{1,3},{4,0},{5,1},{8,4},{9,5},{12,8},{13,9},{14,12},{15,13},... | collective-permute-start | bytes 798728 | tf_op jit(solution)/shard_map/ppermute | solution.py:244
  13.4 8.4 %collective-permute-start.30 = (bf16[65,16,128]{2,1,0:T(8,128)(2,1)S(1)}, bf16[65,16,128]{2,1,0:T(8,128)(2,1)}, u32[]{:S(2)}, u32[]{:S(2)}) collective-permute-start(bf16[65,16,128]{2,1,0:T(8,128)(2,1)S(1)} %get-tuple-element.86.c1_ref), channel_id=1, source_target_pairs={{0,4},{1,5},{4,8},{5,9},{8,12},{9,13},{12,14},{13,15},{14,10},{15,... | collective-permute-start | bytes 798728 | tf_op jit(solution)/shard_map/ppermute | solution.py:243
  16.4 5.4 %collective-permute-start.23 = (bf16[65,16,128]{2,1,0:T(8,128)(2,1)S(1)}, bf16[65,16,128]{2,1,0:T(8,128)(2,1)S(1)}, u32[]{:S(2)}, u32[]{:S(2)}) collective-permute-start(bf16[65,16,128]{2,1,0:T(8,128)(2,1)S(1)} %collective-permute-done.3.c0_ref), channel_id=1, source_target_pairs={{0,1},{1,0},{2,3},{3,2},{4,5},{5,4},{6,7},{7,6},{8,9},{9,8},{10,11... | collective-permute-start | bytes 798728 | tf_op jit(solution)/shard_map/ppermute | solution.py:245
  17.1 5.9 %collective-permute-start.24 = (bf16[65,16,128]{2,1,0:T(8,128)(2,1)S(1)}, bf16[65,16,128]{2,1,0:T(8,128)(2,1)S(1)}, u32[]{:S(2)}, u32[]{:S(2)}) collective-permute-start(bf16[65,16,128]{2,1,0:T(8,128)(2,1)S(1)} %collective-permute-done.7.c1_ref), channel_id=1, source_target_pairs={{0,1},{1,0},{2,3},{3,2},{4,5},{5,4},{6,7},{7,6},{8,9},{9,8},{10,11... | collective-permute-start | bytes 798728 | tf_op jit(solution)/shard_map/ppermute | solution.py:245
  18.3 8.4 %collective-permute-start.4 = (bf16[65,16,128]{2,1,0:T(8,128)(2,1)S(1)}, bf16[65,16,128]{2,1,0:T(8,128)(2,1)S(1)}, u32[]{:S(2)}, u32[]{:S(2)}) collective-permute-start(bf16[65,16,128]{2,1,0:T(8,128)(2,1)S(1)} %collective-permute-done.3.c0_ref), channel_id=1, source_target_pairs={{0,4},{1,5},{4,8},{5,9},{8,12},{9,13},{12,14},{13,15},{14,10},{15,... | collective-permute-start | bytes 798728 | tf_op jit(solution)/shard_map/ppermute | solution.py:243
  20.6 9.4 %collective-permute-start.8 = (bf16[65,16,128]{2,1,0:T(8,128)(2,1)S(1)}, bf16[65,16,128]{2,1,0:T(8,128)(2,1)}, u32[]{:S(2)}, u32[]{:S(2)}) collective-permute-start(bf16[65,16,128]{2,1,0:T(8,128)(2,1)S(1)} %collective-permute-done.7.c1_ref), channel_id=1, source_target_pairs={{0,2},{1,3},{4,0},{5,1},{8,4},{9,5},{12,8},{13,9},{14,12},{15,13},... | collective-permute-start | bytes 798728 | tf_op jit(solution)/shard_map/ppermute | solution.py:244
  21.8 8.3 %collective-permute-start.41 = (bf16[65,16,128]{2,1,0:T(8,128)(2,1)S(1)}, bf16[65,16,128]{2,1,0:T(8,128)(2,1)S(1)}, u32[]{:S(2)}, u32[]{:S(2)}) collective-permute-start(bf16[65,16,128]{2,1,0:T(8,128)(2,1)S(1)} %collective-permute-done.27.c0_ref), channel_id=1, source_target_pairs={{0,1},{1,0},{2,3},{3,2},{4,5},{5,4},{6,7},{7,6},{8,9},{9,8},{10,11... | collective-permute-start | bytes 798728 | tf_op jit(solution)/shard_map/ppermute | solution.py:245
  22.5 8.8 %collective-permute-start.42 = (bf16[65,16,128]{2,1,0:T(8,128)(2,1)}, bf16[65,16,128]{2,1,0:T(8,128)(2,1)S(1)}, u32[]{:S(2)}, u32[]{:S(2)}) collective-permute-start(bf16[65,16,128]{2,1,0:T(8,128)(2,1)} %collective-permute-done.30.c1_ref), channel_id=1, source_target_pairs={{0,1},{1,0},{2,3},{3,2},{4,5},{5,4},{6,7},{7,6},{8,9},{9,8},{10,11... | collective-permute-start | bytes 798728 | tf_op jit(solution)/shard_map/ppermute | solution.py:245
  23.7 20.2 %collective-permute-start.28 = (bf16[65,16,128]{2,1,0:T(8,128)(2,1)S(1)}, bf16[65,16,128]{2,1,0:T(8,128)(2,1)S(1)}, u32[]{:S(2)}, u32[]{:S(2)}) collective-permute-start(bf16[65,16,128]{2,1,0:T(8,128)(2,1)S(1)} %collective-permute-done.27.c0_ref), channel_id=1, source_target_pairs={{0,2},{1,3},{4,0},{5,1},{8,4},{9,5},{12,8},{13,9},{14,12},{15,13},... | collective-permute-start | bytes 798728 | tf_op jit(solution)/shard_map/ppermute | solution.py:244
  26.7 17.7 %collective-permute-start.31 = (bf16[65,16,128]{2,1,0:T(8,128)(2,1)}, bf16[65,16,128]{2,1,0:T(8,128)(2,1)}, u32[]{:S(2)}, u32[]{:S(2)}) collective-permute-start(bf16[65,16,128]{2,1,0:T(8,128)(2,1)} %collective-permute-done.30.c1_ref), channel_id=1, source_target_pairs={{0,4},{1,5},{4,8},{5,9},{8,12},{9,13},{12,14},{13,15},{14,10},{15,... | collective-permute-start | bytes 798728 | tf_op jit(solution)/shard_map/ppermute | solution.py:243
  30.0 20.1 %collective-permute-start.19 = (bf16[65,16,128]{2,1,0:T(8,128)(2,1)S(1)}, bf16[65,16,128]{2,1,0:T(8,128)(2,1)}, u32[]{:S(2)}, u32[]{:S(2)}) collective-permute-start(bf16[65,16,128]{2,1,0:T(8,128)(2,1)S(1)} %collective-permute-done.4.c0_ref), channel_id=1, source_target_pairs={{0,1},{1,0},{2,3},{3,2},{4,5},{5,4},{6,7},{7,6},{8,9},{9,8},{10,11... | collective-permute-start | bytes 798728 | tf_op jit(solution)/shard_map/ppermute | solution.py:245
  30.7 19.8 %collective-permute-start.20 = (bf16[65,16,128]{2,1,0:T(8,128)(2,1)}, bf16[65,16,128]{2,1,0:T(8,128)(2,1)}, u32[]{:S(2)}, u32[]{:S(2)}) collective-permute-start(bf16[65,16,128]{2,1,0:T(8,128)(2,1)} %collective-permute-done.8.c1_ref), channel_id=1, source_target_pairs={{0,1},{1,0},{2,3},{3,2},{4,5},{5,4},{6,7},{7,6},{8,9},{9,8},{10,11... | collective-permute-start | bytes 798728 | tf_op jit(solution)/shard_map/ppermute | solution.py:245
  31.9 18.6 %collective-permute-start.5 = (bf16[65,16,128]{2,1,0:T(8,128)(2,1)S(1)}, bf16[65,16,128]{2,1,0:T(8,128)(2,1)S(1)}, u32[]{:S(2)}, u32[]{:S(2)}) collective-permute-start(bf16[65,16,128]{2,1,0:T(8,128)(2,1)S(1)} %collective-permute-done.4.c0_ref), channel_id=1, source_target_pairs={{0,4},{1,5},{4,8},{5,9},{8,12},{9,13},{12,14},{13,15},{14,10},{15,... | collective-permute-start | bytes 798728 | tf_op jit(solution)/shard_map/ppermute | solution.py:243
  43.9 16.1 %collective-permute-start.29 = (bf16[65,16,128]{2,1,0:T(8,128)(2,1)S(1)}, bf16[65,16,128]{2,1,0:T(8,128)(2,1)S(1)}, u32[]{:S(2)}, u32[]{:S(2)}) collective-permute-start(bf16[65,16,128]{2,1,0:T(8,128)(2,1)S(1)} %collective-permute-done.28.c0_ref), channel_id=1, source_target_pairs={{0,2},{1,3},{4,0},{5,1},{8,4},{9,5},{12,8},{13,9},{14,12},{15,13},... | collective-permute-start | bytes 798728 | tf_op jit(solution)/shard_map/ppermute | solution.py:244
  44.4 15.7 %collective-permute-start.32 = (bf16[65,16,128]{2,1,0:T(8,128)(2,1)}, bf16[65,16,128]{2,1,0:T(8,128)(2,1)S(1)}, u32[]{:S(2)}, u32[]{:S(2)}) collective-permute-start(bf16[65,16,128]{2,1,0:T(8,128)(2,1)} %collective-permute-done.31.c1_ref), channel_id=1, source_target_pairs={{0,4},{1,5},{4,8},{5,9},{8,12},{9,13},{12,14},{13,15},{14,10},{15,... | collective-permute-start | bytes 798728 | tf_op jit(solution)/shard_map/ppermute | solution.py:243
  50.1 13.4 %collective-permute-start.9 = (bf16[65,16,128]{2,1,0:T(8,128)(2,1)}, bf16[65,16,128]{2,1,0:T(8,128)(2,1)S(1)}, u32[]{:S(2)}, u32[]{:S(2)}) collective-permute-start(bf16[65,16,128]{2,1,0:T(8,128)(2,1)} %collective-permute-done.8.c1_ref), channel_id=1, source_target_pairs={{0,2},{1,3},{4,0},{5,1},{8,4},{9,5},{12,8},{13,9},{14,12},{15,13},... | collective-permute-start | bytes 798728 | tf_op jit(solution)/shard_map/ppermute | solution.py:244
  50.6 13.1 %collective-permute-start.37 = (bf16[65,16,128]{2,1,0:T(8,128)(2,1)S(1)}, bf16[65,16,128]{2,1,0:T(8,128)(2,1)S(1)}, u32[]{:S(2)}, u32[]{:S(2)}) collective-permute-start(bf16[65,16,128]{2,1,0:T(8,128)(2,1)S(1)} %collective-permute-done.28.c0_ref), channel_id=1, source_target_pairs={{0,1},{1,0},{2,3},{3,2},{4,5},{5,4},{6,7},{7,6},{8,9},{9,8},{10,11... | collective-permute-start | bytes 798728 | tf_op jit(solution)/shard_map/ppermute | solution.py:245
  50.6 13.5 %collective-permute-start.38 = (bf16[65,16,128]{2,1,0:T(8,128)(2,1)}, bf16[65,16,128]{2,1,0:T(8,128)(2,1)S(1)}, u32[]{:S(2)}, u32[]{:S(2)}) collective-permute-start(bf16[65,16,128]{2,1,0:T(8,128)(2,1)} %collective-permute-done.31.c1_ref), channel_id=1, source_target_pairs={{0,1},{1,0},{2,3},{3,2},{4,5},{5,4},{6,7},{7,6},{8,9},{9,8},{10,11... | collective-permute-start | bytes 798728 | tf_op jit(solution)/shard_map/ppermute | solution.py:245
  60.0 13.7 %collective-permute-start.33 = (bf16[65,16,128]{2,1,0:T(8,128)(2,1)S(1)}, bf16[65,16,128]{2,1,0:T(8,128)(2,1)S(1)}, u32[]{:S(2)}, u32[]{:S(2)}) collective-permute-start(bf16[65,16,128]{2,1,0:T(8,128)(2,1)S(1)} %collective-permute-done.29.c0_ref), channel_id=1, source_target_pairs={{0,1},{1,0},{2,3},{3,2},{4,5},{5,4},{6,7},{7,6},{8,9},{9,8},{10,11... | collective-permute-start | bytes 798728 | tf_op jit(solution)/shard_map/ppermute | solution.py:245
  60.1 15.2 %collective-permute-start.34 = (bf16[65,16,128]{2,1,0:T(8,128)(2,1)S(1)}, bf16[65,16,128]{2,1,0:T(8,128)(2,1)S(1)}, u32[]{:S(2)}, u32[]{:S(2)}) collective-permute-start(bf16[65,16,128]{2,1,0:T(8,128)(2,1)S(1)} %collective-permute-done.32.c1_ref), channel_id=1, source_target_pairs={{0,1},{1,0},{2,3},{3,2},{4,5},{5,4},{6,7},{7,6},{8,9},{9,8},{10,11... | collective-permute-start | bytes 798728 | tf_op jit(solution)/shard_map/ppermute | solution.py:245
  63.5 91.8 %collective-permute-start.2 = (bf16[33,16,128]{2,1,0:T(8,128)(2,1)}, bf16[33,16,128]{2,1,0:T(8,128)(2,1)S(1)}, u32[]{:S(2)}, u32[]{:S(2)}) collective-permute-start(bf16[33,16,128]{2,1,0:T(8,128)(2,1)} %get-tuple-element.88), channel_id=1, source_target_pairs={{0,1},{1,0},{2,3},{3,2},{4,5},{5,4},{6,7},{7,6},{8,9},{9,8},{10,11... | collective-permute-start | bytes 405512 | tf_op jit(solution)/shard_map/ppermute | solution.py:245
  63.7 13.9 %collective-permute-start.15 = (bf16[65,16,128]{2,1,0:T(8,128)(2,1)S(1)}, bf16[65,16,128]{2,1,0:T(8,128)(2,1)S(1)}, u32[]{:S(2)}, u32[]{:S(2)}) collective-permute-start(bf16[65,16,128]{2,1,0:T(8,128)(2,1)S(1)} %collective-permute-done.5.c0_ref), channel_id=1, source_target_pairs={{0,1},{1,0},{2,3},{3,2},{4,5},{5,4},{6,7},{7,6},{8,9},{9,8},{10,11... | collective-permute-start | bytes 798728 | tf_op jit(solution)/shard_map/ppermute | solution.py:245
  64.1 13.6 %collective-permute-start.16 = (bf16[65,16,128]{2,1,0:T(8,128)(2,1)S(1)}, bf16[65,16,128]{2,1,0:T(8,128)(2,1)S(1)}, u32[]{:S(2)}, u32[]{:S(2)}) collective-permute-start(bf16[65,16,128]{2,1,0:T(8,128)(2,1)S(1)} %collective-permute-done.9.c1_ref), channel_id=1, source_target_pairs={{0,1},{1,0},{2,3},{3,2},{4,5},{5,4},{6,7},{7,6},{8,9},{9,8},{10,11... | collective-permute-start | bytes 798728 | tf_op jit(solution)/shard_map/ppermute | solution.py:245
  73.7 11.8 %collective-permute-start.6 = (bf16[65,16,128]{2,1,0:T(8,128)(2,1)S(1)}, bf16[65,16,128]{2,1,0:T(8,128)(2,1)S(1)}, u32[]{:S(2)}, u32[]{:S(2)}) collective-permute-start(bf16[65,16,128]{2,1,0:T(8,128)(2,1)S(1)} %collective-permute-done.5.c0_ref), channel_id=1, source_target_pairs={{0,4},{1,5},{4,8},{5,9},{8,12},{9,13},{12,14},{13,15},{14,10},{15,... | collective-permute-start | bytes 798728 | tf_op jit(solution)/shard_map/ppermute | solution.py:243
  75.3 10.3 %collective-permute-start.10 = (bf16[65,16,128]{2,1,0:T(8,128)(2,1)S(1)}, bf16[65,16,128]{2,1,0:T(8,128)(2,1)S(1)}, u32[]{:S(2)}, u32[]{:S(2)}) collective-permute-start(bf16[65,16,128]{2,1,0:T(8,128)(2,1)S(1)} %collective-permute-done.9.c1_ref), channel_id=1, source_target_pairs={{0,2},{1,3},{4,0},{5,1},{8,4},{9,5},{12,8},{13,9},{14,12},{15,13},... | collective-permute-start | bytes 798728 | tf_op jit(solution)/shard_map/ppermute | solution.py:244
  77.7 80.8 %collective-permute-start.45 = (bf16[33,16,128]{2,1,0:T(8,128)(2,1)S(1)}, bf16[33,16,128]{2,1,0:T(8,128)(2,1)S(1)}, u32[]{:S(2)}, u32[]{:S(2)}) collective-permute-start(bf16[33,16,128]{2,1,0:T(8,128)(2,1)S(1)} %copy-done.36), channel_id=1, source_target_pairs={{0,1},{1,0},{2,3},{3,2},{4,5},{5,4},{6,7},{7,6},{8,9},{9,8},{10,11... | collective-permute-start | bytes 405512 | tf_op jit(solution)/shard_map/ppermute | solution.py:245
  77.7 8.3 %collective-permute-start.46 = (bf16[33,16,128]{2,1,0:T(8,128)(2,1)S(1)}, bf16[33,16,128]{2,1,0:T(8,128)(2,1)S(1)}, u32[]{:S(2)}, u32[]{:S(2)}) collective-permute-start(bf16[33,16,128]{2,1,0:T(8,128)(2,1)S(1)} %get-tuple-element.106), channel_id=1, source_target_pairs={{0,1},{1,0},{2,3},{3,2},{4,5},{5,4},{6,7},{7,6},{8,9},{9,8},{10,11... | collective-permute-start | bytes 405512 | tf_op jit(solution)/shard_map/ppermute | solution.py:245
  85.6 1.4 collective-permute-start.35
  85.7 1.7 %collective-permute-start.11 = (bf16[65,16,128]{2,1,0:T(8,128)(2,1)S(1)}, bf16[65,16,128]{2,1,0:T(8,128)(2,1)S(1)}, u32[]{:S(2)}, u32[]{:S(2)}) collective-permute-start(bf16[65,16,128]{2,1,0:T(8,128)(2,1)S(1)} %collective-permute-done.6.c0_ref), channel_id=1, source_target_pairs={{0,1},{1,0},{2,3},{3,2},{4,5},{5,4},{6,7},{7,6},{8,9},{9,8},{10,11... | collective-permute-start | bytes 798728 | tf_op jit(solution)/shard_map/ppermute | solution.py:245
  86.1 1.6 collective-permute-start.12
  86.9 16.1 %collective-permute-start.50 = (bf16[33,16,128]{2,1,0:T(8,128)(2,1)S(1)}, bf16[33,16,128]{2,1,0:T(8,128)(2,1)S(1)}, u32[]{:S(2)}, u32[]{:S(2)}) collective-permute-start(bf16[33,16,128]{2,1,0:T(8,128)(2,1)S(1)} %copy-done.44), channel_id=1, source_target_pairs={{0,1},{1,0},{2,3},{3,2},{4,5},{5,4},{6,7},{7,6},{8,9},{9,8},{10,11... | collective-permute-start | bytes 405512 | tf_op jit(solution)/shard_map/ppermute | solution.py:245
  87.3 6.8 %collective-permute-start.48 = (bf16[33,16,128]{2,1,0:T(8,128)(2,1)S(1)}, bf16[33,16,128]{2,1,0:T(8,128)(2,1)S(1)}, u32[]{:S(2)}, u32[]{:S(2)}) collective-permute-start(bf16[33,16,128]{2,1,0:T(8,128)(2,1)S(1)} %get-tuple-element.108), channel_id=1, source_target_pairs={{0,1},{1,0},{2,3},{3,2},{4,5},{5,4},{6,7},{7,6},{8,9},{9,8},{10,11... | collective-permute-start | bytes 405512 | tf_op jit(solution)/shard_map/ppermute | solution.py:245
  87.7 6.8 %collective-permute-start.47 = (bf16[33,16,128]{2,1,0:T(8,128)(2,1)S(1)}, bf16[33,16,128]{2,1,0:T(8,128)(2,1)S(1)}, u32[]{:S(2)}, u32[]{:S(2)}) collective-permute-start(bf16[33,16,128]{2,1,0:T(8,128)(2,1)S(1)} %add_convert_fusion.9), channel_id=1, source_target_pairs={{0,2},{1,3},{4,0},{5,1},{8,4},{9,5},{12,8},{13,9},{14,12},{15,13},... | collective-permute-start | bytes 405512 | tf_op jit(solution)/shard_map/ppermute | solution.py:244
  94.2 2.2 %collective-permute-start.39 = (bf16[33,16,128]{2,1,0:T(8,128)(2,1)S(1)}, bf16[33,16,128]{2,1,0:T(8,128)(2,1)S(1)}, u32[]{:S(2)}, u32[]{:S(2)}) collective-permute-start(bf16[33,16,128]{2,1,0:T(8,128)(2,1)S(1)} %get-tuple-element.100), channel_id=1, source_target_pairs={{0,1},{1,0},{2,3},{3,2},{4,5},{5,4},{6,7},{7,6},{8,9},{9,8},{10,11... | collective-permute-start | bytes 405512 | tf_op jit(solution)/shard_map/ppermute | solution.py:245
  94.5 5.8 %collective-permute-start.36 = (bf16[33,16,128]{2,1,0:T(8,128)(2,1)S(1)}, bf16[33,16,128]{2,1,0:T(8,128)(2,1)S(1)}, u32[]{:S(2)}, u32[]{:S(2)}) collective-permute-start(bf16[33,16,128]{2,1,0:T(8,128)(2,1)S(1)} %add_convert_fusion.12), channel_id=1, source_target_pairs={{0,4},{1,5},{4,8},{5,9},{8,12},{9,13},{12,14},{13,15},{14,10},{15,... | collective-permute-start | bytes 405512 | tf_op jit(solution)/shard_map/ppermute | solution.py:243
  96.3 14.3 %collective-permute-start.43 = (bf16[33,16,128]{2,1,0:T(8,128)(2,1)S(1)}, bf16[33,16,128]{2,1,0:T(8,128)(2,1)S(1)}, u32[]{:S(2)}, u32[]{:S(2)}) collective-permute-start(bf16[33,16,128]{2,1,0:T(8,128)(2,1)S(1)} %copy-done.42), channel_id=1, source_target_pairs={{0,1},{1,0},{2,3},{3,2},{4,5},{5,4},{6,7},{7,6},{8,9},{9,8},{10,11... | collective-permute-start | bytes 405512 | tf_op jit(solution)/shard_map/ppermute | solution.py:245
  100.2 1.4 collective-permute-start.52
  101.6 1.4 collective-permute-start.13
  102.9 5.8 %collective-permute-start.49 = (bf16[33,16,128]{2,1,0:T(8,128)(2,1)S(1)}, bf16[33,16,128]{2,1,0:T(8,128)(2,1)S(1)}, u32[]{:S(2)}, u32[]{:S(2)}) collective-permute-start(bf16[33,16,128]{2,1,0:T(8,128)(2,1)S(1)} %add_convert_fusion.8), channel_id=1, source_target_pairs={{0,2},{1,3},{4,0},{5,1},{8,4},{9,5},{12,8},{13,9},{14,12},{15,13},... | collective-permute-start | bytes 405512 | tf_op jit(solution)/shard_map/ppermute | solution.py:244
  103.1 12.5 %collective-permute-start.54 = (bf16[33,16,128]{2,1,0:T(8,128)(2,1)S(1)}, bf16[33,16,128]{2,1,0:T(8,128)(2,1)S(1)}, u32[]{:S(2)}, u32[]{:S(2)}) collective-permute-start(bf16[33,16,128]{2,1,0:T(8,128)(2,1)S(1)} %get-tuple-element.114), channel_id=1, source_target_pairs={{0,1},{1,0},{2,3},{3,2},{4,5},{5,4},{6,7},{7,6},{8,9},{9,8},{10,11... | collective-permute-start | bytes 405512 | tf_op jit(solution)/shard_map/ppermute | solution.py:245
  108.8 5.0 %collective-permute-start.40 = (bf16[33,16,128]{2,1,0:T(8,128)(2,1)S(1)}, bf16[33,16,128]{2,1,0:T(8,128)(2,1)S(1)}, u32[]{:S(2)}, u32[]{:S(2)}) collective-permute-start(bf16[33,16,128]{2,1,0:T(8,128)(2,1)S(1)} %add_convert_fusion.11), channel_id=1, source_target_pairs={{0,4},{1,5},{4,8},{5,9},{8,12},{9,13},{12,14},{13,15},{14,10},{15,... | collective-permute-start | bytes 405512 | tf_op jit(solution)/shard_map/ppermute | solution.py:243
  110.6 8.4 %collective-permute-start.17 = (bf16[33,16,128]{2,1,0:T(8,128)(2,1)S(1)}, bf16[33,16,128]{2,1,0:T(8,128)(2,1)S(1)}, u32[]{:S(2)}, u32[]{:S(2)}) collective-permute-start(bf16[33,16,128]{2,1,0:T(8,128)(2,1)S(1)} %get-tuple-element.92), channel_id=1, source_target_pairs={{0,1},{1,0},{2,3},{3,2},{4,5},{5,4},{6,7},{7,6},{8,9},{9,8},{10,11... | collective-permute-start | bytes 405512 | tf_op jit(solution)/shard_map/ppermute | solution.py:245
  113.8 5.0 %collective-permute-start.53 = (bf16[33,16,128]{2,1,0:T(8,128)(2,1)S(1)}, bf16[33,16,128]{2,1,0:T(8,128)(2,1)S(1)}, u32[]{:S(2)}, u32[]{:S(2)}) collective-permute-start(bf16[33,16,128]{2,1,0:T(8,128)(2,1)S(1)} %add_convert_fusion.6), channel_id=1, source_target_pairs={{0,4},{1,5},{4,8},{5,9},{8,12},{9,13},{12,14},{13,15},{14,10},{15,... | collective-permute-start | bytes 405512 | tf_op jit(solution)/shard_map/ppermute | solution.py:243
  115.6 10.7 %collective-permute-start.62 = (bf16[192,1024]{1,0:T(8,128)(2,1)S(1)}, bf16[192,1024]{1,0:T(8,128)(2,1)S(1)}, u32[]{:S(2)}, u32[]{:S(2)}) collective-permute-start(bf16[192,1024]{1,0:T(8,128)(2,1)S(1)} %get-tuple-element.164), channel_id=1, source_target_pairs={{0,16},{16,0},{1,17},{17,1},{2,18},{18,2},{3,19},{19,3},{4,20},{20... | collective-permute-start | bytes 1179656 | tf_op jit(solution)/shard_map/ppermute | solution.py:311
  118.8 5.0 %collective-permute-start.14 = (bf16[33,16,128]{2,1,0:T(8,128)(2,1)S(1)}, bf16[33,16,128]{2,1,0:T(8,128)(2,1)S(1)}, u32[]{:S(2)}, u32[]{:S(2)}) collective-permute-start(bf16[33,16,128]{2,1,0:T(8,128)(2,1)S(1)} %add_convert_fusion.16), channel_id=1, source_target_pairs={{0,2},{1,3},{4,0},{5,1},{8,4},{9,5},{12,8},{13,9},{14,12},{15,13},... | collective-permute-start | bytes 405512 | tf_op jit(solution)/shard_map/ppermute | solution.py:244
  119.0 43.6 %copy-start.5 = (s32[128,8]{0,1:T(8,128)S(1)}, s32[128,8]{0,1:T(8,128)}, u32[]{:S(2)}) copy-start(s32[128,8]{0,1:T(8,128)} %param.9) | copy-start | bytes 12292
  119.0 25.7 %collective-permute-start.58 = (bf16[33,16,128]{2,1,0:T(8,128)(2,1)S(1)}, bf16[33,16,128]{2,1,0:T(8,128)(2,1)S(1)}, u32[]{:S(2)}, u32[]{:S(2)}) collective-permute-start(bf16[33,16,128]{2,1,0:T(8,128)(2,1)S(1)} %copy-done.40), channel_id=1, source_target_pairs={{0,1},{1,0},{2,3},{3,2},{4,5},{5,4},{6,7},{7,6},{8,9},{9,8},{10,11... | collective-permute-start | bytes 405512 | tf_op jit(solution)/shard_map/ppermute | solution.py:245
  123.8 9.2 %collective-permute-start.61 = (bf16[512,384]{1,0:T(8,128)(2,1)S(1)}, bf16[512,384]{1,0:T(8,128)(2,1)S(1)}, u32[]{:S(2)}, u32[]{:S(2)}) collective-permute-start(bf16[512,384]{1,0:T(8,128)(2,1)S(1)} %get-tuple-element.162), channel_id=1, source_target_pairs={{0,16},{16,0},{1,17},{17,1},{2,18},{18,2},{3,19},{19,3},{4,20},{20... | collective-permute-start | bytes 1179656 | tf_op jit(solution)/shard_map/ppermute | solution.py:311
  126.3 9.2 %collective-permute-start.56 = (bf16[33,16,128]{2,1,0:T(8,128)(2,1)S(1)}, bf16[33,16,128]{2,1,0:T(8,128)(2,1)S(1)}, u32[]{:S(2)}, u32[]{:S(2)}) collective-permute-start(bf16[33,16,128]{2,1,0:T(8,128)(2,1)S(1)} %get-tuple-element.116), channel_id=1, source_target_pairs={{0,1},{1,0},{2,3},{3,2},{4,5},{5,4},{6,7},{7,6},{8,9},{9,8},{10,11... | collective-permute-start | bytes 405512 | tf_op jit(solution)/shard_map/ppermute | solution.py:245
  133.0 5.0 %collective-permute-start.55 = (bf16[33,16,128]{2,1,0:T(8,128)(2,1)S(1)}, bf16[33,16,128]{2,1,0:T(8,128)(2,1)S(1)}, u32[]{:S(2)}, u32[]{:S(2)}) collective-permute-start(bf16[33,16,128]{2,1,0:T(8,128)(2,1)S(1)} %add_convert_fusion.5), channel_id=1, source_target_pairs={{0,4},{1,5},{4,8},{5,9},{8,12},{9,13},{12,14},{13,15},{14,10},{15,... | collective-permute-start | bytes 405512 | tf_op jit(solution)/shard_map/ppermute | solution.py:243
  135.4 3.1 %collective-permute-start.21 = (bf16[33,16,128]{2,1,0:T(8,128)(2,1)S(1)}, bf16[33,16,128]{2,1,0:T(8,128)(2,1)S(1)}, u32[]{:S(2)}, u32[]{:S(2)}) collective-permute-start(bf16[33,16,128]{2,1,0:T(8,128)(2,1)S(1)} %get-tuple-element.94), channel_id=1, source_target_pairs={{0,1},{1,0},{2,3},{3,2},{4,5},{5,4},{6,7},{7,6},{8,9},{9,8},{10,11... | collective-permute-start | bytes 405512 | tf_op jit(solution)/shard_map/ppermute | solution.py:245
  138.0 5.0 %collective-permute-start.18 = (bf16[33,16,128]{2,1,0:T(8,128)(2,1)S(1)}, bf16[33,16,128]{2,1,0:T(8,128)(2,1)S(1)}, u32[]{:S(2)}, u32[]{:S(2)}) collective-permute-start(bf16[33,16,128]{2,1,0:T(8,128)(2,1)S(1)} %add_convert_fusion.15), channel_id=1, source_target_pairs={{0,2},{1,3},{4,0},{5,1},{8,4},{9,5},{12,8},{13,9},{14,12},{15,13},... | collective-permute-start | bytes 405512 | tf_op jit(solution)/shard_map/ppermute | solution.py:244
  138.6 10.0 %collective-permute-start.25 = (bf16[33,16,128]{2,1,0:T(8,128)(2,1)S(1)}, bf16[33,16,128]{2,1,0:T(8,128)(2,1)S(1)}, u32[]{:S(2)}, u32[]{:S(2)}) collective-permute-start(bf16[33,16,128]{2,1,0:T(8,128)(2,1)S(1)} %copy-done.38), channel_id=1, source_target_pairs={{0,1},{1,0},{2,3},{3,2},{4,5},{5,4},{6,7},{7,6},{8,9},{9,8},{10,11... | collective-permute-start | bytes 405512 | tf_op jit(solution)/shard_map/ppermute | solution.py:245
  143.0 5.0 %collective-permute-start.57 = (bf16[33,16,128]{2,1,0:T(8,128)(2,1)S(1)}, bf16[33,16,128]{2,1,0:T(8,128)(2,1)S(1)}, u32[]{:S(2)}, u32[]{:S(2)}) collective-permute-start(bf16[33,16,128]{2,1,0:T(8,128)(2,1)S(1)} %add_convert_fusion.4), channel_id=1, source_target_pairs={{0,4},{1,5},{4,8},{5,9},{8,12},{9,13},{12,14},{13,15},{14,10},{15,... | collective-permute-start | bytes 405512 | tf_op jit(solution)/shard_map/ppermute | solution.py:243
  144.7 12.9 %collective-permute-start.60 = (bf16[512,384]{1,0:T(8,128)(2,1)S(1)}, bf16[512,384]{1,0:T(8,128)(2,1)S(1)}, u32[]{:S(2)}, u32[]{:S(2)}) collective-permute-start(bf16[512,384]{1,0:T(8,128)(2,1)S(1)} %get-tuple-element.160), channel_id=1, source_target_pairs={{0,16},{16,0},{1,17},{17,1},{2,18},{18,2},{3,19},{19,3},{4,20},{20... | collective-permute-start | bytes 1179656 | tf_op jit(solution)/shard_map/ppermute | solution.py:311
  148.0 5.4 %collective-permute-start.22 = (bf16[33,16,128]{2,1,0:T(8,128)(2,1)S(1)}, bf16[33,16,128]{2,1,0:T(8,128)(2,1)S(1)}, u32[]{:S(2)}, u32[]{:S(2)}) collective-permute-start(bf16[33,16,128]{2,1,0:T(8,128)(2,1)S(1)} %add_convert_fusion.14), channel_id=1, source_target_pairs={{0,2},{1,3},{4,0},{5,1},{8,4},{9,5},{12,8},{13,9},{14,12},{15,13},... | collective-permute-start | bytes 405512 | tf_op jit(solution)/shard_map/ppermute | solution.py:244
  148.6 9.8 %collective-permute-start.51 = (bf16[33,16,128]{2,1,0:T(8,128)(2,1)S(1)}, bf16[33,16,128]{2,1,0:T(8,128)(2,1)S(1)}, u32[]{:S(2)}, u32[]{:S(2)}) collective-permute-start(bf16[33,16,128]{2,1,0:T(8,128)(2,1)S(1)} %add_convert_fusion.7), channel_id=1, source_target_pairs={{0,2},{1,3},{4,0},{5,1},{8,4},{9,5},{12,8},{13,9},{14,12},{15,13},... | collective-permute-start | bytes 405512 | tf_op jit(solution)/shard_map/ppermute | solution.py:244
  153.5 5.0 %collective-permute-start.44 = (bf16[33,16,128]{2,1,0:T(8,128)(2,1)S(1)}, bf16[33,16,128]{2,1,0:T(8,128)(2,1)S(1)}, u32[]{:S(2)}, u32[]{:S(2)}) collective-permute-start(bf16[33,16,128]{2,1,0:T(8,128)(2,1)S(1)} %add_convert_fusion.10), channel_id=1, source_target_pairs={{0,4},{1,5},{4,8},{5,9},{8,12},{9,13},{12,14},{13,15},{14,10},{15,... | collective-permute-start | bytes 405512 | tf_op jit(solution)/shard_map/ppermute | solution.py:243
  155.3 5.1 %collective-permute-start.59 = (bf16[33,16,128]{2,1,0:T(8,128)(2,1)S(1)}, bf16[33,16,128]{2,1,0:T(8,128)(2,1)S(1)}, u32[]{:S(2)}, u32[]{:S(2)}) collective-permute-start(bf16[33,16,128]{2,1,0:T(8,128)(2,1)S(1)} %add_convert_fusion.3), channel_id=1, source_target_pairs={{0,4},{1,5},{4,8},{5,9},{8,12},{9,13},{12,14},{13,15},{14,10},{15,... | collective-permute-start | bytes 405512 | tf_op jit(solution)/shard_map/ppermute | solution.py:243
  157.6 5.0 %collective-permute-start.26 = (bf16[33,16,128]{2,1,0:T(8,128)(2,1)S(1)}, bf16[33,16,128]{2,1,0:T(8,128)(2,1)S(1)}, u32[]{:S(2)}, u32[]{:S(2)}) collective-permute-start(bf16[33,16,128]{2,1,0:T(8,128)(2,1)S(1)} %add_convert_fusion.13), channel_id=1, source_target_pairs={{0,2},{1,3},{4,0},{5,1},{8,4},{9,5},{12,8},{13,9},{14,12},{15,13},... | collective-permute-start | bytes 405512 | tf_op jit(solution)/shard_map/ppermute | solution.py:244
  (44 other events, 191.1 us)

commit v2 on v1

v2 whole, which is shorter than its diff:
```python
import functools

import jax
import jax.numpy as jnp
from jax import lax
from jax.experimental import pallas as pl
from jax.experimental.pallas import tpu as pltpu
from jax.sharding import PartitionSpec as P

BF16, F32 = jnp.bfloat16, jnp.float32
ROWS, LANES = 16, 128
VMEM = pl.BlockSpec(memory_space=pltpu.VMEM)
SMEM = pl.BlockSpec(memory_space=pltpu.SMEM)
PARAMS = pltpu.CompilerParams(vmem_limit_bytes=16 * 1024 * 1024)


def iota(shape, dim):
    return lax.broadcasted_iota(jnp.int32, shape, dim)


def nt(a, b):
    return lax.dot_general(a, b, (((1,), (1,)), ((), ())), preferred_element_type=F32)


def put_tiles(ref, first, value):
    rows, width = value.shape
    across = width // LANES
    for i in range(rows // ROWS):
        for j in range(across):
            ref[first + i * across + j] = value[
                i * ROWS : (i + 1) * ROWS, j * LANES : (j + 1) * LANES
            ]


def take_tiles(ref, first, dst, row, rows, width):
    across = width // LANES
    for i in range(rows // ROWS):
        for j in range(across):
            dst[row + i * ROWS : row + (i + 1) * ROWS, j * LANES : (j + 1) * LANES] = ref[
                first + i * across + j
            ]


def pack_kernel(tok_ref, cot_ref, ids_ref, prob_ref, out_ref):
    tok_dev, width = tok_ref.shape
    half = tok_dev // 2
    block = half * width // (ROWS * LANES)
    ids, prob = ids_ref[...], prob_ref[...].astype(F32)
    for i in range(out_ref.shape[1] - 2 * block):
        expert = iota((ROWS, tok_dev), 0) + i * ROWS
        dense = jnp.zeros((ROWS, tok_dev), F32)
        for k in range(ids.shape[0]):
            dense += jnp.where(ids[k : k + 1] == expert, prob[k : k + 1], 0.0)
        for n in range(2):
            out_ref[n, 2 * block + i] = dense.astype(BF16)
    for n in range(2):
        put_tiles(out_ref.at[n], 0, tok_ref[n * half : (n + 1) * half])
        put_tiles(out_ref.at[n], block, cot_ref[n * half : (n + 1) * half])


def expert_kernel(halves, half, *refs):
    me_ref, refs = refs[0], refs[1:]
    packets, refs = refs[: len(halves)], refs[len(halves) :]
    weights, refs = (refs[:3], refs[3:6]), refs[6:]
    grads, refs = refs[: len(halves)], refs[len(halves) :]
    xt_ref, outs, (x_ref, dy_ref) = refs[0], (refs[1:4], refs[4:7]), refs[7:]
    width, ff = weights[0][0].shape
    block = half * width // (ROWS * LANES)
    pieces = [
        (ref.at[i], grad.at[i], which)
        for ref, grad, names in zip(packets, grads, halves)
        for i, which in enumerate(names)
    ]
    extra = packets[0].shape[1] - 2 * block
    eyes = [iota((half, LANES), 0) + n * half == iota((half, LANES), 1) for n in range(2)]
    for n, (ref, _, _) in enumerate(pieces):
        take_tiles(ref, 0, x_ref, n * half, half, width)
        take_tiles(ref, block, dy_ref, n * half, half, width)
    x, dy = x_ref[...], dy_ref[...]
    rows, by_expert = None, [[0.0] * extra for _ in pieces]
    for e, (wg_ref, wu_ref, wd_ref) in enumerate(weights):
        me = me_ref[e]
        mine = [iota((ROWS, LANES), 0) + i * ROWS == me for i in range(extra)]
        probs = []
        for ref, _, which in pieces:
            row = sum(
                jnp.sum(
                    jnp.where(mine[i], ref[2 * block + i].astype(F32), 0.0), axis=0, keepdims=True
                )
                for i in range(extra)
            )
            probs.append(jnp.sum(jnp.where(eyes[which], row, 0.0), axis=1, keepdims=True))
        prob = jnp.concatenate(probs, axis=0)
        gate = jnp.dot(x, wg_ref[...], preferred_element_type=F32)
        up = jnp.dot(x, wu_ref[...], preferred_element_type=F32)
        dz = nt(dy, wd_ref[...])
        sig = jax.nn.sigmoid(gate)
        act, dact = gate * sig, sig + gate * sig * (1.0 - sig)
        hidden = (act * up).astype(BF16)
        gate_grad = jnp.sum(dz * hidden.astype(F32), axis=1, keepdims=True)
        dh = prob * dz
        d_gate = (dh * up * dact).astype(BF16)
        d_up = (dh * act).astype(BF16)
        back = nt(d_gate, wg_ref[...]) + nt(d_up, wu_ref[...])
        rows = back if rows is None else rows + back
        for n, (_, _, which) in enumerate(pieces):
            row = jnp.sum(
                jnp.where(eyes[which], gate_grad[n * half : (n + 1) * half], 0.0),
                axis=0,
                keepdims=True,
            )
            for i in range(extra):
                by_expert[n][i] += jnp.where(mine[i], row, 0.0)
        dgu_ref, ht_ref, sc_ref = outs[e]
        dgu_ref[:, :ff] = d_gate
        dgu_ref[:, ff:] = d_up
        ht_ref[...] = hidden.T
        sc_ref[...] = (prob * dy.astype(F32)).astype(BF16)
    for n, (_, grad, _) in enumerate(pieces):
        put_tiles(grad, 0, rows[n * half : (n + 1) * half].astype(BF16))
        for i in range(extra):
            grad[block + i] = by_expert[n][i].astype(BF16)
    xt_ref[...] = x.T


def weight_kernel(groups, start, extra, final, *refs):
    refs = refs[1:]
    total_w = total_d = None
    for n in range(start + extra):
        w, d = refs[0][...].astype(F32), refs[1][...].astype(F32)
        total_w = w if total_w is None else total_w + w
        total_d = d if total_d is None else total_d + d
        refs = refs[2:]
    for g in range(groups):
        xt, dgu, ht, sc = refs[4 * g : 4 * g + 4]
        w = jnp.dot(xt[...], dgu[...], preferred_element_type=F32)
        d = jnp.dot(ht[...], sc[...], preferred_element_type=F32)
        total_w = w if total_w is None else total_w + w
        total_d = d if total_d is None else total_d + d
    out_w, out_d = refs[4 * groups :]
    out_w[...] = total_w.astype(out_w.dtype)
    out_d[...] = total_d.astype(out_d.dtype)


def weight_sums(totals, groups, width, ff, part=None, parts=1, extra=None, kind=F32):
    steps = 4 // parts
    tile_w, tile_d = width // 4, ff // 4
    first = jnp.zeros((1,), jnp.int32) if part is None else (part * steps).astype(jnp.int32)[None]
    row = lambda i, s: (s[0] + i, 0)
    whole = lambda i, s: (0, 0)
    out_row = lambda i, s: (i, 0)
    blocks = ((tile_w, 2 * ff), (tile_d, width))
    specs, args = [], []
    if totals is not None:
        specs += [pl.BlockSpec(b, row) for b in blocks]
        args += list(totals)
    if extra is not None:
        specs += [pl.BlockSpec(b, out_row) for b in blocks]
        args += list(extra)
    for xt, dgu, ht, sc in groups:
        k = xt.shape[1]
        specs += [
            pl.BlockSpec((tile_w, k), row),
            pl.BlockSpec((k, 2 * ff), whole),
            pl.BlockSpec((tile_d, k), row),
            pl.BlockSpec((k, width), whole),
        ]
        args += [xt, dgu, ht, sc]
    rows = sum(g[0].shape[1] for g in groups)
    return pl.pallas_call(
        functools.partial(
            weight_kernel, len(groups), int(totals is not None), int(extra is not None), kind
        ),
        out_shape=tuple(jax.ShapeDtypeStruct((r * steps, c), kind) for r, c in blocks),
        grid_spec=pltpu.PrefetchScalarGridSpec(
            num_scalar_prefetch=1,
            grid=(steps,),
            in_specs=specs,
            out_specs=tuple(pl.BlockSpec(b, out_row) for b in blocks),
        ),
        compiler_params=PARAMS,
        cost_estimate=pl.CostEstimate(
            flops=6 * rows * width * ff // parts, bytes_accessed=8 * 2**20 // parts, transcendentals=0
        ),
        name="weight_sums",
    )(first, *args)


def home_kernel(count, ids_ref, *refs):
    out_ref, prob_ref = refs[count:]
    tok_dev, width = out_ref.shape
    half = tok_dev // 2
    block = half * width // (ROWS * LANES)
    across = width // LANES
    sums = []
    for n in range(2):
        total = sum(ref[n].astype(F32) for ref in refs[:count])
        for i in range(half // ROWS):
            for j in range(across):
                out_ref[
                    n * half + i * ROWS : n * half + (i + 1) * ROWS, j * LANES : (j + 1) * LANES
                ] = total[i * across + j].astype(BF16)
        sums.append(total[block:])
    by_expert = sums[0] + sums[1]
    ids = ids_ref[...]
    for k in range(ids.shape[0]):
        row = jnp.zeros((1, tok_dev), F32)
        for i in range(by_expert.shape[0]):
            expert = iota((ROWS, tok_dev), 0) + i * ROWS
            row += jnp.sum(
                jnp.where(ids[k : k + 1] == expert, by_expert[i], 0.0), axis=0, keepdims=True
            )
        prob_ref[k : k + 1] = row


def on_device(tokens, cotangent, expert_ids, gate_probs, w_gate, w_up, w_down):
    tok_dev, width = tokens.shape
    ff = w_gate.shape[2]
    half = tok_dev // 2
    devices = lax.axis_size("expert")
    groups = lax.axis_size("dp")
    experts = devices * w_gate.shape[0]
    block = half * width // (ROWS * LANES)
    extra = experts // ROWS

    chips = devices // 2
    ring = list(range(0, chips, 2)) + list(range(1, chips, 2))[::-1]
    hop = {
        d: [
            (2 * ring[i] + c, 2 * ring[(i + d) % chips] + c)
            for i in range(chips)
            for c in range(2)
        ]
        for d in (1, -1)
    }
    right = lambda v: lax.ppermute(v, "expert", hop[1])
    left = lambda v: lax.ppermute(v, "expert", hop[-1])
    swap = lambda v: lax.ppermute(v, "expert", [(i, i ^ 1) for i in range(devices)])
    full, odd = (chips - 1) // 2, chips % 2 == 0

    me = lax.axis_index("expert").astype(jnp.int32)
    pair = jnp.stack([me, me ^ 1])
    ids_t, probs_t = expert_ids.T, gate_probs.T
    own = (w_gate[0], w_up[0], w_down[0])

    whole = lambda v: pl.BlockSpec(v.shape, lambda i: (0,) * len(v.shape))
    packet = jax.ShapeDtypeStruct((2, 2 * block + extra, ROWS, LANES), BF16)
    start = pl.pallas_call(
        pack_kernel,
        grid=(1,),
        out_shape=packet,
        in_specs=[whole(v) for v in (tokens, cotangent, ids_t, probs_t)],
        out_specs=whole(packet),
        compiler_params=PARAMS,
        name="pack",
    )(tokens, cotangent, ids_t, probs_t)

    weights = own + tuple(swap(v) for v in own)

    def expert(*packets, halves):
        rows = half * sum(len(h) for h in halves)
        shape = lambda *s: jax.ShapeDtypeStruct(s, BF16)
        each = (shape(rows, 2 * ff), shape(ff, rows), shape(rows, width))
        outs = pl.pallas_call(
            functools.partial(expert_kernel, halves, half),
            out_shape=tuple(shape(len(h), block + extra, ROWS, LANES) for h in halves)
            + (shape(width, rows),)
            + each * 2,
            in_specs=[SMEM] + [VMEM] * (len(packets) + 6),
            out_specs=(VMEM,) * (len(packets) + 7),
            scratch_shapes=[pltpu.VMEM((rows, width), BF16), pltpu.VMEM((rows, width), BF16)],
            compiler_params=PARAMS,
            cost_estimate=pl.CostEstimate(
                flops=20 * rows * width * ff,
                bytes_accessed=8 * 2**20,
                transcendentals=2 * rows * ff,
            ),
            name="expert",
        )(pair, *packets, *weights)
        grads, xt, rest = outs[: len(packets)], outs[len(packets)], outs[len(packets) + 1 :]
        return grads, ((xt,) + rest[:3], (xt,) + rest[3:])

    both = (0, 1)
    (home,), group = expert(start, halves=(both,))
    group = [group]
    r = l = start
    local = {}
    for s in range(1, full + 1):
        r, l = right(r), left(l)
        local[s], new = expert(r, l, halves=(both, both))
        group.append(new)
    if odd:
        ends = right(r[:1]), left(l[1:])
        local[full + 1], new = expert(*ends, halves=((0,), (1,)))
        group.append(new)

    sums = functools.partial(weight_sums, width=width, ff=ff)
    totals = [None, None]
    for some in (group[:-2], group[-2:-1]):
        for e in range(2):
            totals[e] = sums(totals[e], [g[e] for g in some])
    final = [[g[e] for g in group[-1:]] for e in range(2)]

    def both_cores(**part):
        other = [swap(v) for v in sums(totals[1], final[1], kind=BF16, **part)]
        return sums(totals[0], final[0], kind=BF16, extra=other, **part)

    if groups == 2:
        here = lax.axis_index("dp")
        got = [
            lax.ppermute(v, "dp", [(0, 1), (1, 0)]) for v in both_cores(part=1 - here, parts=2)
        ]
        keep = both_cores(part=here, parts=2)
        grad_w, grad_d = [
            (a.astype(F32) + b.astype(F32)).astype(BF16) for a, b in zip(keep, got)
        ]
    else:
        grad_w, grad_d = [
            lax.psum_scatter(v, "dp", scatter_dimension=0, tiled=True) for v in both_cores()
        ]

    def add(a, b):
        return (a.astype(F32) + b.astype(F32)).astype(BF16)

    def back(side, move):
        moving = None
        if odd:
            moving = move(local[full + 1][side])
        for s in range(full, 0, -1):
            here = local[s][side]
            if moving is None:
                moving = here
            elif moving.shape == here.shape:
                moving = add(moving, here)
            elif side == 0:
                moving = jnp.concatenate([add(moving, here[:1]), here[1:]])
            else:
                moving = jnp.concatenate([here[:1], add(moving, here[1:])])
            moving = move(moving)
        return moving

    parts = (home, back(0, left), back(1, right))
    grad_tokens, grad_probs = pl.pallas_call(
        functools.partial(home_kernel, len(parts)),
        out_shape=(
            jax.ShapeDtypeStruct((tok_dev, width), BF16),
            jax.ShapeDtypeStruct(ids_t.shape, F32),
        ),
        in_specs=[VMEM] * (1 + len(parts)),
        out_specs=(VMEM, VMEM),
        compiler_params=PARAMS,
        name="home",
    )(ids_t, *parts)
    return (
        grad_tokens,
        grad_probs.T.astype(BF16),
        grad_w[None, :, :ff],
        grad_w[None, :, ff:],
        grad_d[None],
    )


def solution(mesh):
    return jax.shard_map(
        on_device,
        mesh=mesh,
        in_specs=(
            P(("dp", "expert"), None),
            P(("dp", "expert"), None),
            P(("dp", "expert"), None),
            P(("dp", "expert"), None),
            P("expert", None, None),
            P("expert", None, None),
            P("expert", None, None),
        ),
        out_specs=(
            P(("dp", "expert"), None),
            P(("dp", "expert"), None),
            P("expert", "dp", None),
            P("expert", "dp", None),
            P("expert", "dp", None),
        ),
        check_vma=False,
    )
```

time: 165 us -> 120 us (0.73)
  starting transfers between devices: 43.7 us -> 21.3 us
  local copies, waits for them, and re-layouts: 24.6 us -> 8.48 us
  Pallas kernels: 38 us -> 31.1 us
  waiting for transfers between devices: 52.7 us -> 55.5 us
  other arithmetic: 3.89 us -> 2.16 us
    ppermute x14 -> x8, starting transfers between devices: 25.2 us -> 6.82 us  [on_device(): right = lambda v: lax.ppermute(v, 'expert', hop[1])]
    unnamed x90 -> x24, local copies, waits for them, and re-layouts: 24.6 us -> 7.46 us
    ppermute x14 -> x8, waiting for transfers between devices: 19.1 us -> 6.73 us  [on_device(): right = lambda v: lax.ppermute(v, 'expert', hop[1])]
    ppermute x3 -> x2, waiting for transfers between devices: 6.78 us -> 16.8 us  [on_device(): lax.ppermute(v, 'dp', [(0, 1), (1, 0)])]
    ppermute x14 -> x8, waiting for transfers between devices: 23.4 us -> 32 us  [on_device(): left = lambda v: lax.ppermute(v, 'expert', hop[-1])]
    pallas_call x15, Pallas kernels: 38 us -> 31.1 us  [the longest x5 19.7 us: expert(): pl.pallas_call(functools.partial(expert_kernel, halves, half), out_shape=...]
    ppermute x32 -> x7, starting transfers between devices: 6.38 us -> 1.23 us  [on_device(): lax.ppermute(v, 'expert', [(i, i ^ 1) for i in range(devices)])]
    ppermute x14 -> x8, starting transfers between devices: 7.6 us -> 11.2 us  [on_device(): left = lambda v: lax.ppermute(v, 'expert', hop[-1])]
  transfers between devices with their start and end apart: 63 -> 25, of which waited for: 23 -> 9; matrix products, arithmetic and copies ran while one was open for 2% -> 2% of each run, Pallas kernels for 23% -> 23%
where the time goes in v2:
time: 120 us; the launch traced here: 119 us
  waiting for transfers between devices  55.5 us (46%)
  Pallas kernels  31.1 us (26%)
  starting transfers between devices  21.3 us (18%)
  local copies, waits for them, and re-layouts  8.48 us (7%)
  other arithmetic  2.16 us (2%)
    ppermute x8, waiting for transfers between devices, on_device(): left = lambda v: lax.ppermute(v, 'expert', hop[-1])  32 us
    pallas_call x5, Pallas kernels, expert(): pl.pallas_call(functools.partial(expert_kernel, halves, half), out_shape=...  19.7 us
    ppermute x2, waiting for transfers between devices, on_device(): lax.ppermute(v, 'dp', [(0, 1), (1, 0)])  16.8 us
    ppermute x8, starting transfers between devices, on_device(): left = lambda v: lax.ppermute(v, 'expert', hop[-1])  11.2 us
    pallas_call x8, Pallas kernels, weight_sums(): pl.pallas_call(functools.partial(weight_kernel, len(groups), int(totals i...  10.5 us
    unnamed x24, local copies, waits for them, and re-layouts  7.46 us
    ppermute x8, starting transfers between devices, on_device(): right = lambda v: lax.ppermute(v, 'expert', hop[1])  6.82 us
    ppermute x8, waiting for transfers between devices, on_device(): right = lambda v: lax.ppermute(v, 'expert', hop[1])  6.73 us
  transfers between devices with their start and end apart: 25, of which 9 were waited for; matrix products, arithmetic and copies ran while one was open for 2% of the time, Pallas kernels for 23%

profile of v2, /device:TPU:0, one launch (start us, length us, event | category | flops | bytes accessed | tf_op | source)
XLA Modules:
  0.0 119.4 jit_solution(16315765966974624673)
XLA Ops:
  0.7 1.0 copy-done.7
  1.7 0.9 copy-done.8
  2.6 0.7 copy-done.9
  3.3 0.7 copy-done.11
  4.0 0.1 pack.1.refs_1_
  4.1 3.0 %collective-permute-start.7 = (bf16[2,65,16,128]{3,2,1,0:T(8,128)(2,1)S(1)}, bf16[2,65,16,128]{3,2,1,0:T(8,128)(2,1)}, u32[]{:S(2)}, u32[]{:S(2)}) collective-permute-start(bf16[2,65,16,128]{3,2,1,0:T(8,128)(2,1)S(1)} %pack.1.refs_1_), channel_id=1, source_target_pairs={{0,2},{1,3},{4,0},{5,1},{8,4},{9,5},{12,8},{13,9},{14,12},{15,13},... | collective-permute-start | bytes 1597448 | tf_op jit(solution)/shard_map/ppermute | solution.py:237
  7.1 0.1 collective-permute-start.3
  7.2 0.8 copy-done.5
  8.0 0.5 collective-permute-start.1
  8.5 10.8 %collective-permute-done.7.refs_2_ = bf16[2,65,16,128]{3,2,1,0:T(8,128)(2,1)} collective-permute-done((bf16[2,65,16,128]{3,2,1,0:T(8,128)(2,1)S(1)}, bf16[2,65,16,128]{3,2,1,0:T(8,128)(2,1)}, u32[]{:S(2)}, u32[]{:S(2)}) %collective-permute-start.7) | collective-permute-done | bytes 532512 | tf_op jit(solution)/shard_map/ppermute | solution.py:237
  19.3 1.7 %collective-permute-start.8 = (bf16[2,65,16,128]{3,2,1,0:T(8,128)(2,1)}, bf16[2,65,16,128]{3,2,1,0:T(8,128)(2,1)}, u32[]{:S(2)}, u32[]{:S(2)}) collective-permute-start(bf16[2,65,16,128]{3,2,1,0:T(8,128)(2,1)} %collective-permute-done.7.refs_2_), channel_id=1, source_target_pairs={{0,2},{1,3},{4,0},{5,1},{8,4},{9,5},{12,8},{13,9},{14,12},{15,13},... | collective-permute-start | bytes 1597448 | tf_op jit(solution)/shard_map/ppermute | solution.py:237
  21.0 0.3 collective-permute-start.4
  21.4 11.6 %collective-permute-done.8.refs_2_ = bf16[2,65,16,128]{3,2,1,0:T(8,128)(2,1)} collective-permute-done((bf16[2,65,16,128]{3,2,1,0:T(8,128)(2,1)}, bf16[2,65,16,128]{3,2,1,0:T(8,128)(2,1)}, u32[]{:S(2)}, u32[]{:S(2)}) %collective-permute-start.8) | collective-permute-done | bytes 532512 | tf_op jit(solution)/shard_map/ppermute | solution.py:237
  32.9 1.4 %collective-permute-start.9 = (bf16[2,65,16,128]{3,2,1,0:T(8,128)(2,1)}, bf16[2,65,16,128]{3,2,1,0:T(8,128)(2,1)S(1)}, u32[]{:S(2)}, u32[]{:S(2)}) collective-permute-start(bf16[2,65,16,128]{3,2,1,0:T(8,128)(2,1)} %collective-permute-done.8.refs_2_), channel_id=1, source_target_pairs={{0,2},{1,3},{4,0},{5,1},{8,4},{9,5},{12,8},{13,9},{14,12},{15,13},... | collective-permute-start | bytes 1597448 | tf_op jit(solution)/shard_map/ppermute | solution.py:237
  34.3 0.7 collective-permute-start.5
  35.0 0.1 pad_add_fusion.refs_0_
  35.1 1.1 copy-done.1
  36.2 1.1 copy-done.3
  37.3 1.0 copy-done.6
  38.4 3.2 %expert.5 = (bf16[2,33,16,128]{3,2,1,0:T(8,128)(2,1)S(1)}, bf16[1024,128]{1,0:T(8,128)(2,1)S(1)}, bf16[128,768]{1,0:T(8,128)(2,1)S(1)}, bf16[384,128]{1,0:T(8,12...) custom-call(s32[2]{0:T(128)S(1)} %pad_add_fusion.refs_0_, ...), custom_call_target="tpu_custom_call" | custom-call | flops 1006632960 | bytes 8388608 | tf_op jit(solution)/shard_map/expert/pallas_call | solution.py:264
  41.6 4.7 %expert.9 = (bf16[2,33,16,128]{3,2,1,0:T(8,128)(2,1)S(1)}, bf16[2,33,16,128]{3,2,1,0:T(8,128)(2,1)S(1)}, bf16[1024,256]{1,0:T(8,128)(2,1)S(1)}, bf16[256,768]{1,...) custom-call(s32[2]{0:T(128)S(1)} %pad_add_fusion.refs_0_, ...), custom_call_target="tpu_custom_call" | custom-call | flops 2013265920 | bytes 8388608 | tf_op jit(solution)/shard_map/expert/pallas_call | solution.py:264
  46.3 4.7 %expert.8 = (bf16[2,33,16,128]{3,2,1,0:T(8,128)(2,1)S(1)}, bf16[2,33,16,128]{3,2,1,0:T(8,128)(2,1)S(1)}, bf16[1024,256]{1,0:T(8,128)(2,1)S(1)}, bf16[256,768]{1,...) custom-call(s32[2]{0:T(128)S(1)} %pad_add_fusion.refs_0_, ...), custom_call_target="tpu_custom_call" | custom-call | flops 2013265920 | bytes 8388608 | tf_op jit(solution)/shard_map/expert/pallas_call | solution.py:264
  51.0 1.4 %collective-permute-start.10 = (bf16[1,65,16,128]{3,2,1,0:T(8,128)(2,1)S(1)}, bf16[1,65,16,128]{3,2,1,0:T(8,128)(2,1)S(1)}, u32[]{:S(2)}, u32[]{:S(2)}) collective-permute-start(bf16[1,65,16,128]{3,2,1,0:T(8,128)(2,1)S(1)} %slice.33), channel_id=1, source_target_pairs={{0,2},{1,3},{4,0},{5,1},{8,4},{9,5},{12,8},{13,9},{14,12},{15,13},... | collective-permute-start | bytes 798728 | tf_op jit(solution)/shard_map/ppermute | solution.py:237
  52.4 0.9 collective-permute-start.6
  53.3 2.6 %weight_sums.8 = (f32[1024,768]{1,0:T(8,128)S(1)}, f32[384,1024]{1,0:T(8,128)S(1)}) custom-call(s32[1]{0:T(128)} %constant.14.clone.1.refs_0_, bf16[1024,128]{1,0:T(8,128)(2,1)S(1)} %get-tuple-element.78.refs_1_, bf16[128,768]{1,0:T(8,128)(2,1)S(1)} %get-tuple-element.79.refs_2_, bf16[384,128]{1,0:T(8,128)(2,1)S(1)} %get-tuple-element.80.refs_3_, ...), custom_call_target="tpu_custom_call" | custom-call | flops 1509949440 | bytes 8388608 | tf_op jit(solution)/shard_map/weight_sums/pallas_call | solution.py:170
  56.0 0.0 copy-start.2
  56.0 2.7 %weight_sums.10 = (f32[1024,768]{1,0:T(8,128)S(1)}, f32[384,1024]{1,0:T(8,128)S(1)}) custom-call(s32[1]{0:T(128)} %constant.14.clone.1.refs_0_, bf16[1024,128]{1,0:T(8,128)(2,1)S(1)} %get-tuple-element.78.refs_1_, bf16[128,768]{1,0:T(8,128)(2,1)S(1)} %get-tuple-element.98.refs_2_, bf16[384,128]{1,0:T(8,128)(2,1)S(1)} %get-tuple-element.99.refs_3_, ...), custom_call_target="tpu_custom_call" | custom-call | flops 1509949440 | bytes 8388608 | tf_op jit(solution)/shard_map/weight_sums/pallas_call | solution.py:170
  58.7 0.4 collective-permute-done.6.refs_1_
  59.1 3.2 %expert.6 = (bf16[1,33,16,128]{3,2,1,0:T(8,128)(2,1)S(1)}, bf16[1,33,16,128]{3,2,1,0:T(8,128)(2,1)S(1)}, bf16[1024,128]{1,0:T(8,128)(2,1)S(1)}, bf16[128,768]{1,...) custom-call(s32[2]{0:T(128)S(1)} %pad_add_fusion.refs_0_, ...), custom_call_target="tpu_custom_call" | custom-call | flops 1006632960 | bytes 8388608 | tf_op jit(solution)/shard_map/expert/pallas_call | solution.py:264
  62.3 1.2 collective-permute-start.15
  63.4 4.0 %expert.7 = (bf16[2,33,16,128]{3,2,1,0:T(8,128)(2,1)S(1)}, bf16[2,33,16,128]{3,2,1,0:T(8,128)(2,1)S(1)}, bf16[1024,256]{1,0:T(8,128)(2,1)S(1)}, bf16[256,768]{1,...) custom-call(s32[2]{0:T(128)S(1)} %pad_add_fusion.refs_0_, ...), custom_call_target="tpu_custom_call" | custom-call | flops 2013265920 | bytes 8388608 | tf_op jit(solution)/shard_map/expert/pallas_call | solution.py:264
  67.5 1.4 %weight_sums.11 = (f32[1024,768]{1,0:T(8,128)S(1)}, f32[384,1024]{1,0:T(8,128)S(1)}) custom-call(s32[1]{0:T(128)} %constant.14.clone.1.refs_0_, f32[1024,768]{1,0:T(8,128)S(1)} %get-tuple-element.107.refs_1_, f32[384,1024]{1,0:T(8,128)S(1)} %get-tuple-element.108.refs_2_, bf16[1024,256]{1,0:T(8,128)(2,1)S(1)} %get-tuple-element.92.refs_3_, ...), custom_call_target="tpu_custom_call" | custom-call | flops 603979776 | bytes 8388608 | tf_op jit(solution)/shard_map/weight_sums/pallas_call | solution.py:170
  68.9 1.0 collective-permute-start.11
  69.9 1.1 collective-permute-start.16
  71.1 4.3 %collective-permute-done.11 = bf16[1,33,16,128]{3,2,1,0:T(8,128)(2,1)S(1)} collective-permute-done((bf16[1,33,16,128]{3,2,1,0:T(8,128)(2,1)S(1)}, bf16[1,33,16,128]{3,2,1,0:T(8,128)(2,1)S(1)}, u32[]{:S(2)}, u32[]{:S(2)}) %collective-permute-start.11) | collective-permute-done | bytes 135200 | tf_op jit(solution)/shard_map/ppermute | solution.py:237
  75.4 0.9 collective-permute-start.12
  76.3 0.6 weight_sums.14
  76.9 0.1 collective-permute-start.22
  77.0 0.5 collective-permute-start.21
  77.5 0.6 weight_sums.12
  78.1 0.1 collective-permute-start.19
  78.3 0.1 add_convert_fusion.3
  78.4 1.2 %collective-permute-start.17 = (bf16[2,33,16,128]{3,2,1,0:T(8,128)(2,1)S(1)}, bf16[2,33,16,128]{3,2,1,0:T(8,128)(2,1)S(1)}, u32[]{:S(2)}, u32[]{:S(2)}) collective-permute-start(bf16[2,33,16,128]{3,2,1,0:T(8,128)(2,1)S(1)} %add_convert_fusion.3), channel_id=1, source_target_pairs={{0,4},{1,5},{4,8},{5,9},{8,12},{9,13},{12,14},{13,15},{14,10},{15,... | collective-permute-start | bytes 811016 | tf_op jit(solution)/shard_map/ppermute | solution.py:236
  79.6 2.3 %collective-permute-done.12 = bf16[2,33,16,128]{3,2,1,0:T(8,128)(2,1)S(1)} collective-permute-done((bf16[2,33,16,128]{3,2,1,0:T(8,128)(2,1)S(1)}, bf16[2,33,16,128]{3,2,1,0:T(8,128)(2,1)S(1)}, u32[]{:S(2)}, u32[]{:S(2)}) %collective-permute-start.12) | collective-permute-done | bytes 270368 | tf_op jit(solution)/shard_map/ppermute | solution.py:237
  82.0 0.1 add_convert_fusion.5
  82.0 0.9 collective-permute-start.13
  82.9 1.3 %weight_sums.9 = (f32[1024,768]{1,0:T(8,128)S(1)}, f32[384,1024]{1,0:T(8,128)S(1)}) custom-call(s32[1]{0:T(128)} %constant.14.clone.1.refs_0_, f32[1024,768]{1,0:T(8,128)S(1)} %get-tuple-element.90.refs_1_, f32[384,1024]{1,0:T(8,128)S(1)} %get-tuple-element.91.refs_2_, bf16[1024,256]{1,0:T(8,128)(2,1)S(1)} %get-tuple-element.92.refs_3_, ...), custom_call_target="tpu_custom_call" | custom-call | flops 603979776 | bytes 8388608 | tf_op jit(solution)/shard_map/weight_sums/pallas_call | solution.py:170
  84.3 3.0 %collective-permute-done.17 = bf16[2,33,16,128]{3,2,1,0:T(8,128)(2,1)S(1)} collective-permute-done((bf16[2,33,16,128]{3,2,1,0:T(8,128)(2,1)S(1)}, bf16[2,33,16,128]{3,2,1,0:T(8,128)(2,1)S(1)}, u32[]{:S(2)}, u32[]{:S(2)}) %collective-permute-start.17) | collective-permute-done | bytes 270368 | tf_op jit(solution)/shard_map/ppermute | solution.py:236
  87.3 0.1 add_convert_fusion.2
  87.3 1.2 %collective-permute-start.18 = (bf16[2,33,16,128]{3,2,1,0:T(8,128)(2,1)S(1)}, bf16[2,33,16,128]{3,2,1,0:T(8,128)(2,1)S(1)}, u32[]{:S(2)}, u32[]{:S(2)}) collective-permute-start(bf16[2,33,16,128]{3,2,1,0:T(8,128)(2,1)S(1)} %add_convert_fusion.2), channel_id=1, source_target_pairs={{0,4},{1,5},{4,8},{5,9},{8,12},{9,13},{12,14},{13,15},{14,10},{15,... | collective-permute-start | bytes 811016 | tf_op jit(solution)/shard_map/ppermute | solution.py:236
  88.6 0.6 weight_sums.15
  89.2 1.6 %collective-permute-start.23 = (bf16[512,768]{1,0:T(8,128)(2,1)S(1)}, bf16[512,768]{1,0:T(8,128)(2,1)S(1)}, u32[]{:S(2)}, u32[]{:S(2)}) collective-permute-start(bf16[512,768]{1,0:T(8,128)(2,1)S(1)} %get-tuple-element.126), channel_id=1, source_target_pairs={{0,16},{16,0},{1,17},{17,1},{2,18},{18,2},{3,19},{19,3},{4,20},{20... | collective-permute-start | bytes 2359304 | tf_op jit(solution)/shard_map/ppermute | solution.py:311
  90.8 0.1 add_convert_fusion.4
  90.9 1.0 collective-permute-start.14
  91.8 0.5 collective-permute-start.24
  92.3 0.6 weight_sums.13
  92.9 3.4 %collective-permute-done.18.refs_2_ = bf16[2,33,16,128]{3,2,1,0:T(8,128)(2,1)S(1)} collective-permute-done((bf16[2,33,16,128]{3,2,1,0:T(8,128)(2,1)S(1)}, bf16[2,33,16,128]{3,2,1,0:T(8,128)(2,1)S(1)}, u32[]{:S(2)}, u32[]{:S(2)}) %collective-permute-start.18) | collective-permute-done | bytes 270368 | tf_op jit(solution)/shard_map/ppermute | solution.py:236
  96.3 3.0 %collective-permute-done.14.refs_1_ = bf16[2,33,16,128]{3,2,1,0:T(8,128)(2,1)S(1)} collective-permute-done((bf16[2,33,16,128]{3,2,1,0:T(8,128)(2,1)S(1)}, bf16[2,33,16,128]{3,2,1,0:T(8,128)(2,1)S(1)}, u32[]{:S(2)}, u32[]{:S(2)}) %collective-permute-start.14) | collective-permute-done | bytes 270368 | tf_op jit(solution)/shard_map/ppermute | solution.py:237
  99.3 0.8 home.1
  100.1 0.6 convert_bitcast_fusion
  100.6 16.8 %collective-permute-done.24 = bf16[192,1024]{1,0:T(8,128)(2,1)S(1)} collective-permute-done((bf16[192,1024]{1,0:T(8,128)(2,1)S(1)}, bf16[192,1024]{1,0:T(8,128)(2,1)S(1)}, u32[]{:S(2)}, u32[]{:S(2)}) %collective-permute-start.24) | collective-permute-done | bytes 393248 | tf_op jit(solution)/shard_map/ppermute | solution.py:311
  117.4 0.9 fusion
  118.3 0.2 add_convert_fusion
  118.5 1.0 slice_bitcast_fusion
  (42 shorter events, 0.3 us)
Async XLA Ops:
  0.6 34.4 %copy-start = (bf16[1,1024,384]{2,1,0:T(8,128)(2,1)S(1)}, bf16[1,1024,384]{2,1,0:T(8,128)(2,1)}, u32[]{:S(2)}) copy-start(bf16[1,1024,384]{2,1,0:T(8,128)(2,1)} %param.11) | copy-start | bytes 2359300
  0.6 1.0 copy-start.7
  1.7 0.9 copy-start.8
  2.6 0.7 copy-start.9
  3.3 0.7 copy-start.11
  4.1 15.3 %collective-permute-start.7 = (bf16[2,65,16,128]{3,2,1,0:T(8,128)(2,1)S(1)}, bf16[2,65,16,128]{3,2,1,0:T(8,128)(2,1)}, u32[]{:S(2)}, u32[]{:S(2)}) collective-permute-start(bf16[2,65,16,128]{3,2,1,0:T(8,128)(2,1)S(1)} %pack.1.refs_1_), channel_id=1, source_target_pairs={{0,2},{1,3},{4,0},{5,1},{8,4},{9,5},{12,8},{13,9},{14,12},{15,13},... | collective-permute-start | bytes 1597448 | tf_op jit(solution)/shard_map/ppermute | solution.py:237
  7.1 13.9 %collective-permute-start.3 = (bf16[2,65,16,128]{3,2,1,0:T(8,128)(2,1)S(1)}, bf16[2,65,16,128]{3,2,1,0:T(8,128)(2,1)}, u32[]{:S(2)}, u32[]{:S(2)}) collective-permute-start(bf16[2,65,16,128]{3,2,1,0:T(8,128)(2,1)S(1)} %pack.1.refs_1_), channel_id=1, source_target_pairs={{0,4},{1,5},{4,8},{5,9},{8,12},{9,13},{12,14},{13,15},{14,10},{15,... | collective-permute-start | bytes 1597448 | tf_op jit(solution)/shard_map/ppermute | solution.py:236
  7.2 0.8 copy-start.5
  8.0 27.0 %collective-permute-start = (bf16[1024,384]{1,0:T(8,128)(2,1)}, bf16[1024,384]{1,0:T(8,128)(2,1)S(1)}, u32[]{:S(2)}, u32[]{:S(2)}) collective-permute-start(bf16[1024,384]{1,0:T(8,128)(2,1)} %bitcast.17), channel_id=1, source_target_pairs={{0,1},{1,0},{2,3},{3,2},{4,5},{5,4},{6,7},{7,6},{8,9},{9,8},{10,11... | collective-permute-start | bytes 2359304 | tf_op jit(solution)/shard_map/ppermute | solution.py:238
  8.0 27.0 %collective-permute-start.1 = (bf16[1024,384]{1,0:T(8,128)(2,1)}, bf16[1024,384]{1,0:T(8,128)(2,1)S(1)}, u32[]{:S(2)}, u32[]{:S(2)}) collective-permute-start(bf16[1024,384]{1,0:T(8,128)(2,1)} %bitcast.23), channel_id=1, source_target_pairs={{0,1},{1,0},{2,3},{3,2},{4,5},{5,4},{6,7},{7,6},{8,9},{9,8},{10,11... | collective-permute-start | bytes 2359304 | tf_op jit(solution)/shard_map/ppermute | solution.py:238
  8.5 26.5 %collective-permute-start.2 = (bf16[384,1024]{1,0:T(8,128)(2,1)}, bf16[384,1024]{1,0:T(8,128)(2,1)S(1)}, u32[]{:S(2)}, u32[]{:S(2)}) collective-permute-start(bf16[384,1024]{1,0:T(8,128)(2,1)} %bitcast.29), channel_id=1, source_target_pairs={{0,1},{1,0},{2,3},{3,2},{4,5},{5,4},{6,7},{7,6},{8,9},{9,8},{10,11... | collective-permute-start | bytes 2359304 | tf_op jit(solution)/shard_map/ppermute | solution.py:238
  19.3 13.6 %collective-permute-start.8 = (bf16[2,65,16,128]{3,2,1,0:T(8,128)(2,1)}, bf16[2,65,16,128]{3,2,1,0:T(8,128)(2,1)}, u32[]{:S(2)}, u32[]{:S(2)}) collective-permute-start(bf16[2,65,16,128]{3,2,1,0:T(8,128)(2,1)} %collective-permute-done.7.refs_2_), channel_id=1, source_target_pairs={{0,2},{1,3},{4,0},{5,1},{8,4},{9,5},{12,8},{13,9},{14,12},{15,13},... | collective-permute-start | bytes 1597448 | tf_op jit(solution)/shard_map/ppermute | solution.py:237
  21.0 13.3 %collective-permute-start.4 = (bf16[2,65,16,128]{3,2,1,0:T(8,128)(2,1)}, bf16[2,65,16,128]{3,2,1,0:T(8,128)(2,1)}, u32[]{:S(2)}, u32[]{:S(2)}) collective-permute-start(bf16[2,65,16,128]{3,2,1,0:T(8,128)(2,1)} %collective-permute-done.3.refs_1_), channel_id=1, source_target_pairs={{0,4},{1,5},{4,8},{5,9},{8,12},{9,13},{12,14},{13,15},{14,10},{15,... | collective-permute-start | bytes 1597448 | tf_op jit(solution)/shard_map/ppermute | solution.py:236
  32.9 18.0 %collective-permute-start.9 = (bf16[2,65,16,128]{3,2,1,0:T(8,128)(2,1)}, bf16[2,65,16,128]{3,2,1,0:T(8,128)(2,1)S(1)}, u32[]{:S(2)}, u32[]{:S(2)}) collective-permute-start(bf16[2,65,16,128]{3,2,1,0:T(8,128)(2,1)} %collective-permute-done.8.refs_2_), channel_id=1, source_target_pairs={{0,2},{1,3},{4,0},{5,1},{8,4},{9,5},{12,8},{13,9},{14,12},{15,13},... | collective-permute-start | bytes 1597448 | tf_op jit(solution)/shard_map/ppermute | solution.py:237
  34.3 18.1 %collective-permute-start.5 = (bf16[2,65,16,128]{3,2,1,0:T(8,128)(2,1)}, bf16[2,65,16,128]{3,2,1,0:T(8,128)(2,1)S(1)}, u32[]{:S(2)}, u32[]{:S(2)}) collective-permute-start(bf16[2,65,16,128]{3,2,1,0:T(8,128)(2,1)} %collective-permute-done.4.refs_1_), channel_id=1, source_target_pairs={{0,4},{1,5},{4,8},{5,9},{8,12},{9,13},{12,14},{13,15},{14,10},{15,... | collective-permute-start | bytes 1597448 | tf_op jit(solution)/shard_map/ppermute | solution.py:236
  35.1 1.1 copy-start.1
  36.2 1.1 copy-start.3
  37.3 1.0 copy-start.6
  51.0 7.7 %collective-permute-start.10 = (bf16[1,65,16,128]{3,2,1,0:T(8,128)(2,1)S(1)}, bf16[1,65,16,128]{3,2,1,0:T(8,128)(2,1)S(1)}, u32[]{:S(2)}, u32[]{:S(2)}) collective-permute-start(bf16[1,65,16,128]{3,2,1,0:T(8,128)(2,1)S(1)} %slice.33), channel_id=1, source_target_pairs={{0,2},{1,3},{4,0},{5,1},{8,4},{9,5},{12,8},{13,9},{14,12},{15,13},... | collective-permute-start | bytes 798728 | tf_op jit(solution)/shard_map/ppermute | solution.py:237
  52.4 6.6 %collective-permute-start.6 = (bf16[1,65,16,128]{3,2,1,0:T(8,128)(2,1)S(1)}, bf16[1,65,16,128]{3,2,1,0:T(8,128)(2,1)S(1)}, u32[]{:S(2)}, u32[]{:S(2)}) collective-permute-start(bf16[1,65,16,128]{3,2,1,0:T(8,128)(2,1)S(1)} %slice.32), channel_id=1, source_target_pairs={{0,4},{1,5},{4,8},{5,9},{8,12},{9,13},{12,14},{13,15},{14,10},{15,... | collective-permute-start | bytes 798728 | tf_op jit(solution)/shard_map/ppermute | solution.py:236
  56.0 3.1 %copy-start.2 = (bf16[1,1024,384]{2,1,0:T(8,128)(2,1)S(1)}, bf16[1,1024,384]{2,1,0:T(8,128)(2,1)}, u32[]{:S(2)}) copy-start(bf16[1,1024,384]{2,1,0:T(8,128)(2,1)} %param.12) | copy-start | bytes 2359300
  56.0 3.1 %copy-start.4 = (bf16[1,384,1024]{2,1,0:T(8,128)(2,1)S(1)}, bf16[1,384,1024]{2,1,0:T(8,128)(2,1)}, u32[]{:S(2)}) copy-start(bf16[1,384,1024]{2,1,0:T(8,128)(2,1)} %param.13) | copy-start | bytes 2359300
  62.3 7.6 %collective-permute-start.15 = (bf16[1,33,16,128]{3,2,1,0:T(8,128)(2,1)S(1)}, bf16[1,33,16,128]{3,2,1,0:T(8,128)(2,1)S(1)}, u32[]{:S(2)}, u32[]{:S(2)}) collective-permute-start(bf16[1,33,16,128]{3,2,1,0:T(8,128)(2,1)S(1)} %get-tuple-element.73), channel_id=1, source_target_pairs={{0,4},{1,5},{4,8},{5,9},{8,12},{9,13},{12,14},{13,15},{14,10},{15,... | collective-permute-start | bytes 405512 | tf_op jit(solution)/shard_map/ppermute | solution.py:236
  68.9 6.5 %collective-permute-start.11 = (bf16[1,33,16,128]{3,2,1,0:T(8,128)(2,1)S(1)}, bf16[1,33,16,128]{3,2,1,0:T(8,128)(2,1)S(1)}, u32[]{:S(2)}, u32[]{:S(2)}) collective-permute-start(bf16[1,33,16,128]{3,2,1,0:T(8,128)(2,1)S(1)} %get-tuple-element.68), channel_id=1, source_target_pairs={{0,2},{1,3},{4,0},{5,1},{8,4},{9,5},{12,8},{13,9},{14,12},{15,13},... | collective-permute-start | bytes 405512 | tf_op jit(solution)/shard_map/ppermute | solution.py:237
  69.9 8.4 %collective-permute-start.16 = (bf16[2,33,16,128]{3,2,1,0:T(8,128)(2,1)S(1)}, bf16[2,33,16,128]{3,2,1,0:T(8,128)(2,1)S(1)}, u32[]{:S(2)}, u32[]{:S(2)}) collective-permute-start(bf16[2,33,16,128]{3,2,1,0:T(8,128)(2,1)S(1)} %pad_maximum_fusion.1), channel_id=1, source_target_pairs={{0,4},{1,5},{4,8},{5,9},{8,12},{9,13},{12,14},{13,15},{14,10},{15,... | collective-permute-start | bytes 811016 | tf_op jit(solution)/shard_map/ppermute | solution.py:236
  75.4 6.5 %collective-permute-start.12 = (bf16[2,33,16,128]{3,2,1,0:T(8,128)(2,1)S(1)}, bf16[2,33,16,128]{3,2,1,0:T(8,128)(2,1)S(1)}, u32[]{:S(2)}, u32[]{:S(2)}) collective-permute-start(bf16[2,33,16,128]{3,2,1,0:T(8,128)(2,1)S(1)} %pad_maximum_fusion), channel_id=1, source_target_pairs={{0,2},{1,3},{4,0},{5,1},{8,4},{9,5},{12,8},{13,9},{14,12},{15,13},... | collective-permute-start | bytes 811016 | tf_op jit(solution)/shard_map/ppermute | solution.py:237
  76.9 10.4 %collective-permute-start.22 = (bf16[192,1024]{1,0:T(8,128)(2,1)S(1)}, bf16[192,1024]{1,0:T(8,128)(2,1)S(1)}, u32[]{:S(2)}, u32[]{:S(2)}) collective-permute-start(bf16[192,1024]{1,0:T(8,128)(2,1)S(1)} %get-tuple-element.125), channel_id=1, source_target_pairs={{0,1},{1,0},{2,3},{3,2},{4,5},{5,4},{6,7},{7,6},{8,9},{9,8},{10,11... | collective-permute-start | bytes 1179656 | tf_op jit(solution)/shard_map/ppermute | solution.py:238
  77.0 11.6 %collective-permute-start.21 = (bf16[512,768]{1,0:T(8,128)(2,1)S(1)}, bf16[512,768]{1,0:T(8,128)(2,1)S(1)}, u32[]{:S(2)}, u32[]{:S(2)}) collective-permute-start(bf16[512,768]{1,0:T(8,128)(2,1)S(1)} %get-tuple-element.124), channel_id=1, source_target_pairs={{0,1},{1,0},{2,3},{3,2},{4,5},{5,4},{6,7},{7,6},{8,9},{9,8},{10,11... | collective-permute-start | bytes 2359304 | tf_op jit(solution)/shard_map/ppermute | solution.py:238
  78.1 14.1 %collective-permute-start.19 = (bf16[512,768]{1,0:T(8,128)(2,1)S(1)}, bf16[512,768]{1,0:T(8,128)(2,1)S(1)}, u32[]{:S(2)}, u32[]{:S(2)}) collective-permute-start(bf16[512,768]{1,0:T(8,128)(2,1)S(1)} %get-tuple-element.118), channel_id=1, source_target_pairs={{0,1},{1,0},{2,3},{3,2},{4,5},{5,4},{6,7},{7,6},{8,9},{9,8},{10,11... | collective-permute-start | bytes 2359304 | tf_op jit(solution)/shard_map/ppermute | solution.py:238
  78.4 8.9 %collective-permute-start.17 = (bf16[2,33,16,128]{3,2,1,0:T(8,128)(2,1)S(1)}, bf16[2,33,16,128]{3,2,1,0:T(8,128)(2,1)S(1)}, u32[]{:S(2)}, u32[]{:S(2)}) collective-permute-start(bf16[2,33,16,128]{3,2,1,0:T(8,128)(2,1)S(1)} %add_convert_fusion.3), channel_id=1, source_target_pairs={{0,4},{1,5},{4,8},{5,9},{8,12},{9,13},{12,14},{13,15},{14,10},{15,... | collective-permute-start | bytes 811016 | tf_op jit(solution)/shard_map/ppermute | solution.py:236
  82.0 8.7 %collective-permute-start.13 = (bf16[2,33,16,128]{3,2,1,0:T(8,128)(2,1)S(1)}, bf16[2,33,16,128]{3,2,1,0:T(8,128)(2,1)S(1)}, u32[]{:S(2)}, u32[]{:S(2)}) collective-permute-start(bf16[2,33,16,128]{3,2,1,0:T(8,128)(2,1)S(1)} %add_convert_fusion.5), channel_id=1, source_target_pairs={{0,2},{1,3},{4,0},{5,1},{8,4},{9,5},{12,8},{13,9},{14,12},{15,13},... | collective-permute-start | bytes 811016 | tf_op jit(solution)/shard_map/ppermute | solution.py:237
  87.3 4.6 %collective-permute-start.20 = (bf16[192,1024]{1,0:T(8,128)(2,1)S(1)}, bf16[192,1024]{1,0:T(8,128)(2,1)S(1)}, u32[]{:S(2)}, u32[]{:S(2)}) collective-permute-start(bf16[192,1024]{1,0:T(8,128)(2,1)S(1)} %get-tuple-element.119), channel_id=1, source_target_pairs={{0,1},{1,0},{2,3},{3,2},{4,5},{5,4},{6,7},{7,6},{8,9},{9,8},{10,11... | collective-permute-start | bytes 1179656 | tf_op jit(solution)/shard_map/ppermute | solution.py:238
  87.3 8.9 %collective-permute-start.18 = (bf16[2,33,16,128]{3,2,1,0:T(8,128)(2,1)S(1)}, bf16[2,33,16,128]{3,2,1,0:T(8,128)(2,1)S(1)}, u32[]{:S(2)}, u32[]{:S(2)}) collective-permute-start(bf16[2,33,16,128]{3,2,1,0:T(8,128)(2,1)S(1)} %add_convert_fusion.2), channel_id=1, source_target_pairs={{0,4},{1,5},{4,8},{5,9},{8,12},{9,13},{12,14},{13,15},{14,10},{15,... | collective-permute-start | bytes 811016 | tf_op jit(solution)/shard_map/ppermute | solution.py:236
  89.2 29.1 %collective-permute-start.23 = (bf16[512,768]{1,0:T(8,128)(2,1)S(1)}, bf16[512,768]{1,0:T(8,128)(2,1)S(1)}, u32[]{:S(2)}, u32[]{:S(2)}) collective-permute-start(bf16[512,768]{1,0:T(8,128)(2,1)S(1)} %get-tuple-element.126), channel_id=1, source_target_pairs={{0,16},{16,0},{1,17},{17,1},{2,18},{18,2},{3,19},{19,3},{4,20},{20... | collective-permute-start | bytes 2359304 | tf_op jit(solution)/shard_map/ppermute | solution.py:311
  90.9 8.4 %collective-permute-start.14 = (bf16[2,33,16,128]{3,2,1,0:T(8,128)(2,1)S(1)}, bf16[2,33,16,128]{3,2,1,0:T(8,128)(2,1)S(1)}, u32[]{:S(2)}, u32[]{:S(2)}) collective-permute-start(bf16[2,33,16,128]{3,2,1,0:T(8,128)(2,1)S(1)} %add_convert_fusion.4), channel_id=1, source_target_pairs={{0,2},{1,3},{4,0},{5,1},{8,4},{9,5},{12,8},{13,9},{14,12},{15,13},... | collective-permute-start | bytes 811016 | tf_op jit(solution)/shard_map/ppermute | solution.py:237
  91.8 7.4 %copy-start.10 = (s32[128,8]{0,1:T(8,128)S(1)}, s32[128,8]{0,1:T(8,128)}, u32[]{:S(2)}) copy-start(s32[128,8]{0,1:T(8,128)} %param.9) | copy-start | bytes 12292
  91.8 25.6 %collective-permute-start.24 = (bf16[192,1024]{1,0:T(8,128)(2,1)S(1)}, bf16[192,1024]{1,0:T(8,128)(2,1)S(1)}, u32[]{:S(2)}, u32[]{:S(2)}) collective-permute-start(bf16[192,1024]{1,0:T(8,128)(2,1)S(1)} %get-tuple-element.128), channel_id=1, source_target_pairs={{0,16},{16,0},{1,17},{17,1},{2,18},{18,2},{3,19},{19,3},{4,20},{20... | collective-permute-start | bytes 1179656 | tf_op jit(solution)/shard_map/ppermute | solution.py:311

commit v3 on v2

v3 whole, which is shorter than its diff:
```python
import functools

import jax
import jax.numpy as jnp
from jax import lax
from jax.experimental import pallas as pl
from jax.experimental.pallas import tpu as pltpu
from jax.sharding import PartitionSpec as P

BF16, F32 = jnp.bfloat16, jnp.float32
ROWS, LANES = 16, 128
VMEM = pl.BlockSpec(memory_space=pltpu.VMEM)
ANY = pl.BlockSpec(memory_space=pl.ANY)
SMEM = pl.BlockSpec(memory_space=pltpu.SMEM)
STEPS = 4
EXPERT_VMEM = 16 * 1024 * 1024
TOKEN = jax.ShapeDtypeStruct((8, LANES), F32)
PARAMS = pltpu.CompilerParams(vmem_limit_bytes=16 * 1024 * 1024)


def iota(shape, dim):
    return lax.broadcasted_iota(jnp.int32, shape, dim)


def kept(*shape, kind=BF16):
    return jax.ShapeDtypeStruct(shape, kind)


def put_tiles(ref, first, value):
    rows, width = value.shape
    across = width // LANES
    for i in range(rows // ROWS):
        for j in range(across):
            ref[first + i * across + j] = value[
                i * ROWS : (i + 1) * ROWS, j * LANES : (j + 1) * LANES
            ]


def take_tiles(ref, first, dst, row, rows, width):
    across = width // LANES
    for i in range(rows // ROWS):
        for j in range(across):
            dst[row + i * ROWS : row + (i + 1) * ROWS, j * LANES : (j + 1) * LANES] = ref[
                first + i * across + j
            ]


def pack_kernel(tok_ref, cot_ref, ids_ref, prob_ref, out_ref, token):
    tok_dev, width = tok_ref.shape
    half = tok_dev // 2
    block = half * width // (ROWS * LANES)
    token[...] = jnp.zeros_like(token)
    ids, prob = ids_ref[...], prob_ref[...].astype(F32)
    for i in range(out_ref.shape[1] - 2 * block):
        expert = iota((ROWS, tok_dev), 0) + i * ROWS
        dense = jnp.zeros((ROWS, tok_dev), F32)
        for k in range(ids.shape[0]):
            dense += jnp.where(ids[k : k + 1] == expert, prob[k : k + 1], 0.0)
        for n in range(2):
            out_ref[n, 2 * block + i] = dense.astype(BF16)
    for n in range(2):
        put_tiles(out_ref.at[n], 0, tok_ref[n * half : (n + 1) * half])
        put_tiles(out_ref.at[n], block, cot_ref[n * half : (n + 1) * half])


def put_strips(ref, e, at, value):
    rows, width = value.shape
    for j in range(width // LANES):
        ref[e, at + j * rows : at + (j + 1) * rows] = value[:, j * LANES : (j + 1) * LANES]


def take_strips(ref, e, at, rows, width):
    return jnp.concatenate(
        [ref[e, at + j * rows : at + (j + 1) * rows] for j in range(width // LANES)], axis=1
    )


def weights_kernel(*refs):
    out_ref = refs[6]
    for e in range(2):
        wg, wu, wd = (ref[...] for ref in refs[3 * e : 3 * e + 3])
        width, ff = wg.shape
        put_strips(out_ref, e, 0, jnp.concatenate([wg, wu], axis=1))
        put_strips(out_ref, e, 2 * ff // LANES * width, wd.T)
        put_strips(out_ref, e, 3 * ff // LANES * width, jnp.concatenate([wg.T, wu.T], axis=0))


def expert_kernel(halves, half, width, ff, start, last, *refs):
    count = len(halves)
    me_ref, refs = refs[0], refs[2:]
    packets, refs = refs[:count], refs[count:]
    weights, refs = refs[0], refs[1:]
    if start:
        before, refs = refs[0], refs[1:]
    grads, refs = refs[:count], refs[count:]
    if not last:
        totals, refs = refs[0], refs[1:]
    token, refs = refs[0], refs[1:]
    xt_ref, outs, (x_ref, dy_ref) = refs[0], (refs[1:4], refs[4:7]), refs[7:]
    token[...] = jnp.zeros_like(token)
    block = half * width // (ROWS * LANES)
    pieces = [
        (ref.at[i], grad.at[i], which)
        for ref, grad, names in zip(packets, grads, halves)
        for i, which in enumerate(names)
    ]
    extra = packets[0].shape[1] - 2 * block
    eyes = [iota((half, LANES), 0) + n * half == iota((half, LANES), 1) for n in range(2)]
    for n, (ref, _, _) in enumerate(pieces):
        take_tiles(ref, 0, x_ref, n * half, half, width)
        take_tiles(ref, block, dy_ref, n * half, half, width)
    x, dy = x_ref[...], dy_ref[...]
    rows, by_expert = None, [[0.0] * extra for _ in pieces]
    for e in range(2):
        w_gu = take_strips(weights, e, 0, width, 2 * ff)
        w_d_t = take_strips(weights, e, 2 * ff // LANES * width, width, ff)
        w_gu_t = take_strips(weights, e, 3 * ff // LANES * width, 2 * ff, width)
        me = me_ref[e]
        mine = [iota((ROWS, LANES), 0) + i * ROWS == me for i in range(extra)]
        probs = []
        for ref, _, which in pieces:
            row = sum(
                jnp.sum(
                    jnp.where(mine[i], ref[2 * block + i].astype(F32), 0.0), axis=0, keepdims=True
                )
                for i in range(extra)
            )
            probs.append(jnp.sum(jnp.where(eyes[which], row, 0.0), axis=1, keepdims=True))
        prob = jnp.concatenate(probs, axis=0)
        both = jnp.dot(x, w_gu, preferred_element_type=F32)
        gate, up = both[:, :ff], both[:, ff:]
        dz = jnp.dot(dy, w_d_t, preferred_element_type=F32)
        sig = jax.nn.sigmoid(gate)
        act, dact = gate * sig, sig + gate * sig * (1.0 - sig)
        hidden = (act * up).astype(BF16)
        gate_grad = jnp.sum(dz * hidden.astype(F32), axis=1, keepdims=True)
        dh = prob * dz
        d_gate = (dh * up * dact).astype(BF16)
        d_up = (dh * act).astype(BF16)
        d_both = jnp.concatenate([d_gate, d_up], axis=1)
        back = jnp.dot(d_both, w_gu_t, preferred_element_type=F32)
        rows = back if rows is None else rows + back
        for n, (_, _, which) in enumerate(pieces):
            row = jnp.sum(
                jnp.where(eyes[which], gate_grad[n * half : (n + 1) * half], 0.0),
                axis=0,
                keepdims=True,
            )
            for i in range(extra):
                by_expert[n][i] += jnp.where(mine[i], row, 0.0)
        dgu_ref, ht_ref, sc_ref = outs[e]
        dgu_ref[...] = d_both
        ht_ref[...] = hidden.T
        sc_ref[...] = (prob * dy.astype(F32)).astype(BF16)
    for n, (_, grad, _) in enumerate(pieces):
        put_tiles(grad, 0, rows[n * half : (n + 1) * half].astype(BF16))
        for i in range(extra):
            grad[block + i] = by_expert[n][i].astype(BF16)
    xt_ref[...] = x.T
    if not last:
        for e, (dgu_ref, ht_ref, sc_ref) in enumerate(outs):
            at = 0
            for a, b in ((xt_ref, dgu_ref), (ht_ref, sc_ref)):
                rows = a.shape[0]
                tile = rows // STEPS
                for step in range(STEPS):
                    new = jnp.dot(
                        a[step * tile : (step + 1) * tile], b[...], preferred_element_type=F32
                    )
                    for j in range(b.shape[1] // LANES):
                        to = pl.ds(at + j * rows + step * tile, tile)
                        strip = new[:, j * LANES : (j + 1) * LANES]
                        totals[e, to] = before[e, to] + strip if start else strip
                at += rows * b.shape[1] // LANES


def weight_kernel(steps, part_ref, turn_ref, *refs):
    totals, xt, refs = refs[0], refs[1], refs[2:]
    groups, outs, token = (refs[:3], refs[3:6]), refs[6:8], refs[8]
    token[...] = jnp.zeros_like(token)
    for e, (dgu, ht, sc) in enumerate(groups):
        to = 0
        for step in range(steps):
            at = 0
            for a, b in ((xt, dgu), (ht, sc)):
                rows, across = a.shape[0], b.shape[1] // LANES
                tile = rows // STEPS
                first = pl.multiple_of((part_ref[0] * steps + step) * tile, tile)
                new = jnp.dot(a[pl.ds(first, tile)], b[...], preferred_element_type=F32)
                for j in range(across):
                    strip = new[:, j * LANES : (j + 1) * LANES]
                    strip += totals[e, pl.ds(at + j * rows + first, tile)]
                    for i in range(tile // ROWS):
                        outs[e][to + i * across + j] = strip[i * ROWS : (i + 1) * ROWS].astype(
                            BF16
                        )
                at += rows * across
                to += tile // ROWS * across


def weight_sums(turn, totals, group, part, parts):
    tiles = totals.size // (2 * parts * ROWS * LANES)
    return pl.pallas_call(
        functools.partial(weight_kernel, STEPS // parts),
        out_shape=(kept(tiles, ROWS, LANES),) * 2 + (TOKEN,),
        in_specs=[SMEM, ANY] + [VMEM] * (1 + len(group)),
        out_specs=(VMEM,) * 3,
        compiler_params=PARAMS,
        cost_estimate=pl.CostEstimate(
            flops=2 * totals.size * group[0].shape[1] // parts,
            bytes_accessed=16 * 2**20 // parts,
            transcendentals=0,
        ),
        name="weight_sums",
    )(part.astype(jnp.int32)[None], turn, totals, *group)


def finish_kernel(count, *refs):
    outs = refs[count:]
    width, ff = outs[2].shape[1], outs[0].shape[1]
    tile_w, tile_d = width // STEPS, ff // STEPS
    across_w, across_d = 2 * ff // LANES, width // LANES
    each = ff // LANES
    n = 0
    for step in range(outs[0].shape[0] // tile_w):
        for i in range(tile_w // ROWS):
            rows = slice(step * tile_w + i * ROWS, step * tile_w + (i + 1) * ROWS)
            for j in range(across_w):
                total = sum(ref[n + j].astype(F32) for ref in refs[:count]).astype(BF16)
                at = slice(j % each * LANES, (j % each + 1) * LANES)
                outs[j // each][rows, at] = total
            n += across_w
        for i in range(tile_d // ROWS):
            rows = slice(step * tile_d + i * ROWS, step * tile_d + (i + 1) * ROWS)
            for j in range(across_d):
                total = sum(ref[n + j].astype(F32) for ref in refs[:count]).astype(BF16)
                outs[2][rows, j * LANES : (j + 1) * LANES] = total
            n += across_d


def home_kernel(count, ids_ref, *refs):
    out_ref, prob_ref = refs[count:]
    tok_dev, width = out_ref.shape
    half = tok_dev // 2
    block = half * width // (ROWS * LANES)
    across = width // LANES
    sums = []
    for n in range(2):
        total = sum(ref[n].astype(F32) for ref in refs[:count])
        for i in range(half // ROWS):
            for j in range(across):
                out_ref[
                    n * half + i * ROWS : n * half + (i + 1) * ROWS, j * LANES : (j + 1) * LANES
                ] = total[i * across + j].astype(BF16)
        sums.append(total[block:])
    by_expert = sums[0] + sums[1]
    ids = ids_ref[...]
    for k in range(ids.shape[0]):
        row = jnp.zeros((1, tok_dev), F32)
        for i in range(by_expert.shape[0]):
            expert = iota((ROWS, tok_dev), 0) + i * ROWS
            row += jnp.sum(
                jnp.where(ids[k : k + 1] == expert, by_expert[i], 0.0), axis=0, keepdims=True
            )
        prob_ref[k : k + 1] = row


def on_device(tokens, cotangent, expert_ids, gate_probs, w_gate, w_up, w_down):
    tok_dev, width = tokens.shape
    ff = w_gate.shape[2]
    half = tok_dev // 2
    devices = lax.axis_size("expert")
    groups = lax.axis_size("dp")
    experts = devices * w_gate.shape[0]
    block = half * width // (ROWS * LANES)
    extra = experts // ROWS

    chips = devices // 2
    ring = list(range(0, chips, 2)) + list(range(1, chips, 2))[::-1]
    hop = {
        d: [
            (2 * ring[i] + c, 2 * ring[(i + d) % chips] + c)
            for i in range(chips)
            for c in range(2)
        ]
        for d in (1, -1)
    }
    right = lambda v: lax.ppermute(v, "expert", hop[1])
    left = lambda v: lax.ppermute(v, "expert", hop[-1])
    swap = lambda v: lax.ppermute(v, "expert", [(i, i ^ 1) for i in range(devices)])
    full, odd = (chips - 1) // 2, chips % 2 == 0

    me = lax.axis_index("expert").astype(jnp.int32)
    pair = jnp.stack([me, me ^ 1])
    ids_t, probs_t = expert_ids.T, gate_probs.T
    own = (w_gate[0], w_up[0], w_down[0])

    whole = lambda v: pl.BlockSpec(v.shape, lambda i: (0,) * len(v.shape))
    packet = jax.ShapeDtypeStruct((2, 2 * block + extra, ROWS, LANES), BF16)
    start, turn = pl.pallas_call(
        pack_kernel,
        grid=(1,),
        out_shape=(packet, TOKEN),
        in_specs=[whole(v) for v in (tokens, cotangent, ids_t, probs_t)],
        out_specs=(whole(packet), whole(TOKEN)),
        compiler_params=PARAMS,
        name="pack",
    )(*(pltpu.with_memory_space_constraint(v, pltpu.HBM) for v in (tokens, cotangent, ids_t, probs_t)))

    raw = own + tuple(swap(v) for v in own)
    weights = pl.pallas_call(
        weights_kernel,
        out_shape=kept(2, 5 * ff // LANES * width, LANES),
        in_specs=[VMEM] * 6,
        out_specs=VMEM,
        compiler_params=PARAMS,
        cost_estimate=pl.CostEstimate(flops=0, bytes_accessed=24 * width * ff, transcendentals=0),
        name="weights",
    )(*raw)

    def expert(turn, *packets, halves, totals=None, last=False):
        rows = half * sum(len(h) for h in halves)
        count = len(packets)
        groups = [(width, rows)] + [(rows, 2 * ff), (ff, rows), (rows, width)] * 2
        sums = (kept(2, 3 * ff // LANES * width, LANES, kind=F32),)
        start = totals is not None and not last
        out_shape = tuple(kept(len(h), block + extra, ROWS, LANES) for h in halves)
        out_shape += () if last else sums
        out_shape += (TOKEN,)
        scratch = [(rows, width), (rows, width)]
        if last:
            out_shape += tuple(kept(*s) for s in groups)
        else:
            scratch = groups + scratch
        inputs = (pair, turn, *packets, weights) + ((totals,) if start else ())
        outs = pl.pallas_call(
            functools.partial(expert_kernel, halves, half, width, ff, start, last),
            out_shape=out_shape,
            in_specs=[SMEM, ANY] + [VMEM] * (len(inputs) - 2),
            out_specs=(VMEM,) * len(out_shape),
            scratch_shapes=[pltpu.VMEM(s, BF16) for s in scratch],

            compiler_params=pltpu.CompilerParams(vmem_limit_bytes=EXPERT_VMEM),
            cost_estimate=pl.CostEstimate(
                flops=(20 if last else 32) * rows * width * ff,
                bytes_accessed=8 * 2**20,
                transcendentals=2 * rows * ff,
            ),
            name="expert",
        )(*inputs)
        grads, outs = outs[:count], outs[count:]
        if last:
            return grads, outs[1:], outs[0]
        return grads, outs[0], outs[1]

    both = (0, 1)
    totals = None
    r, l = right(start), left(start)
    (home,), totals, turn = expert(turn, start, halves=(both,))
    local = {}
    for s in range(1, full + 1):
        came = r, l
        r, l, turn = lax.optimization_barrier((r, l, turn))
        if s < full:
            r, l = right(r), left(l)
        elif odd:
            ends = right(r[:1]), left(l[1:])
        local[s], totals, turn = expert(turn, *came, halves=(both, both), totals=totals)
    assert odd, "even ring"
    *ends, turn = lax.optimization_barrier((*ends, turn))
    local[full + 1], group, turn = expert(turn, *ends, halves=((0,), (1,)), last=True)

    def add(*terms):
        return sum(t.astype(F32) for t in terms).astype(BF16)

    if groups == 2:
        here = lax.axis_index("dp")
        mine, other, turn = weight_sums(turn, totals, group, 1 - here, 2)
        send = add(mine, swap(other))
        mine, other, turn = weight_sums(turn, totals, group, here, 2)
        got = lax.ppermute(send, "dp", [(0, 1), (1, 0)])
        terms = (mine, swap(other), got)
        shape = lambda *s: jax.ShapeDtypeStruct(s, BF16)
        grads = pl.pallas_call(
            functools.partial(finish_kernel, len(terms)),
            out_shape=(shape(width // 2, ff), shape(width // 2, ff), shape(ff // 2, width)),
            in_specs=[VMEM] * len(terms),
            out_specs=(VMEM,) * 3,
            compiler_params=PARAMS,
            name="finish",
        )(*terms)
    else:
        mine, other, turn = weight_sums(turn, totals, group, jnp.int32(0), 1)
        terms = (add(mine, swap(other)),)
        shape = lambda *s: jax.ShapeDtypeStruct(s, BF16)
        grads = pl.pallas_call(
            functools.partial(finish_kernel, len(terms)),
            out_shape=(shape(width, ff), shape(width, ff), shape(ff, width)),
            in_specs=[VMEM] * len(terms),
            out_specs=(VMEM,) * 3,
            compiler_params=PARAMS,
            name="finish",
        )(*terms)
        grads = [lax.psum_scatter(v, "dp", scatter_dimension=0, tiled=True) for v in grads]

    def back(side, move):
        moving = None
        if odd:
            moving = move(local[full + 1][side])
        for s in range(full, 0, -1):
            here = local[s][side]
            if moving is None:
                moving = here
            else:
                if moving.shape != here.shape:
                    at = [(0, 1), (1, 0)][side]
                    moving = jnp.pad(moving, [at] + [(0, 0)] * (moving.ndim - 1))
                moving = add(moving, here)
            moving = move(moving)
        return moving

    parts = (home, back(0, left), back(1, right))
    grad_tokens, grad_probs = pl.pallas_call(
        functools.partial(home_kernel, len(parts)),
        out_shape=(
            jax.ShapeDtypeStruct((tok_dev, width), BF16),
            jax.ShapeDtypeStruct(ids_t.shape, F32),
        ),
        in_specs=[VMEM] * (1 + len(parts)),
        out_specs=(VMEM, VMEM),
        compiler_params=PARAMS,
        name="home",
    )(ids_t, *parts)
    return (
        grad_tokens,
        grad_probs.T.astype(BF16),
        *(v[None] for v in grads),
    )


def solution(mesh):
    return jax.shard_map(
        on_device,
        mesh=mesh,
        in_specs=(
            P(("dp", "expert"), None),
            P(("dp", "expert"), None),
            P(("dp", "expert"), None),
            P(("dp", "expert"), None),
            P("expert", None, None),
            P("expert", None, None),
            P("expert", None, None),
        ),
        out_specs=(
            P(("dp", "expert"), None),
            P(("dp", "expert"), None),
            P("expert", "dp", None),
            P("expert", "dp", None),
            P("expert", "dp", None),
        ),
        check_vma=False,
    )
```

time: 120 us -> 103 us (0.86)
  waiting for transfers between devices: 55.5 us -> 37 us
  local copies, waits for them, and re-layouts: 8.48 us -> 15.4 us
  Pallas kernels: 31.1 us -> 28.4 us
  starting transfers between devices: 21.3 us -> 20 us
    ppermute x8, waiting for transfers between devices: 32 us -> 16.6 us  [on_device(): left = lambda v: lax.ppermute(v, 'expert', hop[-1])]
    ppermute x2 -> x1, waiting for transfers between devices: 16.8 us -> 7.6 us  [on_device(): got = lax.ppermute(send, 'dp', [(0, 1), (1, 0)])]
    unnamed x24 -> x28, local copies, waits for them, and re-layouts: 7.46 us -> 15.4 us
    ppermute x8, starting transfers between devices: 11.2 us -> 3.37 us  [on_device(): left = lambda v: lax.ppermute(v, 'expert', hop[-1])]
    ppermute x8, starting transfers between devices: 6.82 us -> 13.9 us  [on_device(): right = lambda v: lax.ppermute(v, 'expert', hop[1])]
    ppermute x8, waiting for transfers between devices: 6.73 us -> 12.8 us  [on_device(): right = lambda v: lax.ppermute(v, 'expert', hop[1])]
    pallas_call x14 -> x10, Pallas kernels: 30.3 us -> 27.6 us  [the longest x5 20.7 us: expert(): pl.pallas_call(functools.partial(expert_kernel, halves, half, width, ff,...]
  transfers between devices with their start and end apart: 25 -> 22, of which waited for: 9 -> 13; matrix products, arithmetic and copies ran while one was open for 2% -> 1% of each run, Pallas kernels for 23% -> 23%
where the time goes in v3:
time: 103 us
  waiting for transfers between devices  37 us (36%)
  Pallas kernels  28.4 us (28%)
  starting transfers between devices  20 us (19%)
  local copies, waits for them, and re-layouts  15.4 us (15%)
  other arithmetic  1.35 us (1%)
    pallas_call x5, Pallas kernels, expert(): pl.pallas_call(functools.partial(expert_kernel, halves, half, width, ff,...  20.7 us
    ppermute x8, waiting for transfers between devices, on_device(): left = lambda v: lax.ppermute(v, 'expert', hop[-1])  16.6 us
    unnamed x28, local copies, waits for them, and re-layouts  15.4 us
    ppermute x8, starting transfers between devices, on_device(): right = lambda v: lax.ppermute(v, 'expert', hop[1])  13.9 us
    ppermute x8, waiting for transfers between devices, on_device(): right = lambda v: lax.ppermute(v, 'expert', hop[1])  12.8 us
    ppermute x1, waiting for transfers between devices, on_device(): got = lax.ppermute(send, 'dp', [(0, 1), (1, 0)])  7.6 us
    ppermute x8, starting transfers between devices, on_device(): left = lambda v: lax.ppermute(v, 'expert', hop[-1])  3.37 us
    pallas_call x2, Pallas kernels, weight_sums(): pl.pallas_call(functools.partial(weight_kernel, STEPS // parts), out_shap...  2.14 us
  transfers between devices with their start and end apart: 22, of which 13 were waited for; matrix products, arithmetic and copies ran while one was open for 1% of the time, Pallas kernels for 23%

profile of v3, /device:TPU:0, one launch (start us, length us, event | category | flops | bytes accessed | tf_op | source)
XLA Modules:
  0.0 102.9 jit_solution(16212922700006194410)
XLA Ops:
  0.6 0.5 collective-permute-start
  1.1 0.1 collective-permute-start.1
  1.2 0.4 collective-permute-start.2
  1.7 1.9 %pack.1 = (bf16[2,65,16,128]{3,2,1,0:T(8,128)(2,1)}, f32[8,128]{1,0:T(8,128)S(1)}) custom-call(bf16[128,1024]{1,0:T(8,128)(2,1)} %tok_ref.1, bf16[128,1024]{1,0:T(8,128)(2,1)} %cot_ref.1, s32[8,128]{1,0:T(8,128)} %bitcast.20, bf16[8,128]{1,0:T(8,128)(2,1)} %bitcast.22), custom_call_target="tpu_custom_call" | custom-call | tf_op jit(solution)/shard_map/pack/pallas_call | solution.py:300
  3.6 2.7 %collective-permute-start.3 = (bf16[2,65,16,128]{3,2,1,0:T(8,128)(2,1)}, bf16[2,65,16,128]{3,2,1,0:T(8,128)(2,1)S(1)}, u32[]{:S(2)}, u32[]{:S(2)}) collective-permute-start(bf16[2,65,16,128]{3,2,1,0:T(8,128)(2,1)} %get-tuple-element.55.refs_2_), channel_id=1, source_target_pairs={{0,4},{1,5},{4,8},{5,9},{8,12},{9,13},{12,14},{13,15},{14,10},{15,... | collective-permute-start | bytes 1597448 | tf_op jit(solution)/shard_map/ppermute | solution.py:288
  6.2 0.1 pad_add_fusion.refs_0_
  6.3 0.0 collective-permute-done.2.refs_5_
  6.3 0.0 copy-start.4
  6.3 1.1 %copy-done.4 = bf16[1,1024,384]{2,1,0:T(8,128)(2,1)S(1)} copy-done((bf16[1,1024,384]{2,1,0:T(8,128)(2,1)S(1)}, bf16[1,1024,384]{2,1,0:T(8,128)(2,1)}, u32[]{:S(2)}) %copy-start.4) | copy-done | bytes 786456
  7.5 1.1 %copy-done.5 = bf16[1,1024,384]{2,1,0:T(8,128)(2,1)S(1)} copy-done((bf16[1,1024,384]{2,1,0:T(8,128)(2,1)S(1)}, bf16[1,1024,384]{2,1,0:T(8,128)(2,1)}, u32[]{:S(2)}) %copy-start.5) | copy-done | bytes 786456
  8.6 1.1 %copy-done.6 = bf16[1,384,1024]{2,1,0:T(8,128)(2,1)S(1)} copy-done((bf16[1,384,1024]{2,1,0:T(8,128)(2,1)S(1)}, bf16[1,384,1024]{2,1,0:T(8,128)(2,1)}, u32[]{:S(2)}) %copy-start.6) | copy-done | bytes 786456
  9.7 1.4 %weights.1.refs_3_.refs_4_ = bf16[2,15360,128]{2,1,0:T(8,128)(2,1)S(1)} custom-call(bf16[1024,384]{1,0:T(8,128)(2,1)S(1)} %bitcast.15, bf16[1024,384]{1,0:T(8,128)(2,1)S(1)} %bitcast.17, bf16[384,1024]{1,0:T(8,128)(2,1)S(1)} %bitcast.19, bf16[1024,384]{1,0:T(8,128)(2,1)S(1)} %collective-permute-done.refs_3_, ...), custom_call_target="tpu_custom_call" | custom-call | bytes 9437184 | tf_op jit(solution)/shard_map/weights/pallas_call | solution.py:311
  11.2 4.3 %expert.5 = (bf16[2,33,16,128]{3,2,1,0:T(8,128)(2,1)S(1)}, f32[2,9216,128]{2,1,0:T(8,128)S(1)}, f32[8,128]{1,0:T(8,128)S(1)}) custom-call(s32[2]{0:T(128)S(1)} %pad_add_fusion.refs_0_, f32[8,128]{1,0:T(8,128)S(1)} %get-tuple-element.54.refs_1_, bf16[2,65,16,128]{3,2,1,0:T(8,128)(2,1)} %get-tuple-element.55.refs_2_, ...), custom_call_target="tpu_custom_call" | custom-call | flops 1610612736 | bytes 8388608 | tf_op jit(solution)/shard_map/expert/pallas_call | solution.py:336
  15.5 0.0 copy-start.7
  15.5 3.6 %collective-permute-done.3.refs_2_ = bf16[2,65,16,128]{3,2,1,0:T(8,128)(2,1)S(1)} collective-permute-done((bf16[2,65,16,128]{3,2,1,0:T(8,128)(2,1)}, bf16[2,65,16,128]{3,2,1,0:T(8,128)(2,1)S(1)}, u32[]{:S(2)}, u32[]{:S(2)}) %collective-permute-start.3) | collective-permute-done | bytes 532512 | tf_op jit(solution)/shard_map/ppermute | solution.py:288
  19.1 1.5 %collective-permute-done.4.refs_3_ = bf16[2,65,16,128]{3,2,1,0:T(8,128)(2,1)S(1)} collective-permute-done((bf16[2,65,16,128]{3,2,1,0:T(8,128)(2,1)}, bf16[2,65,16,128]{3,2,1,0:T(8,128)(2,1)S(1)}, u32[]{:S(2)}, u32[]{:S(2)}) %collective-permute-start.4) | collective-permute-done | bytes 532512 | tf_op jit(solution)/shard_map/ppermute | solution.py:289
  20.6 1.6 %collective-permute-start.5 = (bf16[2,65,16,128]{3,2,1,0:T(8,128)(2,1)S(1)}, bf16[2,65,16,128]{3,2,1,0:T(8,128)(2,1)S(1)}, u32[]{:S(2)}, u32[]{:S(2)}) collective-permute-start(bf16[2,65,16,128]{3,2,1,0:T(8,128)(2,1)S(1)} %collective-permute-done.3.refs_2_), channel_id=1, source_target_pairs={{0,4},{1,5},{4,8},{5,9},{8,12},{9,13},{12,14},{13,15},{14,10},{15,... | collective-permute-start | bytes 1597448 | tf_op jit(solution)/shard_map/ppermute | solution.py:288
  22.2 0.4 collective-permute-start.6
  22.6 4.9 %expert.6 = (bf16[2,33,16,128]{3,2,1,0:T(8,128)(2,1)S(1)}, bf16[2,33,16,128]{3,2,1,0:T(8,128)(2,1)S(1)}, f32[2,9216,128]{2,1,0:T(8,128)S(1)}, f32[8,128]{1,0:T(8,128)S(1)}) custom-call(s32[2]{0:T(128)S(1)} %pad_add_fusion.refs_0_, f32[8,128]{1,0:T(8,128)S(1)} %get-tuple-element.60.refs_1_, bf16[2,65,16,128]{3,2,1,0:T(8,128)(2,1)S(1)} %collective-permute-done.3.refs_2_, ...), custom_call_target="tpu_custom_call" | custom-call | flops 3221225472 | bytes 8388608 | tf_op jit(solution)/shard_map/expert/pallas_call | solution.py:336
  27.5 3.6 %copy-done.2 = f32[2,9216,128]{2,1,0:T(8,128)} copy-done((f32[2,9216,128]{2,1,0:T(8,128)}, f32[2,9216,128]{2,1,0:T(8,128)S(1)}, u32[]{:S(2)}) %copy-start.2) | copy-done | bytes 9437208
  31.2 0.7 copy-done.9
  31.9 0.7 copy-done.11
  32.6 1.4 %collective-permute-done.5.refs_2_ = bf16[2,65,16,128]{3,2,1,0:T(8,128)(2,1)S(1)} collective-permute-done((bf16[2,65,16,128]{3,2,1,0:T(8,128)(2,1)S(1)}, bf16[2,65,16,128]{3,2,1,0:T(8,128)(2,1)S(1)}, u32[]{:S(2)}, u32[]{:S(2)}) %collective-permute-start.5) | collective-permute-done | bytes 532512 | tf_op jit(solution)/shard_map/ppermute | solution.py:288
  33.9 1.3 %collective-permute-done.6.refs_3_ = bf16[2,65,16,128]{3,2,1,0:T(8,128)(2,1)S(1)} collective-permute-done((bf16[2,65,16,128]{3,2,1,0:T(8,128)(2,1)S(1)}, bf16[2,65,16,128]{3,2,1,0:T(8,128)(2,1)S(1)}, u32[]{:S(2)}, u32[]{:S(2)}) %collective-permute-start.6) | collective-permute-done | bytes 532512 | tf_op jit(solution)/shard_map/ppermute | solution.py:289
  35.2 1.6 %collective-permute-start.7 = (bf16[2,65,16,128]{3,2,1,0:T(8,128)(2,1)S(1)}, bf16[2,65,16,128]{3,2,1,0:T(8,128)(2,1)S(1)}, u32[]{:S(2)}, u32[]{:S(2)}) collective-permute-start(bf16[2,65,16,128]{3,2,1,0:T(8,128)(2,1)S(1)} %collective-permute-done.5.refs_2_), channel_id=1, source_target_pairs={{0,4},{1,5},{4,8},{5,9},{8,12},{9,13},{12,14},{13,15},{14,10},{15,... | collective-permute-start | bytes 1597448 | tf_op jit(solution)/shard_map/ppermute | solution.py:288
  36.8 0.5 collective-permute-start.8
  37.3 3.2 %copy-done.1 = bf16[2,15360,128]{2,1,0:T(8,128)(2,1)S(1)} copy-done((bf16[2,15360,128]{2,1,0:T(8,128)(2,1)S(1)}, bf16[2,15360,128]{2,1,0:T(8,128)(2,1)}, u32[]{:S(2)}) %copy-start.1) | copy-done | bytes 7864344
  40.5 3.7 %copy-done.3 = f32[2,9216,128]{2,1,0:T(8,128)S(1)} copy-done((f32[2,9216,128]{2,1,0:T(8,128)S(1)}, f32[2,9216,128]{2,1,0:T(8,128)}, u32[]{:S(2)}) %copy-start.3) | copy-done | bytes 9437208
  44.2 4.7 %expert.7 = (bf16[2,33,16,128]{3,2,1,0:T(8,128)(2,1)S(1)}, bf16[2,33,16,128]{3,2,1,0:T(8,128)(2,1)S(1)}, f32[2,9216,128]{2,1,0:T(8,128)S(1)}, f32[8,128]{1,0:T(8,128)S(1)}) custom-call(s32[2]{0:T(128)S(1)} %pad_add_fusion.refs_0_, f32[8,128]{1,0:T(8,128)S(1)} %get-tuple-element.65.refs_1_, bf16[2,65,16,128]{3,2,1,0:T(8,128)(2,1)S(1)} %collective-permute-done.5.refs_2_, ...), custom_call_target="tpu_custom_call" | custom-call | flops 3221225472 | bytes 8388608 | tf_op jit(solution)/shard_map/expert/pallas_call | solution.py:336
  48.9 1.6 %collective-permute-start.9 = (bf16[1,65,16,128]{3,2,1,0:T(8,128)(2,1)S(1)}, bf16[1,65,16,128]{3,2,1,0:T(8,128)(2,1)S(1)}, u32[]{:S(2)}, u32[]{:S(2)}) collective-permute-start(bf16[1,65,16,128]{3,2,1,0:T(8,128)(2,1)S(1)} %slice.6), channel_id=1, source_target_pairs={{0,4},{1,5},{4,8},{5,9},{8,12},{9,13},{12,14},{13,15},{14,10},{15,... | collective-permute-start | bytes 798728 | tf_op jit(solution)/shard_map/ppermute | solution.py:288
  50.6 0.5 collective-permute-start.10
  51.1 4.7 %expert.8 = (bf16[2,33,16,128]{3,2,1,0:T(8,128)(2,1)S(1)}, bf16[2,33,16,128]{3,2,1,0:T(8,128)(2,1)S(1)}, f32[2,9216,128]{2,1,0:T(8,128)S(1)}, f32[8,128]{1,0:T(8,128)S(1)}) custom-call(s32[2]{0:T(128)S(1)} %pad_add_fusion.refs_0_, f32[8,128]{1,0:T(8,128)S(1)} %get-tuple-element.70.refs_1_, bf16[2,65,16,128]{3,2,1,0:T(8,128)(2,1)S(1)} %collective-permute-done.7.refs_2_, ...), custom_call_target="tpu_custom_call" | custom-call | flops 3221225472 | bytes 8388608 | tf_op jit(solution)/shard_map/expert/pallas_call | solution.py:336
  55.8 1.2 %collective-permute-done.10.refs_3_ = bf16[1,65,16,128]{3,2,1,0:T(8,128)(2,1)S(1)} collective-permute-done((bf16[1,65,16,128]{3,2,1,0:T(8,128)(2,1)S(1)}, bf16[1,65,16,128]{3,2,1,0:T(8,128)(2,1)S(1)}, u32[]{:S(2)}, u32[]{:S(2)}) %collective-permute-start.10) | collective-permute-done | bytes 266272 | tf_op jit(solution)/shard_map/ppermute | solution.py:289
  57.1 2.1 %expert.9 = (bf16[1,33,16,128]{3,2,1,0:T(8,128)(2,1)S(1)}, bf16[1,33,16,128]{3,2,1,0:T(8,128)(2,1)S(1)}, f32[8,128]{1,0:T(8,128)S(1)}, bf16[1024,128]{1,0:T(8,12...) custom-call(s32[2]{0:T(128)S(1)} %pad_add_fusion.refs_0_, ...), custom_call_target="tpu_custom_call" | custom-call | flops 1006632960 | bytes 8388608 | tf_op jit(solution)/shard_map/expert/pallas_call | solution.py:336
  59.2 0.8 weight_sums.2
  60.0 0.1 collective-permute-start.20
  60.1 0.5 collective-permute-start.11
  60.6 1.6 %collective-permute-start.15 = (bf16[1,33,16,128]{3,2,1,0:T(8,128)(2,1)S(1)}, bf16[1,33,16,128]{3,2,1,0:T(8,128)(2,1)S(1)}, u32[]{:S(2)}, u32[]{:S(2)}) collective-permute-start(bf16[1,33,16,128]{3,2,1,0:T(8,128)(2,1)S(1)} %get-tuple-element.80), channel_id=1, source_target_pairs={{0,4},{1,5},{4,8},{5,9},{8,12},{9,13},{12,14},{13,15},{14,10},{15,... | collective-permute-start | bytes 405512 | tf_op jit(solution)/shard_map/ppermute | solution.py:288
  62.2 3.9 %collective-permute-done.11 = bf16[1,33,16,128]{3,2,1,0:T(8,128)(2,1)S(1)} collective-permute-done((bf16[1,33,16,128]{3,2,1,0:T(8,128)(2,1)S(1)}, bf16[1,33,16,128]{3,2,1,0:T(8,128)(2,1)S(1)}, u32[]{:S(2)}, u32[]{:S(2)}) %collective-permute-start.11) | collective-permute-done | bytes 135200 | tf_op jit(solution)/shard_map/ppermute | solution.py:289
  66.1 0.1 add_convert_fusion.6
  66.1 0.5 collective-permute-start.12
  66.6 1.3 %weight_sums.3 = (bf16[288,16,128]{2,1,0:T(8,128)(2,1)S(1)}, bf16[288,16,128]{2,1,0:T(8,128)(2,1)S(1)}, f32[8,128]{1,0:T(8,128)}) custom-call(s32[1]{0:T(128)} %bitcast.8.part_ref, f32[8,128]{1,0:T(8,128)S(1)} %get-tuple-element.95.turn_ref, f32[2,9216,128]{2,1,0:T(8,128)S(1)} %get-tuple-element.87.refs_0_, bf16[1024,128]{1,0:T(8,128)(2,1)S(1)} %get-tuple-element.88.refs_1_, ...), custom_call_target="tpu_custom_call" | custom-call | flops 301989888 | bytes 8388608 | tf_op jit(solution)/shard_map/weight_sums/pallas_call | solution.py:203
  68.0 1.6 %collective-permute-start.16 = (bf16[2,33,16,128]{3,2,1,0:T(8,128)(2,1)S(1)}, bf16[2,33,16,128]{3,2,1,0:T(8,128)(2,1)S(1)}, u32[]{:S(2)}, u32[]{:S(2)}) collective-permute-start(bf16[2,33,16,128]{3,2,1,0:T(8,128)(2,1)S(1)} %add_convert_fusion.3), channel_id=1, source_target_pairs={{0,4},{1,5},{4,8},{5,9},{8,12},{9,13},{12,14},{13,15},{14,10},{15,... | collective-permute-start | bytes 811016 | tf_op jit(solution)/shard_map/ppermute | solution.py:288
  69.6 4.6 %collective-permute-done.12 = bf16[2,33,16,128]{3,2,1,0:T(8,128)(2,1)S(1)} collective-permute-done((bf16[2,33,16,128]{3,2,1,0:T(8,128)(2,1)S(1)}, bf16[2,33,16,128]{3,2,1,0:T(8,128)(2,1)S(1)}, u32[]{:S(2)}, u32[]{:S(2)}) %collective-permute-start.12) | collective-permute-done | bytes 270368 | tf_op jit(solution)/shard_map/ppermute | solution.py:289
  74.2 0.1 add_convert_fusion.5
  74.3 0.5 collective-permute-start.13
  74.8 0.3 add_convert_fusion
  75.1 0.0 copy-start.10
  75.1 1.6 %collective-permute-start.21 = (bf16[288,16,128]{2,1,0:T(8,128)(2,1)S(1)}, bf16[288,16,128]{2,1,0:T(8,128)(2,1)S(1)}, u32[]{:S(2)}, u32[]{:S(2)}) collective-permute-start(bf16[288,16,128]{2,1,0:T(8,128)(2,1)S(1)} %add_convert_fusion), channel_id=1, source_target_pairs={{0,16},{16,0},{1,17},{17,1},{2,18},{18,2},{3,19},{19,3},{4,20},{20... | collective-permute-start | bytes 3538952 | tf_op jit(solution)/shard_map/ppermute | solution.py:381
  76.7 0.3 collective-permute-done.16
  77.0 0.1 add_convert_fusion.2
  77.0 1.6 %collective-permute-start.17 = (bf16[2,33,16,128]{3,2,1,0:T(8,128)(2,1)S(1)}, bf16[2,33,16,128]{3,2,1,0:T(8,128)(2,1)S(1)}, u32[]{:S(2)}, u32[]{:S(2)}) collective-permute-start(bf16[2,33,16,128]{3,2,1,0:T(8,128)(2,1)S(1)} %add_convert_fusion.2), channel_id=1, source_target_pairs={{0,4},{1,5},{4,8},{5,9},{8,12},{9,13},{12,14},{13,15},{14,10},{15,... | collective-permute-start | bytes 811016 | tf_op jit(solution)/shard_map/ppermute | solution.py:288
  78.7 2.8 %collective-permute-done.13 = bf16[2,33,16,128]{3,2,1,0:T(8,128)(2,1)S(1)} collective-permute-done((bf16[2,33,16,128]{3,2,1,0:T(8,128)(2,1)S(1)}, bf16[2,33,16,128]{3,2,1,0:T(8,128)(2,1)S(1)}, u32[]{:S(2)}, u32[]{:S(2)}) %collective-permute-start.13) | collective-permute-done | bytes 270368 | tf_op jit(solution)/shard_map/ppermute | solution.py:289
  81.5 0.1 add_convert_fusion.4
  81.6 0.5 collective-permute-start.14
  82.1 3.1 %collective-permute-done.17 = bf16[2,33,16,128]{3,2,1,0:T(8,128)(2,1)S(1)} collective-permute-done((bf16[2,33,16,128]{3,2,1,0:T(8,128)(2,1)S(1)}, bf16[2,33,16,128]{3,2,1,0:T(8,128)(2,1)S(1)}, u32[]{:S(2)}, u32[]{:S(2)}) %collective-permute-start.17) | collective-permute-done | bytes 270368 | tf_op jit(solution)/shard_map/ppermute | solution.py:288
  85.2 0.1 add_convert_fusion.1
  85.3 1.6 %collective-permute-start.18 = (bf16[2,33,16,128]{3,2,1,0:T(8,128)(2,1)S(1)}, bf16[2,33,16,128]{3,2,1,0:T(8,128)(2,1)S(1)}, u32[]{:S(2)}, u32[]{:S(2)}) collective-permute-start(bf16[2,33,16,128]{3,2,1,0:T(8,128)(2,1)S(1)} %add_convert_fusion.1), channel_id=1, source_target_pairs={{0,4},{1,5},{4,8},{5,9},{8,12},{9,13},{12,14},{13,15},{14,10},{15,... | collective-permute-start | bytes 811016 | tf_op jit(solution)/shard_map/ppermute | solution.py:288
  86.9 1.2 %collective-permute-done.14.refs_1_ = bf16[2,33,16,128]{3,2,1,0:T(8,128)(2,1)S(1)} collective-permute-done((bf16[2,33,16,128]{3,2,1,0:T(8,128)(2,1)S(1)}, bf16[2,33,16,128]{3,2,1,0:T(8,128)(2,1)S(1)}, u32[]{:S(2)}, u32[]{:S(2)}) %collective-permute-start.14) | collective-permute-done | bytes 270368 | tf_op jit(solution)/shard_map/ppermute | solution.py:289
  88.1 4.5 %collective-permute-done.18.refs_2_ = bf16[2,33,16,128]{3,2,1,0:T(8,128)(2,1)S(1)} collective-permute-done((bf16[2,33,16,128]{3,2,1,0:T(8,128)(2,1)S(1)}, bf16[2,33,16,128]{3,2,1,0:T(8,128)(2,1)S(1)}, u32[]{:S(2)}, u32[]{:S(2)}) %collective-permute-start.18) | collective-permute-done | bytes 270368 | tf_op jit(solution)/shard_map/ppermute | solution.py:288
  92.6 0.8 home.1
  93.4 0.6 convert_bitcast_fusion
  94.0 7.6 %collective-permute-done.21.refs_2_ = bf16[288,16,128]{2,1,0:T(8,128)(2,1)S(1)} collective-permute-done((bf16[288,16,128]{2,1,0:T(8,128)(2,1)S(1)}, bf16[288,16,128]{2,1,0:T(8,128)(2,1)S(1)}, u32[]{:S(2)}, u32[]{:S(2)}) %collective-permute-start.21) | collective-permute-done | bytes 1179680 | tf_op jit(solution)/shard_map/ppermute | solution.py:381
  101.6 1.4 %finish.1 = (bf16[512,384]{1,0:T(8,128)(2,1)}, bf16[512,384]{1,0:T(8,128)(2,1)}, bf16[192,1024]{1,0:T(8,128)(2,1)}) custom-call(bf16[288,16,128]{2,1,0:T(8,128)(2,1)S(1)} %get-tuple-element.96.refs_0_, bf16[288,16,128]{2,1,0:T(8,128)(2,1)S(1)} %collective-permute-done.19.refs_1_, bf16[288,16,128]{2,1,0:T(8,128)(2,1)S(1)} %collective-permute-done.21.refs_2_), custom_call_target="tpu_custom_call" | custom-call | tf_op jit(solution)/shard_map/finish/pallas_call | solution.py:384
  (30 shorter events, 0.1 us)
Async XLA Ops:
  0.6 5.7 %collective-permute-start = (bf16[1024,384]{1,0:T(8,128)(2,1)}, bf16[1024,384]{1,0:T(8,128)(2,1)S(1)}, u32[]{:S(2)}, u32[]{:S(2)}) collective-permute-start(bf16[1024,384]{1,0:T(8,128)(2,1)} %bitcast.14), channel_id=1, source_target_pairs={{0,1},{1,0},{2,3},{3,2},{4,5},{5,4},{6,7},{7,6},{8,9},{9,8},{10,11... | collective-permute-start | bytes 2359304 | tf_op jit(solution)/shard_map/ppermute | solution.py:290
  1.1 5.2 %collective-permute-start.1 = (bf16[1024,384]{1,0:T(8,128)(2,1)}, bf16[1024,384]{1,0:T(8,128)(2,1)S(1)}, u32[]{:S(2)}, u32[]{:S(2)}) collective-permute-start(bf16[1024,384]{1,0:T(8,128)(2,1)} %bitcast.16), channel_id=1, source_target_pairs={{0,1},{1,0},{2,3},{3,2},{4,5},{5,4},{6,7},{7,6},{8,9},{9,8},{10,11... | collective-permute-start | bytes 2359304 | tf_op jit(solution)/shard_map/ppermute | solution.py:290
  1.2 5.1 %collective-permute-start.2 = (bf16[384,1024]{1,0:T(8,128)(2,1)}, bf16[384,1024]{1,0:T(8,128)(2,1)S(1)}, u32[]{:S(2)}, u32[]{:S(2)}) collective-permute-start(bf16[384,1024]{1,0:T(8,128)(2,1)} %bitcast.18), channel_id=1, source_target_pairs={{0,1},{1,0},{2,3},{3,2},{4,5},{5,4},{6,7},{7,6},{8,9},{9,8},{10,11... | collective-permute-start | bytes 2359304 | tf_op jit(solution)/shard_map/ppermute | solution.py:290
  3.6 15.5 %collective-permute-start.3 = (bf16[2,65,16,128]{3,2,1,0:T(8,128)(2,1)}, bf16[2,65,16,128]{3,2,1,0:T(8,128)(2,1)S(1)}, u32[]{:S(2)}, u32[]{:S(2)}) collective-permute-start(bf16[2,65,16,128]{3,2,1,0:T(8,128)(2,1)} %get-tuple-element.55.refs_2_), channel_id=1, source_target_pairs={{0,4},{1,5},{4,8},{5,9},{8,12},{9,13},{12,14},{13,15},{14,10},{15,... | collective-permute-start | bytes 1597448 | tf_op jit(solution)/shard_map/ppermute | solution.py:288
  6.2 14.4 %collective-permute-start.4 = (bf16[2,65,16,128]{3,2,1,0:T(8,128)(2,1)}, bf16[2,65,16,128]{3,2,1,0:T(8,128)(2,1)S(1)}, u32[]{:S(2)}, u32[]{:S(2)}) collective-permute-start(bf16[2,65,16,128]{3,2,1,0:T(8,128)(2,1)} %get-tuple-element.55.refs_2_), channel_id=1, source_target_pairs={{0,2},{1,3},{4,0},{5,1},{8,4},{9,5},{12,8},{13,9},{14,12},{15,13},... | collective-permute-start | bytes 1597448 | tf_op jit(solution)/shard_map/ppermute | solution.py:289
  6.3 1.1 %copy-start.4 = (bf16[1,1024,384]{2,1,0:T(8,128)(2,1)S(1)}, bf16[1,1024,384]{2,1,0:T(8,128)(2,1)}, u32[]{:S(2)}) copy-start(bf16[1,1024,384]{2,1,0:T(8,128)(2,1)} %param.11) | copy-start | bytes 2359300
  7.5 1.1 %copy-start.5 = (bf16[1,1024,384]{2,1,0:T(8,128)(2,1)S(1)}, bf16[1,1024,384]{2,1,0:T(8,128)(2,1)}, u32[]{:S(2)}) copy-start(bf16[1,1024,384]{2,1,0:T(8,128)(2,1)} %param.12) | copy-start | bytes 2359300
  8.6 1.1 %copy-start.6 = (bf16[1,384,1024]{2,1,0:T(8,128)(2,1)S(1)}, bf16[1,384,1024]{2,1,0:T(8,128)(2,1)}, u32[]{:S(2)}) copy-start(bf16[1,384,1024]{2,1,0:T(8,128)(2,1)} %param.13) | copy-start | bytes 2359300
  11.1 11.5 %copy-start = (bf16[2,15360,128]{2,1,0:T(8,128)(2,1)}, bf16[2,15360,128]{2,1,0:T(8,128)(2,1)S(1)}, u32[]{:S(2)}) copy-start(bf16[2,15360,128]{2,1,0:T(8,128)(2,1)S(1)} %weights.1.refs_3_.refs_4_) | copy-start | bytes 23592964
  15.5 12.0 %copy-start.7 = (bf16[2,33,16,128]{3,2,1,0:T(8,128)(2,1)}, bf16[2,33,16,128]{3,2,1,0:T(8,128)(2,1)S(1)}, u32[]{:S(2)}) copy-start(bf16[2,33,16,128]{3,2,1,0:T(8,128)(2,1)S(1)} %get-tuple-element.56.refs_0_) | copy-start | bytes 811012
  20.6 13.3 %collective-permute-start.5 = (bf16[2,65,16,128]{3,2,1,0:T(8,128)(2,1)S(1)}, bf16[2,65,16,128]{3,2,1,0:T(8,128)(2,1)S(1)}, u32[]{:S(2)}, u32[]{:S(2)}) collective-permute-start(bf16[2,65,16,128]{3,2,1,0:T(8,128)(2,1)S(1)} %collective-permute-done.3.refs_2_), channel_id=1, source_target_pairs={{0,4},{1,5},{4,8},{5,9},{8,12},{9,13},{12,14},{13,15},{14,10},{15,... | collective-permute-start | bytes 1597448 | tf_op jit(solution)/shard_map/ppermute | solution.py:288
  22.2 13.1 %collective-permute-start.6 = (bf16[2,65,16,128]{3,2,1,0:T(8,128)(2,1)S(1)}, bf16[2,65,16,128]{3,2,1,0:T(8,128)(2,1)S(1)}, u32[]{:S(2)}, u32[]{:S(2)}) collective-permute-start(bf16[2,65,16,128]{3,2,1,0:T(8,128)(2,1)S(1)} %collective-permute-done.4.refs_3_), channel_id=1, source_target_pairs={{0,2},{1,3},{4,0},{5,1},{8,4},{9,5},{12,8},{13,9},{14,12},{15,13},... | collective-permute-start | bytes 1597448 | tf_op jit(solution)/shard_map/ppermute | solution.py:289
  27.5 3.6 %copy-start.2 = (f32[2,9216,128]{2,1,0:T(8,128)}, f32[2,9216,128]{2,1,0:T(8,128)S(1)}, u32[]{:S(2)}) copy-start(f32[2,9216,128]{2,1,0:T(8,128)S(1)} %get-tuple-element.66.refs_5_) | copy-start | bytes 28311556
  31.1 0.7 copy-start.9
  31.9 0.7 copy-start.11
  35.2 13.6 %collective-permute-start.7 = (bf16[2,65,16,128]{3,2,1,0:T(8,128)(2,1)S(1)}, bf16[2,65,16,128]{3,2,1,0:T(8,128)(2,1)S(1)}, u32[]{:S(2)}, u32[]{:S(2)}) collective-permute-start(bf16[2,65,16,128]{3,2,1,0:T(8,128)(2,1)S(1)} %collective-permute-done.5.refs_2_), channel_id=1, source_target_pairs={{0,4},{1,5},{4,8},{5,9},{8,12},{9,13},{12,14},{13,15},{14,10},{15,... | collective-permute-start | bytes 1597448 | tf_op jit(solution)/shard_map/ppermute | solution.py:288
  36.8 12.1 %collective-permute-start.8 = (bf16[2,65,16,128]{3,2,1,0:T(8,128)(2,1)S(1)}, bf16[2,65,16,128]{3,2,1,0:T(8,128)(2,1)S(1)}, u32[]{:S(2)}, u32[]{:S(2)}) collective-permute-start(bf16[2,65,16,128]{3,2,1,0:T(8,128)(2,1)S(1)} %collective-permute-done.6.refs_3_), channel_id=1, source_target_pairs={{0,2},{1,3},{4,0},{5,1},{8,4},{9,5},{12,8},{13,9},{14,12},{15,13},... | collective-permute-start | bytes 1597448 | tf_op jit(solution)/shard_map/ppermute | solution.py:289
  37.3 3.2 %copy-start.1 = (bf16[2,15360,128]{2,1,0:T(8,128)(2,1)S(1)}, bf16[2,15360,128]{2,1,0:T(8,128)(2,1)}, u32[]{:S(2)}) copy-start(bf16[2,15360,128]{2,1,0:T(8,128)(2,1)} %copy-done) | copy-start | bytes 23592964
  40.5 3.7 %copy-start.3 = (f32[2,9216,128]{2,1,0:T(8,128)S(1)}, f32[2,9216,128]{2,1,0:T(8,128)}, u32[]{:S(2)}) copy-start(f32[2,9216,128]{2,1,0:T(8,128)} %copy-done.2) | copy-start | bytes 28311556
  48.9 6.9 %collective-permute-start.9 = (bf16[1,65,16,128]{3,2,1,0:T(8,128)(2,1)S(1)}, bf16[1,65,16,128]{3,2,1,0:T(8,128)(2,1)S(1)}, u32[]{:S(2)}, u32[]{:S(2)}) collective-permute-start(bf16[1,65,16,128]{3,2,1,0:T(8,128)(2,1)S(1)} %slice.6), channel_id=1, source_target_pairs={{0,4},{1,5},{4,8},{5,9},{8,12},{9,13},{12,14},{13,15},{14,10},{15,... | collective-permute-start | bytes 798728 | tf_op jit(solution)/shard_map/ppermute | solution.py:288
  50.6 6.5 %collective-permute-start.10 = (bf16[1,65,16,128]{3,2,1,0:T(8,128)(2,1)S(1)}, bf16[1,65,16,128]{3,2,1,0:T(8,128)(2,1)S(1)}, u32[]{:S(2)}, u32[]{:S(2)}) collective-permute-start(bf16[1,65,16,128]{3,2,1,0:T(8,128)(2,1)S(1)} %slice.7), channel_id=1, source_target_pairs={{0,2},{1,3},{4,0},{5,1},{8,4},{9,5},{12,8},{13,9},{14,12},{15,13},... | collective-permute-start | bytes 798728 | tf_op jit(solution)/shard_map/ppermute | solution.py:289
  60.0 14.8 %collective-permute-start.20 = (bf16[288,16,128]{2,1,0:T(8,128)(2,1)S(1)}, bf16[288,16,128]{2,1,0:T(8,128)(2,1)S(1)}, u32[]{:S(2)}, u32[]{:S(2)}) collective-permute-start(bf16[288,16,128]{2,1,0:T(8,128)(2,1)S(1)} %get-tuple-element.99), channel_id=1, source_target_pairs={{0,1},{1,0},{2,3},{3,2},{4,5},{5,4},{6,7},{7,6},{8,9},{9,8},{10,11... | collective-permute-start | bytes 3538952 | tf_op jit(solution)/shard_map/ppermute | solution.py:290
  60.1 6.0 %collective-permute-start.11 = (bf16[1,33,16,128]{3,2,1,0:T(8,128)(2,1)S(1)}, bf16[1,33,16,128]{3,2,1,0:T(8,128)(2,1)S(1)}, u32[]{:S(2)}, u32[]{:S(2)}) collective-permute-start(bf16[1,33,16,128]{3,2,1,0:T(8,128)(2,1)S(1)} %get-tuple-element.76), channel_id=1, source_target_pairs={{0,2},{1,3},{4,0},{5,1},{8,4},{9,5},{12,8},{13,9},{14,12},{15,13},... | collective-permute-start | bytes 405512 | tf_op jit(solution)/shard_map/ppermute | solution.py:289
  60.6 7.4 %collective-permute-start.15 = (bf16[1,33,16,128]{3,2,1,0:T(8,128)(2,1)S(1)}, bf16[1,33,16,128]{3,2,1,0:T(8,128)(2,1)S(1)}, u32[]{:S(2)}, u32[]{:S(2)}) collective-permute-start(bf16[1,33,16,128]{3,2,1,0:T(8,128)(2,1)S(1)} %get-tuple-element.80), channel_id=1, source_target_pairs={{0,4},{1,5},{4,8},{5,9},{8,12},{9,13},{12,14},{13,15},{14,10},{15,... | collective-permute-start | bytes 405512 | tf_op jit(solution)/shard_map/ppermute | solution.py:288
  66.1 8.1 %collective-permute-start.12 = (bf16[2,33,16,128]{3,2,1,0:T(8,128)(2,1)S(1)}, bf16[2,33,16,128]{3,2,1,0:T(8,128)(2,1)S(1)}, u32[]{:S(2)}, u32[]{:S(2)}) collective-permute-start(bf16[2,33,16,128]{3,2,1,0:T(8,128)(2,1)S(1)} %add_convert_fusion.6), channel_id=1, source_target_pairs={{0,2},{1,3},{4,0},{5,1},{8,4},{9,5},{12,8},{13,9},{14,12},{15,13},... | collective-permute-start | bytes 811016 | tf_op jit(solution)/shard_map/ppermute | solution.py:289
  68.0 26.0 %collective-permute-start.19 = (bf16[288,16,128]{2,1,0:T(8,128)(2,1)S(1)}, bf16[288,16,128]{2,1,0:T(8,128)(2,1)S(1)}, u32[]{:S(2)}, u32[]{:S(2)}) collective-permute-start(bf16[288,16,128]{2,1,0:T(8,128)(2,1)S(1)} %get-tuple-element.97), channel_id=1, source_target_pairs={{0,1},{1,0},{2,3},{3,2},{4,5},{5,4},{6,7},{7,6},{8,9},{9,8},{10,11... | collective-permute-start | bytes 3538952 | tf_op jit(solution)/shard_map/ppermute | solution.py:290
  68.0 8.9 %collective-permute-start.16 = (bf16[2,33,16,128]{3,2,1,0:T(8,128)(2,1)S(1)}, bf16[2,33,16,128]{3,2,1,0:T(8,128)(2,1)S(1)}, u32[]{:S(2)}, u32[]{:S(2)}) collective-permute-start(bf16[2,33,16,128]{3,2,1,0:T(8,128)(2,1)S(1)} %add_convert_fusion.3), channel_id=1, source_target_pairs={{0,4},{1,5},{4,8},{5,9},{8,12},{9,13},{12,14},{13,15},{14,10},{15,... | collective-permute-start | bytes 811016 | tf_op jit(solution)/shard_map/ppermute | solution.py:288
  74.3 7.2 %collective-permute-start.13 = (bf16[2,33,16,128]{3,2,1,0:T(8,128)(2,1)S(1)}, bf16[2,33,16,128]{3,2,1,0:T(8,128)(2,1)S(1)}, u32[]{:S(2)}, u32[]{:S(2)}) collective-permute-start(bf16[2,33,16,128]{3,2,1,0:T(8,128)(2,1)S(1)} %add_convert_fusion.5), channel_id=1, source_target_pairs={{0,2},{1,3},{4,0},{5,1},{8,4},{9,5},{12,8},{13,9},{14,12},{15,13},... | collective-permute-start | bytes 811016 | tf_op jit(solution)/shard_map/ppermute | solution.py:289
  74.8 6.7 %copy-start.12 = (bf16[2,33,16,128]{3,2,1,0:T(8,128)(2,1)S(1)}, bf16[2,33,16,128]{3,2,1,0:T(8,128)(2,1)}, u32[]{:S(2)}) copy-start(bf16[2,33,16,128]{3,2,1,0:T(8,128)(2,1)} %copy-done.11) | copy-start | bytes 811012
  75.1 10.1 %copy-start.10 = (bf16[2,33,16,128]{3,2,1,0:T(8,128)(2,1)S(1)}, bf16[2,33,16,128]{3,2,1,0:T(8,128)(2,1)}, u32[]{:S(2)}) copy-start(bf16[2,33,16,128]{3,2,1,0:T(8,128)(2,1)} %copy-done.9) | copy-start | bytes 811012
  75.1 26.4 %collective-permute-start.21 = (bf16[288,16,128]{2,1,0:T(8,128)(2,1)S(1)}, bf16[288,16,128]{2,1,0:T(8,128)(2,1)S(1)}, u32[]{:S(2)}, u32[]{:S(2)}) collective-permute-start(bf16[288,16,128]{2,1,0:T(8,128)(2,1)S(1)} %add_convert_fusion), channel_id=1, source_target_pairs={{0,16},{16,0},{1,17},{17,1},{2,18},{18,2},{3,19},{19,3},{4,20},{20... | collective-permute-start | bytes 3538952 | tf_op jit(solution)/shard_map/ppermute | solution.py:381
  77.0 15.6 %copy-start.8 = (bf16[2,33,16,128]{3,2,1,0:T(8,128)(2,1)S(1)}, bf16[2,33,16,128]{3,2,1,0:T(8,128)(2,1)}, u32[]{:S(2)}) copy-start(bf16[2,33,16,128]{3,2,1,0:T(8,128)(2,1)} %copy-done.7) | copy-start | bytes 811012
  77.0 15.6 %copy-start.13 = (s32[128,8]{0,1:T(8,128)S(1)}, s32[128,8]{0,1:T(8,128)}, u32[]{:S(2)}) copy-start(s32[128,8]{0,1:T(8,128)} %param.9) | copy-start | bytes 12292
  77.0 8.2 %collective-permute-start.17 = (bf16[2,33,16,128]{3,2,1,0:T(8,128)(2,1)S(1)}, bf16[2,33,16,128]{3,2,1,0:T(8,128)(2,1)S(1)}, u32[]{:S(2)}, u32[]{:S(2)}) collective-permute-start(bf16[2,33,16,128]{3,2,1,0:T(8,128)(2,1)S(1)} %add_convert_fusion.2), channel_id=1, source_target_pairs={{0,4},{1,5},{4,8},{5,9},{8,12},{9,13},{12,14},{13,15},{14,10},{15,... | collective-permute-start | bytes 811016 | tf_op jit(solution)/shard_map/ppermute | solution.py:288
  81.6 6.5 %collective-permute-start.14 = (bf16[2,33,16,128]{3,2,1,0:T(8,128)(2,1)S(1)}, bf16[2,33,16,128]{3,2,1,0:T(8,128)(2,1)S(1)}, u32[]{:S(2)}, u32[]{:S(2)}) collective-permute-start(bf16[2,33,16,128]{3,2,1,0:T(8,128)(2,1)S(1)} %add_convert_fusion.4), channel_id=1, source_target_pairs={{0,2},{1,3},{4,0},{5,1},{8,4},{9,5},{12,8},{13,9},{14,12},{15,13},... | collective-permute-start | bytes 811016 | tf_op jit(solution)/shard_map/ppermute | solution.py:289
  85.3 7.3 %collective-permute-start.18 = (bf16[2,33,16,128]{3,2,1,0:T(8,128)(2,1)S(1)}, bf16[2,33,16,128]{3,2,1,0:T(8,128)(2,1)S(1)}, u32[]{:S(2)}, u32[]{:S(2)}) collective-permute-start(bf16[2,33,16,128]{3,2,1,0:T(8,128)(2,1)S(1)} %add_convert_fusion.1), channel_id=1, source_target_pairs={{0,4},{1,5},{4,8},{5,9},{8,12},{9,13},{12,14},{13,15},{14,10},{15,... | collective-permute-start | bytes 811016 | tf_op jit(solution)/shard_map/ppermute | solution.py:288

commit v4 on v3

--- a/solution.py
+++ b/solution.py
@@ -11,7 +11,6 @@
 ROWS, LANES = 16, 128
 VMEM = pl.BlockSpec(memory_space=pltpu.VMEM)
 ANY = pl.BlockSpec(memory_space=pl.ANY)
-SMEM = pl.BlockSpec(memory_space=pltpu.SMEM)
 STEPS = 4
 EXPERT_VMEM = 16 * 1024 * 1024
 TOKEN = jax.ShapeDtypeStruct((8, LANES), F32)
@@ -87,7 +86,8 @@
 
 def expert_kernel(halves, half, width, ff, start, last, *refs):
     count = len(halves)
-    me_ref, refs = refs[0], refs[2:]
+    me = lax.axis_index("expert")
+    refs = refs[1:]
     packets, refs = refs[:count], refs[count:]
     weights, refs = refs[0], refs[1:]
     if start:
@@ -115,8 +115,7 @@
         w_gu = take_strips(weights, e, 0, width, 2 * ff)
         w_d_t = take_strips(weights, e, 2 * ff // LANES * width, width, ff)
         w_gu_t = take_strips(weights, e, 3 * ff // LANES * width, 2 * ff, width)
-        me = me_ref[e]
-        mine = [iota((ROWS, LANES), 0) + i * ROWS == me for i in range(extra)]
+        mine = [iota((ROWS, LANES), 0) + i * ROWS == me ^ e for i in range(extra)]
         probs = []
         for ref, _, which in pieces:
             row = sum(
@@ -174,9 +173,10 @@
                 at += rows * b.shape[1] // LANES
 
 
-def weight_kernel(steps, part_ref, turn_ref, *refs):
+def weight_kernel(steps, away, turn_ref, *refs):
     totals, xt, refs = refs[0], refs[1], refs[2:]
     groups, outs, token = (refs[:3], refs[3:6]), refs[6:8], refs[8]
+    part = 0 if away is None else lax.axis_index("dp") ^ away
     token[...] = jnp.zeros_like(token)
     for e, (dgu, ht, sc) in enumerate(groups):
         to = 0
@@ -185,7 +185,7 @@
             for a, b in ((xt, dgu), (ht, sc)):
                 rows, across = a.shape[0], b.shape[1] // LANES
                 tile = rows // STEPS
-                first = pl.multiple_of((part_ref[0] * steps + step) * tile, tile)
+                first = pl.multiple_of((part * steps + step) * tile, tile)
                 new = jnp.dot(a[pl.ds(first, tile)], b[...], preferred_element_type=F32)
                 for j in range(across):
                     strip = new[:, j * LANES : (j + 1) * LANES]
@@ -198,12 +198,13 @@
                 to += tile // ROWS * across
 
 
-def weight_sums(turn, totals, group, part, parts):
+def weight_sums(turn, totals, group, away=None):
+    parts = 1 if away is None else 2
     tiles = totals.size // (2 * parts * ROWS * LANES)
     return pl.pallas_call(
-        functools.partial(weight_kernel, STEPS // parts),
+        functools.partial(weight_kernel, STEPS // parts, away),
         out_shape=(kept(tiles, ROWS, LANES),) * 2 + (TOKEN,),
-        in_specs=[SMEM, ANY] + [VMEM] * (1 + len(group)),
+        in_specs=[ANY] + [VMEM] * (1 + len(group)),
         out_specs=(VMEM,) * 3,
         compiler_params=PARAMS,
         cost_estimate=pl.CostEstimate(
@@ -212,11 +213,12 @@
             transcendentals=0,
         ),
         name="weight_sums",
-    )(part.astype(jnp.int32)[None], turn, totals, *group)
+    )(turn, totals, *group)
 
 
 def finish_kernel(count, *refs):
-    outs = refs[count:]
+    outs, token = refs[count:-1], refs[-1]
+    token[...] = jnp.zeros_like(token)
     width, ff = outs[2].shape[1], outs[0].shape[1]
     tile_w, tile_d = width // STEPS, ff // STEPS
     across_w, across_d = 2 * ff // LANES, width // LANES
@@ -238,7 +240,7 @@
             n += across_d
 
 
-def home_kernel(count, ids_ref, *refs):
+def home_kernel(count, turn_ref, ids_ref, *refs):
     out_ref, prob_ref = refs[count:]
     tok_dev, width = out_ref.shape
     half = tok_dev // 2
@@ -290,8 +292,6 @@
     swap = lambda v: lax.ppermute(v, "expert", [(i, i ^ 1) for i in range(devices)])
     full, odd = (chips - 1) // 2, chips % 2 == 0
 
-    me = lax.axis_index("expert").astype(jnp.int32)
-    pair = jnp.stack([me, me ^ 1])
     ids_t, probs_t = expert_ids.T, gate_probs.T
     own = (w_gate[0], w_up[0], w_down[0])
 
@@ -332,11 +332,11 @@
             out_shape += tuple(kept(*s) for s in groups)
         else:
             scratch = groups + scratch
-        inputs = (pair, turn, *packets, weights) + ((totals,) if start else ())
+        inputs = (turn, *packets, weights) + ((totals,) if start else ())
         outs = pl.pallas_call(
             functools.partial(expert_kernel, halves, half, width, ff, start, last),
             out_shape=out_shape,
-            in_specs=[SMEM, ANY] + [VMEM] * (len(inputs) - 2),
+            in_specs=[ANY] + [VMEM] * (len(inputs) - 1),
             out_specs=(VMEM,) * len(out_shape),
             scratch_shapes=[pltpu.VMEM(s, BF16) for s in scratch],
 
@@ -360,7 +360,8 @@
     local = {}
     for s in range(1, full + 1):
         came = r, l
-        r, l, turn = lax.optimization_barrier((r, l, turn))
+        r, turn = lax.optimization_barrier((r, turn))
+        l, turn = lax.optimization_barrier((l, turn))
         if s < full:
             r, l = right(r), left(l)
         elif odd:
@@ -373,35 +374,33 @@
     def add(*terms):
         return sum(t.astype(F32) for t in terms).astype(BF16)
 
-    if groups == 2:
-        here = lax.axis_index("dp")
-        mine, other, turn = weight_sums(turn, totals, group, 1 - here, 2)
-        send = add(mine, swap(other))
-        mine, other, turn = weight_sums(turn, totals, group, here, 2)
-        got = lax.ppermute(send, "dp", [(0, 1), (1, 0)])
-        terms = (mine, swap(other), got)
+    def finish(*terms, rows):
         shape = lambda *s: jax.ShapeDtypeStruct(s, BF16)
-        grads = pl.pallas_call(
+        return pl.pallas_call(
             functools.partial(finish_kernel, len(terms)),
-            out_shape=(shape(width // 2, ff), shape(width // 2, ff), shape(ff // 2, width)),
+            out_shape=(shape(width // rows, ff), shape(width // rows, ff))
+            + (shape(ff // rows, width), TOKEN),
             in_specs=[VMEM] * len(terms),
-            out_specs=(VMEM,) * 3,
+            out_specs=(VMEM,) * 4,
             compiler_params=PARAMS,
             name="finish",
         )(*terms)
+
+    if groups == 2:
+        mine, other, turn = weight_sums(turn, totals, group, 1)
+        send = add(mine, swap(other))
+        mine, other, turn = weight_sums(turn, totals, group, 0)
+        got = lax.ppermute(send, "dp", [(0, 1), (1, 0)])
+        terms = (mine, swap(other), got)
+        grads = finish(*terms, rows=2)
     else:
-        mine, other, turn = weight_sums(turn, totals, group, jnp.int32(0), 1)
-        terms = (add(mine, swap(other)),)
-        shape = lambda *s: jax.ShapeDtypeStruct(s, BF16)
-        grads = pl.pallas_call(
-            functools.partial(finish_kernel, len(terms)),
-            out_shape=(shape(width, ff), shape(width, ff), shape(ff, width)),
-            in_specs=[VMEM] * len(terms),
-            out_specs=(VMEM,) * 3,
-            compiler_params=PARAMS,
-            name="finish",
-        )(*terms)
-        grads = [lax.psum_scatter(v, "dp", scatter_dimension=0, tiled=True) for v in grads]
+        mine, other, turn = weight_sums(turn, totals, group)
+        grads = finish(add(mine, swap(other)), rows=1)
+        turn, grads = grads[-1], [
+            lax.psum_scatter(v, "dp", scatter_dimension=0, tiled=True) for v in grads[:-1]
+        ]
+        grads = (*grads, turn)
+    *grads, turn = grads
 
     def back(side, move):
         moving = None
@@ -426,11 +425,11 @@
             jax.ShapeDtypeStruct((tok_dev, width), BF16),
             jax.ShapeDtypeStruct(ids_t.shape, F32),
         ),
-        in_specs=[VMEM] * (1 + len(parts)),
+        in_specs=[ANY] + [VMEM] * (1 + len(parts)),
         out_specs=(VMEM, VMEM),
         compiler_params=PARAMS,
         name="home",
-    )(ids_t, *parts)
+    )(turn, ids_t, *parts)
     return (
         grad_tokens,
         grad_probs.T.astype(BF16),

time: 103 us -> 94.5 us (0.917)
  local copies, waits for them, and re-layouts: 15.4 us -> 3.44 us
  waiting for transfers between devices: 37 us -> 44.8 us
  Pallas kernels: 28.4 us -> 24.2 us
    ppermute x8, waiting for transfers between devices: 12.8 us -> 31.6 us  [on_device(): right = lambda v: lax.ppermute(v, 'expert', hop[1])]
    ppermute x8, waiting for transfers between devices: 16.6 us -> 1.22 us  [on_device(): left = lambda v: lax.ppermute(v, 'expert', hop[-1])]
    unnamed x28 -> x8, local copies, waits for them, and re-layouts: 15.4 us -> 3.4 us
    ppermute x1, waiting for transfers between devices: 7.6 us -> 11.9 us  [on_device(): got = lax.ppermute(send, 'dp', [(0, 1), (1, 0)])]
    pallas_call x5, Pallas kernels: 20.7 us -> 17.3 us  [expert(): pl.pallas_call(functools.partial(expert_kernel, halves, half, width, ff,...]
  transfers between devices with their start and end apart: 22 -> 22, of which waited for: 13 -> 10; matrix products, arithmetic and copies ran while one was open for 1% -> 1% of each run, Pallas kernels for 23% -> 22%
where the time goes in v4:
time: 94.5 us; the launch traced here: 94.2 us
  waiting for transfers between devices  44.8 us (47%)
  Pallas kernels  24.2 us (26%)
  starting transfers between devices  19.9 us (21%)
  local copies, waits for them, and re-layouts  3.44 us (4%)
  other arithmetic  1.27 us (1%)
    ppermute x8, waiting for transfers between devices, on_device(): right = lambda v: lax.ppermute(v, 'expert', hop[1])  31.6 us
    pallas_call x5, Pallas kernels, expert(): pl.pallas_call(functools.partial(expert_kernel, halves, half, width, ff,...  17.3 us
    ppermute x8, starting transfers between devices, on_device(): right = lambda v: lax.ppermute(v, 'expert', hop[1])  13.4 us
    ppermute x1, waiting for transfers between devices, on_device(): got = lax.ppermute(send, 'dp', [(0, 1), (1, 0)])  11.9 us
    ppermute x8, starting transfers between devices, on_device(): left = lambda v: lax.ppermute(v, 'expert', hop[-1])  3.95 us
    unnamed x8, local copies, waits for them, and re-layouts  3.4 us
    pallas_call x2, Pallas kernels, weight_sums(): pl.pallas_call(functools.partial(weight_kernel, STEPS // parts, away), ou...  2.17 us
  transfers between devices with their start and end apart: 22, of which 10 were waited for; matrix products, arithmetic and copies ran while one was open for 1% of the time, Pallas kernels for 22%

profile of v4, /device:TPU:0, one launch (start us, length us, event | category | flops | bytes accessed | tf_op | source)
XLA Modules:
  0.0 94.2 jit_solution(13139176131672010414)
XLA Ops:
  0.6 0.5 collective-permute-start.1
  1.1 0.1 collective-permute-start.2
  1.2 0.4 collective-permute-start.3
  1.7 1.1 %pack.1 = (bf16[2,65,16,128]{3,2,1,0:T(8,128)(2,1)S(1)}, f32[8,128]{1,0:T(8,128)S(1)}) custom-call(bf16[128,1024]{1,0:T(8,128)(2,1)} %tok_ref.1, bf16[128,1024]{1,0:T(8,128)(2,1)} %cot_ref.1, s32[8,128]{1,0:T(8,128)} %bitcast.16, bf16[8,128]{1,0:T(8,128)(2,1)} %bitcast.18), custom_call_target="tpu_custom_call" | custom-call | tf_op jit(solution)/shard_map/pack/pallas_call | solution.py:300
  2.8 2.7 %collective-permute-start = (bf16[2,65,16,128]{3,2,1,0:T(8,128)(2,1)S(1)}, bf16[2,65,16,128]{3,2,1,0:T(8,128)(2,1)S(1)}, u32[]{:S(2)}, u32[]{:S(2)}) collective-permute-start(bf16[2,65,16,128]{3,2,1,0:T(8,128)(2,1)S(1)} %get-tuple-element.58.refs_1_), channel_id=1, source_target_pairs={{0,4},{1,5},{4,8},{5,9},{8,12},{9,13},{12,14},{13,15},{14,10},{15,... | collective-permute-start | bytes 1597448 | tf_op jit(solution)/shard_map/ppermute | solution.py:290
  5.5 0.0 collective-permute-start.5
  5.5 0.0 collective-permute-done.1.refs_3_
  5.5 0.0 collective-permute-done.2.refs_4_
  5.5 0.0 collective-permute-done.3.refs_5_
  5.5 1.1 %copy-done = bf16[1,1024,384]{2,1,0:T(8,128)(2,1)S(1)} copy-done((bf16[1,1024,384]{2,1,0:T(8,128)(2,1)S(1)}, bf16[1,1024,384]{2,1,0:T(8,128)(2,1)}, u32[]{:S(2)}) %copy-start) | copy-done | bytes 786456
  6.7 1.1 %copy-done.1 = bf16[1,1024,384]{2,1,0:T(8,128)(2,1)S(1)} copy-done((bf16[1,1024,384]{2,1,0:T(8,128)(2,1)S(1)}, bf16[1,1024,384]{2,1,0:T(8,128)(2,1)}, u32[]{:S(2)}) %copy-start.1) | copy-done | bytes 786456
  7.8 1.1 %copy-done.2 = bf16[1,384,1024]{2,1,0:T(8,128)(2,1)S(1)} copy-done((bf16[1,384,1024]{2,1,0:T(8,128)(2,1)S(1)}, bf16[1,384,1024]{2,1,0:T(8,128)(2,1)}, u32[]{:S(2)}) %copy-start.2) | copy-done | bytes 786456
  8.9 1.4 %weights.1.refs_2_.refs_3_ = bf16[2,15360,128]{2,1,0:T(8,128)(2,1)S(1)} custom-call(bf16[1024,384]{1,0:T(8,128)(2,1)S(1)} %bitcast.11, bf16[1024,384]{1,0:T(8,128)(2,1)S(1)} %bitcast.13, bf16[384,1024]{1,0:T(8,128)(2,1)S(1)} %bitcast.15, bf16[1024,384]{1,0:T(8,128)(2,1)S(1)} %collective-permute-done.1.refs_3_, ...), custom_call_target="tpu_custom_call" | custom-call | bytes 9437184 | tf_op jit(solution)/shard_map/weights/pallas_call | solution.py:311
  10.3 2.9 %expert.5 = (bf16[2,33,16,128]{3,2,1,0:T(8,128)(2,1)S(1)}, f32[2,9216,128]{2,1,0:T(8,128)S(1)}, f32[8,128]{1,0:T(8,128)S(1)}) custom-call(f32[8,128]{1,0:T(8,128)S(1)} %get-tuple-element.59.refs_0_, bf16[2,65,16,128]{3,2,1,0:T(8,128)(2,1)S(1)} %get-tuple-element.58.refs_1_, bf16[2,15360,128]{2,1,0:T(8,128)(2,1)S(1)} %weights.1.refs_2_.refs_3_), custom_call_target="tpu_custom_call" | custom-call | flops 1610612736 | bytes 8388608 | tf_op jit(solution)/shard_map/expert/pallas_call | solution.py:336
  13.2 4.9 %collective-permute-done.refs_1_ = bf16[2,65,16,128]{3,2,1,0:T(8,128)(2,1)S(1)} collective-permute-done((bf16[2,65,16,128]{3,2,1,0:T(8,128)(2,1)S(1)}, bf16[2,65,16,128]{3,2,1,0:T(8,128)(2,1)S(1)}, u32[]{:S(2)}, u32[]{:S(2)}) %collective-permute-start) | collective-permute-done | bytes 532512 | tf_op jit(solution)/shard_map/ppermute | solution.py:290
  18.1 1.8 %collective-permute-start.4 = (bf16[2,65,16,128]{3,2,1,0:T(8,128)(2,1)S(1)}, bf16[2,65,16,128]{3,2,1,0:T(8,128)(2,1)S(1)}, u32[]{:S(2)}, u32[]{:S(2)}) collective-permute-start(bf16[2,65,16,128]{3,2,1,0:T(8,128)(2,1)S(1)} %collective-permute-done.refs_1_), channel_id=1, source_target_pairs={{0,4},{1,5},{4,8},{5,9},{8,12},{9,13},{12,14},{13,15},{14,10},{15,... | collective-permute-start | bytes 1597448 | tf_op jit(solution)/shard_map/ppermute | solution.py:290
  19.9 0.0 collective-permute-done.5.refs_2_
  19.9 0.2 collective-permute-start.7
  20.1 4.3 %expert.6 = (bf16[2,33,16,128]{3,2,1,0:T(8,128)(2,1)S(1)}, bf16[2,33,16,128]{3,2,1,0:T(8,128)(2,1)S(1)}, f32[2,9216,128]{2,1,0:T(8,128)S(1)}, f32[8,128]{1,0:T(8,128)S(1)}) custom-call(f32[8,128]{1,0:T(8,128)S(1)} %get-tuple-element.63.refs_0_, bf16[2,65,16,128]{3,2,1,0:T(8,128)(2,1)S(1)} %collective-permute-done.refs_1_, ...), custom_call_target="tpu_custom_call" | custom-call | flops 3221225472 | bytes 8388608 | tf_op jit(solution)/shard_map/expert/pallas_call | solution.py:336
  24.4 7.6 %collective-permute-done.4.refs_1_ = bf16[2,65,16,128]{3,2,1,0:T(8,128)(2,1)S(1)} collective-permute-done((bf16[2,65,16,128]{3,2,1,0:T(8,128)(2,1)S(1)}, bf16[2,65,16,128]{3,2,1,0:T(8,128)(2,1)S(1)}, u32[]{:S(2)}, u32[]{:S(2)}) %collective-permute-start.4) | collective-permute-done | bytes 532512 | tf_op jit(solution)/shard_map/ppermute | solution.py:290
  32.0 1.6 %collective-permute-start.6 = (bf16[2,65,16,128]{3,2,1,0:T(8,128)(2,1)S(1)}, bf16[2,65,16,128]{3,2,1,0:T(8,128)(2,1)S(1)}, u32[]{:S(2)}, u32[]{:S(2)}) collective-permute-start(bf16[2,65,16,128]{3,2,1,0:T(8,128)(2,1)S(1)} %collective-permute-done.4.refs_1_), channel_id=1, source_target_pairs={{0,4},{1,5},{4,8},{5,9},{8,12},{9,13},{12,14},{13,15},{14,10},{15,... | collective-permute-start | bytes 1597448 | tf_op jit(solution)/shard_map/ppermute | solution.py:290
  33.6 0.0 collective-permute-done.7.refs_2_
  33.6 0.4 collective-permute-start.9
  34.0 4.2 %expert.7 = (bf16[2,33,16,128]{3,2,1,0:T(8,128)(2,1)S(1)}, bf16[2,33,16,128]{3,2,1,0:T(8,128)(2,1)S(1)}, f32[2,9216,128]{2,1,0:T(8,128)S(1)}, f32[8,128]{1,0:T(8,128)S(1)}) custom-call(f32[8,128]{1,0:T(8,128)S(1)} %get-tuple-element.69.refs_0_, bf16[2,65,16,128]{3,2,1,0:T(8,128)(2,1)S(1)} %collective-permute-done.4.refs_1_, ...), custom_call_target="tpu_custom_call" | custom-call | flops 3221225472 | bytes 8388608 | tf_op jit(solution)/shard_map/expert/pallas_call | solution.py:336
  38.2 6.7 %collective-permute-done.6.refs_1_ = bf16[2,65,16,128]{3,2,1,0:T(8,128)(2,1)S(1)} collective-permute-done((bf16[2,65,16,128]{3,2,1,0:T(8,128)(2,1)S(1)}, bf16[2,65,16,128]{3,2,1,0:T(8,128)(2,1)S(1)}, u32[]{:S(2)}, u32[]{:S(2)}) %collective-permute-start.6) | collective-permute-done | bytes 532512 | tf_op jit(solution)/shard_map/ppermute | solution.py:290
  45.0 1.1 %collective-permute-done.9.refs_2_ = bf16[2,65,16,128]{3,2,1,0:T(8,128)(2,1)S(1)} collective-permute-done((bf16[2,65,16,128]{3,2,1,0:T(8,128)(2,1)S(1)}, bf16[2,65,16,128]{3,2,1,0:T(8,128)(2,1)S(1)}, u32[]{:S(2)}, u32[]{:S(2)}) %collective-permute-start.9) | collective-permute-done | bytes 532512 | tf_op jit(solution)/shard_map/ppermute | solution.py:291
  46.1 0.7 collective-permute-start.10
  46.8 1.5 %collective-permute-start.8 = (bf16[1,65,16,128]{3,2,1,0:T(8,128)(2,1)S(1)}, bf16[1,65,16,128]{3,2,1,0:T(8,128)(2,1)S(1)}, u32[]{:S(2)}, u32[]{:S(2)}) collective-permute-start(bf16[1,65,16,128]{3,2,1,0:T(8,128)(2,1)S(1)} %slice.6), channel_id=1, source_target_pairs={{0,4},{1,5},{4,8},{5,9},{8,12},{9,13},{12,14},{13,15},{14,10},{15,... | collective-permute-start | bytes 798728 | tf_op jit(solution)/shard_map/ppermute | solution.py:290
  48.3 4.2 %expert.8 = (bf16[2,33,16,128]{3,2,1,0:T(8,128)(2,1)S(1)}, bf16[2,33,16,128]{3,2,1,0:T(8,128)(2,1)S(1)}, f32[2,9216,128]{2,1,0:T(8,128)S(1)}, f32[8,128]{1,0:T(8,128)S(1)}) custom-call(f32[8,128]{1,0:T(8,128)S(1)} %get-tuple-element.76.refs_0_, bf16[2,65,16,128]{3,2,1,0:T(8,128)(2,1)S(1)} %collective-permute-done.6.refs_1_, ...), custom_call_target="tpu_custom_call" | custom-call | flops 3221225472 | bytes 8388608 | tf_op jit(solution)/shard_map/expert/pallas_call | solution.py:336
  52.5 0.1 collective-permute-done.10.refs_2_
  52.6 0.7 collective-permute-done.8.refs_1_
  53.3 1.7 %expert.9 = (bf16[1,33,16,128]{3,2,1,0:T(8,128)(2,1)S(1)}, bf16[1,33,16,128]{3,2,1,0:T(8,128)(2,1)S(1)}, f32[8,128]{1,0:T(8,128)S(1)}, bf16[1024,128]{1,0:T(8,12...) custom-call(f32[8,128]{1,0:T(8,128)S(1)} %get-tuple-element.79.refs_, ...), custom_call_target="tpu_custom_call" | custom-call | flops 1006632960 | bytes 8388608 | tf_op jit(solution)/shard_map/expert/pallas_call | solution.py:336
  54.9 0.8 weight_sums.2
  55.8 0.1 collective-permute-start.12
  55.9 1.5 %collective-permute-start.18 = (bf16[1,33,16,128]{3,2,1,0:T(8,128)(2,1)S(1)}, bf16[1,33,16,128]{3,2,1,0:T(8,128)(2,1)S(1)}, u32[]{:S(2)}, u32[]{:S(2)}) collective-permute-start(bf16[1,33,16,128]{3,2,1,0:T(8,128)(2,1)S(1)} %get-tuple-element.102), channel_id=1, source_target_pairs={{0,4},{1,5},{4,8},{5,9},{8,12},{9,13},{12,14},{13,15},{14,10},{15,... | collective-permute-start | bytes 405512 | tf_op jit(solution)/shard_map/ppermute | solution.py:290
  57.3 0.6 collective-permute-start.14
  57.9 1.3 %weight_sums.3 = (bf16[288,16,128]{2,1,0:T(8,128)(2,1)S(1)}, bf16[288,16,128]{2,1,0:T(8,128)(2,1)S(1)}, f32[8,128]{1,0:T(8,128)}) custom-call(f32[8,128]{1,0:T(8,128)S(1)} %get-tuple-element.91.turn_ref, f32[2,9216,128]{2,1,0:T(8,128)S(1)} %get-tuple-element.83.refs_0_, bf16[1024,128]{1,0:T(8,128)(2,1)S(1)} %get-tuple-element.84.refs_1_, ...), custom_call_target="tpu_custom_call" | custom-call | flops 301989888 | bytes 8388608 | tf_op jit(solution)/shard_map/weight_sums/pallas_call | solution.py:204
  59.3 0.0 collective-permute-start.11
  59.3 2.6 %collective-permute-done.18 = bf16[1,33,16,128]{3,2,1,0:T(8,128)(2,1)S(1)} collective-permute-done((bf16[1,33,16,128]{3,2,1,0:T(8,128)(2,1)S(1)}, bf16[1,33,16,128]{3,2,1,0:T(8,128)(2,1)S(1)}, u32[]{:S(2)}, u32[]{:S(2)}) %collective-permute-start.18) | collective-permute-done | bytes 135200 | tf_op jit(solution)/shard_map/ppermute | solution.py:290
  61.9 1.5 %collective-permute-start.19 = (bf16[2,33,16,128]{3,2,1,0:T(8,128)(2,1)S(1)}, bf16[2,33,16,128]{3,2,1,0:T(8,128)(2,1)S(1)}, u32[]{:S(2)}, u32[]{:S(2)}) collective-permute-start(bf16[2,33,16,128]{3,2,1,0:T(8,128)(2,1)S(1)} %add_convert_fusion.3), channel_id=1, source_target_pairs={{0,4},{1,5},{4,8},{5,9},{8,12},{9,13},{12,14},{13,15},{14,10},{15,... | collective-permute-start | bytes 811016 | tf_op jit(solution)/shard_map/ppermute | solution.py:290
  63.4 0.0 collective-permute-done.14
  63.4 0.7 collective-permute-start.15
  64.1 0.0 collective-permute-done.12
  64.1 0.3 add_convert_fusion
  64.4 1.4 %collective-permute-start.13 = (bf16[288,16,128]{2,1,0:T(8,128)(2,1)S(1)}, bf16[288,16,128]{2,1,0:T(8,128)(2,1)S(1)}, u32[]{:S(2)}, u32[]{:S(2)}) collective-permute-start(bf16[288,16,128]{2,1,0:T(8,128)(2,1)S(1)} %add_convert_fusion), channel_id=1, source_target_pairs={{0,16},{16,0},{1,17},{17,1},{2,18},{18,2},{3,19},{19,3},{4,20},{20... | collective-permute-start | bytes 3538952 | tf_op jit(solution)/shard_map/ppermute | solution.py:393
  65.8 4.2 %collective-permute-done.19 = bf16[2,33,16,128]{3,2,1,0:T(8,128)(2,1)S(1)} collective-permute-done((bf16[2,33,16,128]{3,2,1,0:T(8,128)(2,1)S(1)}, bf16[2,33,16,128]{3,2,1,0:T(8,128)(2,1)S(1)}, u32[]{:S(2)}, u32[]{:S(2)}) %collective-permute-start.19) | collective-permute-done | bytes 270368 | tf_op jit(solution)/shard_map/ppermute | solution.py:290
  70.0 0.1 add_convert_fusion.2
  70.1 1.5 %collective-permute-start.20 = (bf16[2,33,16,128]{3,2,1,0:T(8,128)(2,1)S(1)}, bf16[2,33,16,128]{3,2,1,0:T(8,128)(2,1)S(1)}, u32[]{:S(2)}, u32[]{:S(2)}) collective-permute-start(bf16[2,33,16,128]{3,2,1,0:T(8,128)(2,1)S(1)} %add_convert_fusion.2), channel_id=1, source_target_pairs={{0,4},{1,5},{4,8},{5,9},{8,12},{9,13},{12,14},{13,15},{14,10},{15,... | collective-permute-start | bytes 811016 | tf_op jit(solution)/shard_map/ppermute | solution.py:290
  71.5 0.0 collective-permute-done.15
  71.5 0.1 add_convert_fusion.5
  71.6 0.7 collective-permute-start.16
  72.3 5.0 %collective-permute-done.20 = bf16[2,33,16,128]{3,2,1,0:T(8,128)(2,1)S(1)} collective-permute-done((bf16[2,33,16,128]{3,2,1,0:T(8,128)(2,1)S(1)}, bf16[2,33,16,128]{3,2,1,0:T(8,128)(2,1)S(1)}, u32[]{:S(2)}, u32[]{:S(2)}) %collective-permute-start.20) | collective-permute-done | bytes 270368 | tf_op jit(solution)/shard_map/ppermute | solution.py:290
  77.3 0.1 add_convert_fusion.1
  77.4 1.5 %collective-permute-start.21 = (bf16[2,33,16,128]{3,2,1,0:T(8,128)(2,1)S(1)}, bf16[2,33,16,128]{3,2,1,0:T(8,128)(2,1)S(1)}, u32[]{:S(2)}, u32[]{:S(2)}) collective-permute-start(bf16[2,33,16,128]{3,2,1,0:T(8,128)(2,1)S(1)} %add_convert_fusion.1), channel_id=1, source_target_pairs={{0,4},{1,5},{4,8},{5,9},{8,12},{9,13},{12,14},{13,15},{14,10},{15,... | collective-permute-start | bytes 811016 | tf_op jit(solution)/shard_map/ppermute | solution.py:290
  78.8 0.0 collective-permute-done.16
  78.8 0.1 add_convert_fusion.4
  78.9 0.7 collective-permute-start.17
  79.6 0.0 collective-permute-done.11.refs_1_
  79.6 11.9 %collective-permute-done.13.refs_2_ = bf16[288,16,128]{2,1,0:T(8,128)(2,1)S(1)} collective-permute-done((bf16[288,16,128]{2,1,0:T(8,128)(2,1)S(1)}, bf16[288,16,128]{2,1,0:T(8,128)(2,1)S(1)}, u32[]{:S(2)}, u32[]{:S(2)}) %collective-permute-start.13) | collective-permute-done | bytes 1179680 | tf_op jit(solution)/shard_map/ppermute | solution.py:393
  91.4 1.4 %finish.1 = (bf16[512,384]{1,0:T(8,128)(2,1)}, bf16[512,384]{1,0:T(8,128)(2,1)}, bf16[192,1024]{1,0:T(8,128)(2,1)}, f32[8,128]{1,0:T(8,128)S(1)}) custom-call(bf16[288,16,128]{2,1,0:T(8,128)(2,1)S(1)} %get-tuple-element.92.refs_0_, bf16[288,16,128]{2,1,0:T(8,128)(2,1)S(1)} %collective-permute-done.11.refs_1_, ...), custom_call_target="tpu_custom_call" | custom-call | tf_op jit(solution)/shard_map/finish/pallas_call | solution.py:379
  92.8 0.0 collective-permute-done.21.refs_2_
  92.8 0.0 collective-permute-done.17.refs_1_
  92.8 0.8 home.1
  93.7 0.6 convert_bitcast_fusion
  (9 shorter events, 0.1 us)
Async XLA Ops:
  0.6 4.9 %collective-permute-start.1 = (bf16[1024,384]{1,0:T(8,128)(2,1)}, bf16[1024,384]{1,0:T(8,128)(2,1)S(1)}, u32[]{:S(2)}, u32[]{:S(2)}) collective-permute-start(bf16[1024,384]{1,0:T(8,128)(2,1)} %bitcast.10), channel_id=1, source_target_pairs={{0,1},{1,0},{2,3},{3,2},{4,5},{5,4},{6,7},{7,6},{8,9},{9,8},{10,11... | collective-permute-start | bytes 2359304 | tf_op jit(solution)/shard_map/ppermute | solution.py:292
  1.1 4.3 %collective-permute-start.2 = (bf16[1024,384]{1,0:T(8,128)(2,1)}, bf16[1024,384]{1,0:T(8,128)(2,1)S(1)}, u32[]{:S(2)}, u32[]{:S(2)}) collective-permute-start(bf16[1024,384]{1,0:T(8,128)(2,1)} %bitcast.12), channel_id=1, source_target_pairs={{0,1},{1,0},{2,3},{3,2},{4,5},{5,4},{6,7},{7,6},{8,9},{9,8},{10,11... | collective-permute-start | bytes 2359304 | tf_op jit(solution)/shard_map/ppermute | solution.py:292
  1.2 4.3 %collective-permute-start.3 = (bf16[384,1024]{1,0:T(8,128)(2,1)}, bf16[384,1024]{1,0:T(8,128)(2,1)S(1)}, u32[]{:S(2)}, u32[]{:S(2)}) collective-permute-start(bf16[384,1024]{1,0:T(8,128)(2,1)} %bitcast.14), channel_id=1, source_target_pairs={{0,1},{1,0},{2,3},{3,2},{4,5},{5,4},{6,7},{7,6},{8,9},{9,8},{10,11... | collective-permute-start | bytes 2359304 | tf_op jit(solution)/shard_map/ppermute | solution.py:292
  2.8 15.3 %collective-permute-start = (bf16[2,65,16,128]{3,2,1,0:T(8,128)(2,1)S(1)}, bf16[2,65,16,128]{3,2,1,0:T(8,128)(2,1)S(1)}, u32[]{:S(2)}, u32[]{:S(2)}) collective-permute-start(bf16[2,65,16,128]{3,2,1,0:T(8,128)(2,1)S(1)} %get-tuple-element.58.refs_1_), channel_id=1, source_target_pairs={{0,4},{1,5},{4,8},{5,9},{8,12},{9,13},{12,14},{13,15},{14,10},{15,... | collective-permute-start | bytes 1597448 | tf_op jit(solution)/shard_map/ppermute | solution.py:290
  5.5 14.5 %collective-permute-start.5 = (bf16[2,65,16,128]{3,2,1,0:T(8,128)(2,1)S(1)}, bf16[2,65,16,128]{3,2,1,0:T(8,128)(2,1)S(1)}, u32[]{:S(2)}, u32[]{:S(2)}) collective-permute-start(bf16[2,65,16,128]{3,2,1,0:T(8,128)(2,1)S(1)} %get-tuple-element.58.refs_1_), channel_id=1, source_target_pairs={{0,2},{1,3},{4,0},{5,1},{8,4},{9,5},{12,8},{13,9},{14,12},{15,13},... | collective-permute-start | bytes 1597448 | tf_op jit(solution)/shard_map/ppermute | solution.py:291
  5.5 1.1 %copy-start = (bf16[1,1024,384]{2,1,0:T(8,128)(2,1)S(1)}, bf16[1,1024,384]{2,1,0:T(8,128)(2,1)}, u32[]{:S(2)}) copy-start(bf16[1,1024,384]{2,1,0:T(8,128)(2,1)} %param.11) | copy-start | bytes 2359300
  6.7 1.1 %copy-start.1 = (bf16[1,1024,384]{2,1,0:T(8,128)(2,1)S(1)}, bf16[1,1024,384]{2,1,0:T(8,128)(2,1)}, u32[]{:S(2)}) copy-start(bf16[1,1024,384]{2,1,0:T(8,128)(2,1)} %param.12) | copy-start | bytes 2359300
  7.8 1.1 %copy-start.2 = (bf16[1,384,1024]{2,1,0:T(8,128)(2,1)S(1)}, bf16[1,384,1024]{2,1,0:T(8,128)(2,1)}, u32[]{:S(2)}) copy-start(bf16[1,384,1024]{2,1,0:T(8,128)(2,1)} %param.13) | copy-start | bytes 2359300
  18.1 13.9 %collective-permute-start.4 = (bf16[2,65,16,128]{3,2,1,0:T(8,128)(2,1)S(1)}, bf16[2,65,16,128]{3,2,1,0:T(8,128)(2,1)S(1)}, u32[]{:S(2)}, u32[]{:S(2)}) collective-permute-start(bf16[2,65,16,128]{3,2,1,0:T(8,128)(2,1)S(1)} %collective-permute-done.refs_1_), channel_id=1, source_target_pairs={{0,4},{1,5},{4,8},{5,9},{8,12},{9,13},{12,14},{13,15},{14,10},{15,... | collective-permute-start | bytes 1597448 | tf_op jit(solution)/shard_map/ppermute | solution.py:290
  19.9 13.7 %collective-permute-start.7 = (bf16[2,65,16,128]{3,2,1,0:T(8,128)(2,1)S(1)}, bf16[2,65,16,128]{3,2,1,0:T(8,128)(2,1)S(1)}, u32[]{:S(2)}, u32[]{:S(2)}) collective-permute-start(bf16[2,65,16,128]{3,2,1,0:T(8,128)(2,1)S(1)} %collective-permute-done.5.refs_2_), channel_id=1, source_target_pairs={{0,2},{1,3},{4,0},{5,1},{8,4},{9,5},{12,8},{13,9},{14,12},{15,13},... | collective-permute-start | bytes 1597448 | tf_op jit(solution)/shard_map/ppermute | solution.py:291
  32.0 13.0 %collective-permute-start.6 = (bf16[2,65,16,128]{3,2,1,0:T(8,128)(2,1)S(1)}, bf16[2,65,16,128]{3,2,1,0:T(8,128)(2,1)S(1)}, u32[]{:S(2)}, u32[]{:S(2)}) collective-permute-start(bf16[2,65,16,128]{3,2,1,0:T(8,128)(2,1)S(1)} %collective-permute-done.4.refs_1_), channel_id=1, source_target_pairs={{0,4},{1,5},{4,8},{5,9},{8,12},{9,13},{12,14},{13,15},{14,10},{15,... | collective-permute-start | bytes 1597448 | tf_op jit(solution)/shard_map/ppermute | solution.py:290
  33.6 12.5 %collective-permute-start.9 = (bf16[2,65,16,128]{3,2,1,0:T(8,128)(2,1)S(1)}, bf16[2,65,16,128]{3,2,1,0:T(8,128)(2,1)S(1)}, u32[]{:S(2)}, u32[]{:S(2)}) collective-permute-start(bf16[2,65,16,128]{3,2,1,0:T(8,128)(2,1)S(1)} %collective-permute-done.7.refs_2_), channel_id=1, source_target_pairs={{0,2},{1,3},{4,0},{5,1},{8,4},{9,5},{12,8},{13,9},{14,12},{15,13},... | collective-permute-start | bytes 1597448 | tf_op jit(solution)/shard_map/ppermute | solution.py:291
  46.1 6.5 %collective-permute-start.10 = (bf16[1,65,16,128]{3,2,1,0:T(8,128)(2,1)S(1)}, bf16[1,65,16,128]{3,2,1,0:T(8,128)(2,1)S(1)}, u32[]{:S(2)}, u32[]{:S(2)}) collective-permute-start(bf16[1,65,16,128]{3,2,1,0:T(8,128)(2,1)S(1)} %slice.7), channel_id=1, source_target_pairs={{0,2},{1,3},{4,0},{5,1},{8,4},{9,5},{12,8},{13,9},{14,12},{15,13},... | collective-permute-start | bytes 798728 | tf_op jit(solution)/shard_map/ppermute | solution.py:291
  46.8 6.5 %collective-permute-start.8 = (bf16[1,65,16,128]{3,2,1,0:T(8,128)(2,1)S(1)}, bf16[1,65,16,128]{3,2,1,0:T(8,128)(2,1)S(1)}, u32[]{:S(2)}, u32[]{:S(2)}) collective-permute-start(bf16[1,65,16,128]{3,2,1,0:T(8,128)(2,1)S(1)} %slice.6), channel_id=1, source_target_pairs={{0,4},{1,5},{4,8},{5,9},{8,12},{9,13},{12,14},{13,15},{14,10},{15,... | collective-permute-start | bytes 798728 | tf_op jit(solution)/shard_map/ppermute | solution.py:290
  55.8 8.3 %collective-permute-start.12 = (bf16[288,16,128]{2,1,0:T(8,128)(2,1)S(1)}, bf16[288,16,128]{2,1,0:T(8,128)(2,1)S(1)}, u32[]{:S(2)}, u32[]{:S(2)}) collective-permute-start(bf16[288,16,128]{2,1,0:T(8,128)(2,1)S(1)} %get-tuple-element.95), channel_id=1, source_target_pairs={{0,1},{1,0},{2,3},{3,2},{4,5},{5,4},{6,7},{7,6},{8,9},{9,8},{10,11... | collective-permute-start | bytes 3538952 | tf_op jit(solution)/shard_map/ppermute | solution.py:292
  55.9 6.0 %collective-permute-start.18 = (bf16[1,33,16,128]{3,2,1,0:T(8,128)(2,1)S(1)}, bf16[1,33,16,128]{3,2,1,0:T(8,128)(2,1)S(1)}, u32[]{:S(2)}, u32[]{:S(2)}) collective-permute-start(bf16[1,33,16,128]{3,2,1,0:T(8,128)(2,1)S(1)} %get-tuple-element.102), channel_id=1, source_target_pairs={{0,4},{1,5},{4,8},{5,9},{8,12},{9,13},{12,14},{13,15},{14,10},{15,... | collective-permute-start | bytes 405512 | tf_op jit(solution)/shard_map/ppermute | solution.py:290
  57.3 6.0 %collective-permute-start.14 = (bf16[1,33,16,128]{3,2,1,0:T(8,128)(2,1)S(1)}, bf16[1,33,16,128]{3,2,1,0:T(8,128)(2,1)S(1)}, u32[]{:S(2)}, u32[]{:S(2)}) collective-permute-start(bf16[1,33,16,128]{3,2,1,0:T(8,128)(2,1)S(1)} %get-tuple-element.98), channel_id=1, source_target_pairs={{0,2},{1,3},{4,0},{5,1},{8,4},{9,5},{12,8},{13,9},{14,12},{15,13},... | collective-permute-start | bytes 405512 | tf_op jit(solution)/shard_map/ppermute | solution.py:291
  59.3 20.3 %collective-permute-start.11 = (bf16[288,16,128]{2,1,0:T(8,128)(2,1)S(1)}, bf16[288,16,128]{2,1,0:T(8,128)(2,1)S(1)}, u32[]{:S(2)}, u32[]{:S(2)}) collective-permute-start(bf16[288,16,128]{2,1,0:T(8,128)(2,1)S(1)} %get-tuple-element.93), channel_id=1, source_target_pairs={{0,1},{1,0},{2,3},{3,2},{4,5},{5,4},{6,7},{7,6},{8,9},{9,8},{10,11... | collective-permute-start | bytes 3538952 | tf_op jit(solution)/shard_map/ppermute | solution.py:292
  61.9 8.1 %collective-permute-start.19 = (bf16[2,33,16,128]{3,2,1,0:T(8,128)(2,1)S(1)}, bf16[2,33,16,128]{3,2,1,0:T(8,128)(2,1)S(1)}, u32[]{:S(2)}, u32[]{:S(2)}) collective-permute-start(bf16[2,33,16,128]{3,2,1,0:T(8,128)(2,1)S(1)} %add_convert_fusion.3), channel_id=1, source_target_pairs={{0,4},{1,5},{4,8},{5,9},{8,12},{9,13},{12,14},{13,15},{14,10},{15,... | collective-permute-start | bytes 811016 | tf_op jit(solution)/shard_map/ppermute | solution.py:290
  63.4 8.1 %collective-permute-start.15 = (bf16[2,33,16,128]{3,2,1,0:T(8,128)(2,1)S(1)}, bf16[2,33,16,128]{3,2,1,0:T(8,128)(2,1)S(1)}, u32[]{:S(2)}, u32[]{:S(2)}) collective-permute-start(bf16[2,33,16,128]{3,2,1,0:T(8,128)(2,1)S(1)} %add_convert_fusion.6), channel_id=1, source_target_pairs={{0,2},{1,3},{4,0},{5,1},{8,4},{9,5},{12,8},{13,9},{14,12},{15,13},... | collective-permute-start | bytes 811016 | tf_op jit(solution)/shard_map/ppermute | solution.py:291
  64.4 27.0 %collective-permute-start.13 = (bf16[288,16,128]{2,1,0:T(8,128)(2,1)S(1)}, bf16[288,16,128]{2,1,0:T(8,128)(2,1)S(1)}, u32[]{:S(2)}, u32[]{:S(2)}) collective-permute-start(bf16[288,16,128]{2,1,0:T(8,128)(2,1)S(1)} %add_convert_fusion), channel_id=1, source_target_pairs={{0,16},{16,0},{1,17},{17,1},{2,18},{18,2},{3,19},{19,3},{4,20},{20... | collective-permute-start | bytes 3538952 | tf_op jit(solution)/shard_map/ppermute | solution.py:393
  70.1 7.2 %collective-permute-start.20 = (bf16[2,33,16,128]{3,2,1,0:T(8,128)(2,1)S(1)}, bf16[2,33,16,128]{3,2,1,0:T(8,128)(2,1)S(1)}, u32[]{:S(2)}, u32[]{:S(2)}) collective-permute-start(bf16[2,33,16,128]{3,2,1,0:T(8,128)(2,1)S(1)} %add_convert_fusion.2), channel_id=1, source_target_pairs={{0,4},{1,5},{4,8},{5,9},{8,12},{9,13},{12,14},{13,15},{14,10},{15,... | collective-permute-start | bytes 811016 | tf_op jit(solution)/shard_map/ppermute | solution.py:290
  71.6 7.2 %collective-permute-start.16 = (bf16[2,33,16,128]{3,2,1,0:T(8,128)(2,1)S(1)}, bf16[2,33,16,128]{3,2,1,0:T(8,128)(2,1)S(1)}, u32[]{:S(2)}, u32[]{:S(2)}) collective-permute-start(bf16[2,33,16,128]{3,2,1,0:T(8,128)(2,1)S(1)} %add_convert_fusion.5), channel_id=1, source_target_pairs={{0,2},{1,3},{4,0},{5,1},{8,4},{9,5},{12,8},{13,9},{14,12},{15,13},... | collective-permute-start | bytes 811016 | tf_op jit(solution)/shard_map/ppermute | solution.py:291
  77.4 15.5 %collective-permute-start.21 = (bf16[2,33,16,128]{3,2,1,0:T(8,128)(2,1)S(1)}, bf16[2,33,16,128]{3,2,1,0:T(8,128)(2,1)S(1)}, u32[]{:S(2)}, u32[]{:S(2)}) collective-permute-start(bf16[2,33,16,128]{3,2,1,0:T(8,128)(2,1)S(1)} %add_convert_fusion.1), channel_id=1, source_target_pairs={{0,4},{1,5},{4,8},{5,9},{8,12},{9,13},{12,14},{13,15},{14,10},{15,... | collective-permute-start | bytes 811016 | tf_op jit(solution)/shard_map/ppermute | solution.py:290
  78.9 13.9 %collective-permute-start.17 = (bf16[2,33,16,128]{3,2,1,0:T(8,128)(2,1)S(1)}, bf16[2,33,16,128]{3,2,1,0:T(8,128)(2,1)S(1)}, u32[]{:S(2)}, u32[]{:S(2)}) collective-permute-start(bf16[2,33,16,128]{3,2,1,0:T(8,128)(2,1)S(1)} %add_convert_fusion.4), channel_id=1, source_target_pairs={{0,2},{1,3},{4,0},{5,1},{8,4},{9,5},{12,8},{13,9},{14,12},{15,13},... | collective-permute-start | bytes 811016 | tf_op jit(solution)/shard_map/ppermute | solution.py:291
  91.4 1.4 %copy-start.3 = (s32[128,8]{0,1:T(8,128)S(1)}, s32[128,8]{0,1:T(8,128)}, u32[]{:S(2)}) copy-start(s32[128,8]{0,1:T(8,128)} %param.9) | copy-start | bytes 12292

commit v5 on v4

--- a/solution.py
+++ b/solution.py
@@ -11,6 +11,7 @@
 ROWS, LANES = 16, 128
 VMEM = pl.BlockSpec(memory_space=pltpu.VMEM)
 ANY = pl.BlockSpec(memory_space=pl.ANY)
+PIECES = 3
 STEPS = 4
 EXPERT_VMEM = 16 * 1024 * 1024
 TOKEN = jax.ShapeDtypeStruct((8, LANES), F32)
@@ -216,7 +217,7 @@
     )(turn, totals, *group)
 
 
-def finish_kernel(count, *refs):
+def finish_kernel(count, whole, *refs):
     outs, token = refs[count:-1], refs[-1]
     token[...] = jnp.zeros_like(token)
     width, ff = outs[2].shape[1], outs[0].shape[1]
@@ -224,19 +225,25 @@
     across_w, across_d = 2 * ff // LANES, width // LANES
     each = ff // LANES
     n = 0
+
+    def total(n):
+        size = refs[count - 1].shape[0]
+        terms = [ref[n] for ref in refs[:whole]]
+        if whole < count:
+            terms.append(refs[whole + n // size][n % size])
+        return sum(t.astype(F32) for t in terms).astype(BF16)
+
     for step in range(outs[0].shape[0] // tile_w):
         for i in range(tile_w // ROWS):
             rows = slice(step * tile_w + i * ROWS, step * tile_w + (i + 1) * ROWS)
             for j in range(across_w):
-                total = sum(ref[n + j].astype(F32) for ref in refs[:count]).astype(BF16)
                 at = slice(j % each * LANES, (j % each + 1) * LANES)
-                outs[j // each][rows, at] = total
+                outs[j // each][rows, at] = total(n + j)
             n += across_w
         for i in range(tile_d // ROWS):
             rows = slice(step * tile_d + i * ROWS, step * tile_d + (i + 1) * ROWS)
             for j in range(across_d):
-                total = sum(ref[n + j].astype(F32) for ref in refs[:count]).astype(BF16)
-                outs[2][rows, j * LANES : (j + 1) * LANES] = total
+                outs[2][rows, j * LANES : (j + 1) * LANES] = total(n + j)
             n += across_d
 
 
@@ -256,7 +263,7 @@
                 ] = total[i * across + j].astype(BF16)
         sums.append(total[block:])
     by_expert = sums[0] + sums[1]
-    ids = ids_ref[...]
+    ids, rows = ids_ref[...], []
     for k in range(ids.shape[0]):
         row = jnp.zeros((1, tok_dev), F32)
         for i in range(by_expert.shape[0]):
@@ -264,7 +271,8 @@
             row += jnp.sum(
                 jnp.where(ids[k : k + 1] == expert, by_expert[i], 0.0), axis=0, keepdims=True
             )
-        prob_ref[k : k + 1] = row
+        rows.append(row)
+    prob_ref[...] = jnp.concatenate(rows, axis=0).astype(BF16)
 
 
 def on_device(tokens, cotangent, expert_ids, gate_probs, w_gate, w_up, w_down):
@@ -374,10 +382,10 @@
     def add(*terms):
         return sum(t.astype(F32) for t in terms).astype(BF16)
 
-    def finish(*terms, rows):
+    def finish(*terms, rows, whole):
         shape = lambda *s: jax.ShapeDtypeStruct(s, BF16)
         return pl.pallas_call(
-            functools.partial(finish_kernel, len(terms)),
+            functools.partial(finish_kernel, len(terms), whole),
             out_shape=(shape(width // rows, ff), shape(width // rows, ff))
             + (shape(ff // rows, width), TOKEN),
             in_specs=[VMEM] * len(terms),
@@ -388,14 +396,19 @@
 
     if groups == 2:
         mine, other, turn = weight_sums(turn, totals, group, 1)
-        send = add(mine, swap(other))
+        came = swap(other)
+        size = mine.shape[0] // PIECES
+        cuts = [slice(i * size, (i + 1) * size) for i in range(PIECES)]
+        send = [add(mine[cut], came[cut]) for cut in cuts]
         mine, other, turn = weight_sums(turn, totals, group, 0)
-        got = lax.ppermute(send, "dp", [(0, 1), (1, 0)])
-        terms = (mine, swap(other), got)
-        grads = finish(*terms, rows=2)
+        got = [lax.ppermute(v, "dp", [(0, 1), (1, 0)]) for v in send]
+        for n in range(min(PIECES - 1, full)):
+            at = full - 1 - n if PIECES > 2 else 1
+            *local[at], got[n] = lax.optimization_barrier((*local[at], got[n]))
+        grads = finish(mine, swap(other), *got, rows=2, whole=2)
     else:
         mine, other, turn = weight_sums(turn, totals, group)
-        grads = finish(add(mine, swap(other)), rows=1)
+        grads = finish(add(mine, swap(other)), rows=1, whole=1)
         turn, grads = grads[-1], [
             lax.psum_scatter(v, "dp", scatter_dimension=0, tiled=True) for v in grads[:-1]
         ]
@@ -423,7 +436,7 @@
         functools.partial(home_kernel, len(parts)),
         out_shape=(
             jax.ShapeDtypeStruct((tok_dev, width), BF16),
-            jax.ShapeDtypeStruct(ids_t.shape, F32),
+            jax.ShapeDtypeStruct(ids_t.shape, BF16),
         ),
         in_specs=[ANY] + [VMEM] * (1 + len(parts)),
         out_specs=(VMEM, VMEM),
@@ -432,7 +445,7 @@
     )(turn, ids_t, *parts)
     return (
         grad_tokens,
-        grad_probs.T.astype(BF16),
+        grad_probs.T,
         *(v[None] for v in grads),
     )
 

time: 94.5 us -> 89.6 us (0.948)
  waiting for transfers between devices: 44.8 us -> 37.8 us
  starting transfers between devices: 19.9 us -> 22.5 us
    ppermute x8, waiting for transfers between devices: 31.6 us -> 21.3 us  [on_device(): right = lambda v: lax.ppermute(v, 'expert', hop[1])]
    ppermute x1 -> x3, starting transfers between devices: 1.39 us -> 4.03 us  [on_device(): got = [lax.ppermute(v, 'dp', [(0, 1), (1, 0)]) for v in send]]
    ppermute x1 -> x3, waiting for transfers between devices: 11.9 us -> 14.4 us  [on_device(): got = [lax.ppermute(v, 'dp', [(0, 1), (1, 0)]) for v in send]]
  transfers between devices with their start and end apart: 22 -> 24, of which waited for: 10 -> 11; matrix products, arithmetic and copies ran while one was open for 1% -> 1% of each run, Pallas kernels for 22% -> 23%
where the time goes in v5:
time: 89.6 us; the launch traced here: 89.3 us
  waiting for transfers between devices  37.8 us (42%)
  Pallas kernels  24.1 us (27%)
  starting transfers between devices  22.5 us (25%)
  local copies, waits for them, and re-layouts  3.44 us (4%)
    ppermute x8, waiting for transfers between devices, on_device(): right = lambda v: lax.ppermute(v, 'expert', hop[1])  21.3 us
    pallas_call x5, Pallas kernels, expert(): pl.pallas_call(functools.partial(expert_kernel, halves, half, width, ff,...  17.3 us
    ppermute x3, waiting for transfers between devices, on_device(): got = [lax.ppermute(v, 'dp', [(0, 1), (1, 0)]) for v in send]  14.4 us
    ppermute x8, starting transfers between devices, on_device(): right = lambda v: lax.ppermute(v, 'expert', hop[1])  13.4 us
    ppermute x3, starting transfers between devices, on_device(): got = [lax.ppermute(v, 'dp', [(0, 1), (1, 0)]) for v in send]  4.03 us
    ppermute x8, starting transfers between devices, on_device(): left = lambda v: lax.ppermute(v, 'expert', hop[-1])  3.95 us
    unnamed x8, local copies, waits for them, and re-layouts  3.4 us
    pallas_call x2, Pallas kernels, weight_sums(): pl.pallas_call(functools.partial(weight_kernel, STEPS // parts, away), ou...  2.14 us
  transfers between devices with their start and end apart: 24, of which 11 were waited for; matrix products, arithmetic and copies ran while one was open for 1% of the time, Pallas kernels for 23%

profile of v5, /device:TPU:0, one launch (start us, length us, event | category | flops | bytes accessed | tf_op | source)
XLA Modules:
  0.0 89.3 jit_solution(18382814110904478948)
XLA Ops:
  0.6 0.5 collective-permute-start.1
  1.1 0.1 collective-permute-start.2
  1.2 0.4 collective-permute-start.3
  1.7 1.1 %pack.1 = (bf16[2,65,16,128]{3,2,1,0:T(8,128)(2,1)S(1)}, f32[8,128]{1,0:T(8,128)S(1)}) custom-call(bf16[128,1024]{1,0:T(8,128)(2,1)} %tok_ref.1, bf16[128,1024]{1,0:T(8,128)(2,1)} %cot_ref.1, s32[8,128]{1,0:T(8,128)} %bitcast.15, bf16[8,128]{1,0:T(8,128)(2,1)} %bitcast.17), custom_call_target="tpu_custom_call" | custom-call | tf_op jit(solution)/shard_map/pack/pallas_call | solution.py:308
  2.8 2.7 %collective-permute-start = (bf16[2,65,16,128]{3,2,1,0:T(8,128)(2,1)S(1)}, bf16[2,65,16,128]{3,2,1,0:T(8,128)(2,1)S(1)}, u32[]{:S(2)}, u32[]{:S(2)}) collective-permute-start(bf16[2,65,16,128]{3,2,1,0:T(8,128)(2,1)S(1)} %get-tuple-element.64.refs_1_), channel_id=1, source_target_pairs={{0,4},{1,5},{4,8},{5,9},{8,12},{9,13},{12,14},{13,15},{14,10},{15,... | collective-permute-start | bytes 1597448 | tf_op jit(solution)/shard_map/ppermute | solution.py:298
  5.5 0.0 collective-permute-start.5
  5.5 0.0 collective-permute-done.1.refs_3_
  5.5 0.0 collective-permute-done.2.refs_4_
  5.5 0.0 collective-permute-done.3.refs_5_
  5.5 1.1 %copy-done = bf16[1,1024,384]{2,1,0:T(8,128)(2,1)S(1)} copy-done((bf16[1,1024,384]{2,1,0:T(8,128)(2,1)S(1)}, bf16[1,1024,384]{2,1,0:T(8,128)(2,1)}, u32[]{:S(2)}) %copy-start) | copy-done | bytes 786456
  6.7 1.1 %copy-done.1 = bf16[1,1024,384]{2,1,0:T(8,128)(2,1)S(1)} copy-done((bf16[1,1024,384]{2,1,0:T(8,128)(2,1)S(1)}, bf16[1,1024,384]{2,1,0:T(8,128)(2,1)}, u32[]{:S(2)}) %copy-start.1) | copy-done | bytes 786456
  7.8 1.1 %copy-done.2 = bf16[1,384,1024]{2,1,0:T(8,128)(2,1)S(1)} copy-done((bf16[1,384,1024]{2,1,0:T(8,128)(2,1)S(1)}, bf16[1,384,1024]{2,1,0:T(8,128)(2,1)}, u32[]{:S(2)}) %copy-start.2) | copy-done | bytes 786456
  8.9 1.4 %weights.1.refs_2_.refs_3_ = bf16[2,15360,128]{2,1,0:T(8,128)(2,1)S(1)} custom-call(bf16[1024,384]{1,0:T(8,128)(2,1)S(1)} %bitcast.10, bf16[1024,384]{1,0:T(8,128)(2,1)S(1)} %bitcast.12, bf16[384,1024]{1,0:T(8,128)(2,1)S(1)} %bitcast.14, bf16[1024,384]{1,0:T(8,128)(2,1)S(1)} %collective-permute-done.1.refs_3_, ...), custom_call_target="tpu_custom_call" | custom-call | bytes 9437184 | tf_op jit(solution)/shard_map/weights/pallas_call | solution.py:319
  10.3 2.9 %expert.5 = (bf16[2,33,16,128]{3,2,1,0:T(8,128)(2,1)S(1)}, f32[2,9216,128]{2,1,0:T(8,128)S(1)}, f32[8,128]{1,0:T(8,128)S(1)}) custom-call(f32[8,128]{1,0:T(8,128)S(1)} %get-tuple-element.65.refs_0_, bf16[2,65,16,128]{3,2,1,0:T(8,128)(2,1)S(1)} %get-tuple-element.64.refs_1_, bf16[2,15360,128]{2,1,0:T(8,128)(2,1)S(1)} %weights.1.refs_2_.refs_3_), custom_call_target="tpu_custom_call" | custom-call | flops 1610612736 | bytes 8388608 | tf_op jit(solution)/shard_map/expert/pallas_call | solution.py:344
  13.2 4.9 %collective-permute-done.refs_1_ = bf16[2,65,16,128]{3,2,1,0:T(8,128)(2,1)S(1)} collective-permute-done((bf16[2,65,16,128]{3,2,1,0:T(8,128)(2,1)S(1)}, bf16[2,65,16,128]{3,2,1,0:T(8,128)(2,1)S(1)}, u32[]{:S(2)}, u32[]{:S(2)}) %collective-permute-start) | collective-permute-done | bytes 532512 | tf_op jit(solution)/shard_map/ppermute | solution.py:298
  18.1 1.8 %collective-permute-start.4 = (bf16[2,65,16,128]{3,2,1,0:T(8,128)(2,1)S(1)}, bf16[2,65,16,128]{3,2,1,0:T(8,128)(2,1)S(1)}, u32[]{:S(2)}, u32[]{:S(2)}) collective-permute-start(bf16[2,65,16,128]{3,2,1,0:T(8,128)(2,1)S(1)} %collective-permute-done.refs_1_), channel_id=1, source_target_pairs={{0,4},{1,5},{4,8},{5,9},{8,12},{9,13},{12,14},{13,15},{14,10},{15,... | collective-permute-start | bytes 1597448 | tf_op jit(solution)/shard_map/ppermute | solution.py:298
  19.9 0.0 collective-permute-done.5.refs_2_
  19.9 0.2 collective-permute-start.7
  20.1 4.3 %expert.6 = (bf16[2,33,16,128]{3,2,1,0:T(8,128)(2,1)S(1)}, bf16[2,33,16,128]{3,2,1,0:T(8,128)(2,1)S(1)}, f32[2,9216,128]{2,1,0:T(8,128)S(1)}, f32[8,128]{1,0:T(8,128)S(1)}) custom-call(f32[8,128]{1,0:T(8,128)S(1)} %get-tuple-element.69.refs_0_, bf16[2,65,16,128]{3,2,1,0:T(8,128)(2,1)S(1)} %collective-permute-done.refs_1_, ...), custom_call_target="tpu_custom_call" | custom-call | flops 3221225472 | bytes 8388608 | tf_op jit(solution)/shard_map/expert/pallas_call | solution.py:344
  24.4 7.6 %collective-permute-done.4.refs_1_ = bf16[2,65,16,128]{3,2,1,0:T(8,128)(2,1)S(1)} collective-permute-done((bf16[2,65,16,128]{3,2,1,0:T(8,128)(2,1)S(1)}, bf16[2,65,16,128]{3,2,1,0:T(8,128)(2,1)S(1)}, u32[]{:S(2)}, u32[]{:S(2)}) %collective-permute-start.4) | collective-permute-done | bytes 532512 | tf_op jit(solution)/shard_map/ppermute | solution.py:298
  32.0 1.6 %collective-permute-start.6 = (bf16[2,65,16,128]{3,2,1,0:T(8,128)(2,1)S(1)}, bf16[2,65,16,128]{3,2,1,0:T(8,128)(2,1)S(1)}, u32[]{:S(2)}, u32[]{:S(2)}) collective-permute-start(bf16[2,65,16,128]{3,2,1,0:T(8,128)(2,1)S(1)} %collective-permute-done.4.refs_1_), channel_id=1, source_target_pairs={{0,4},{1,5},{4,8},{5,9},{8,12},{9,13},{12,14},{13,15},{14,10},{15,... | collective-permute-start | bytes 1597448 | tf_op jit(solution)/shard_map/ppermute | solution.py:298
  33.6 0.0 collective-permute-done.7.refs_2_
  33.6 0.4 collective-permute-start.9
  34.0 4.2 %expert.7 = (bf16[2,33,16,128]{3,2,1,0:T(8,128)(2,1)S(1)}, bf16[2,33,16,128]{3,2,1,0:T(8,128)(2,1)S(1)}, f32[2,9216,128]{2,1,0:T(8,128)S(1)}, f32[8,128]{1,0:T(8,128)S(1)}) custom-call(f32[8,128]{1,0:T(8,128)S(1)} %get-tuple-element.75.refs_0_, bf16[2,65,16,128]{3,2,1,0:T(8,128)(2,1)S(1)} %collective-permute-done.4.refs_1_, ...), custom_call_target="tpu_custom_call" | custom-call | flops 3221225472 | bytes 8388608 | tf_op jit(solution)/shard_map/expert/pallas_call | solution.py:344
  38.2 6.7 %collective-permute-done.6.refs_1_ = bf16[2,65,16,128]{3,2,1,0:T(8,128)(2,1)S(1)} collective-permute-done((bf16[2,65,16,128]{3,2,1,0:T(8,128)(2,1)S(1)}, bf16[2,65,16,128]{3,2,1,0:T(8,128)(2,1)S(1)}, u32[]{:S(2)}, u32[]{:S(2)}) %collective-permute-start.6) | collective-permute-done | bytes 532512 | tf_op jit(solution)/shard_map/ppermute | solution.py:298
  45.0 1.1 %collective-permute-done.9.refs_2_ = bf16[2,65,16,128]{3,2,1,0:T(8,128)(2,1)S(1)} collective-permute-done((bf16[2,65,16,128]{3,2,1,0:T(8,128)(2,1)S(1)}, bf16[2,65,16,128]{3,2,1,0:T(8,128)(2,1)S(1)}, u32[]{:S(2)}, u32[]{:S(2)}) %collective-permute-start.9) | collective-permute-done | bytes 532512 | tf_op jit(solution)/shard_map/ppermute | solution.py:299
  46.1 0.7 collective-permute-start.10
  46.8 1.5 %collective-permute-start.8 = (bf16[1,65,16,128]{3,2,1,0:T(8,128)(2,1)S(1)}, bf16[1,65,16,128]{3,2,1,0:T(8,128)(2,1)S(1)}, u32[]{:S(2)}, u32[]{:S(2)}) collective-permute-start(bf16[1,65,16,128]{3,2,1,0:T(8,128)(2,1)S(1)} %slice.24), channel_id=1, source_target_pairs={{0,4},{1,5},{4,8},{5,9},{8,12},{9,13},{12,14},{13,15},{14,10},{15,... | collective-permute-start | bytes 798728 | tf_op jit(solution)/shard_map/ppermute | solution.py:298
  48.3 4.2 %expert.8 = (bf16[2,33,16,128]{3,2,1,0:T(8,128)(2,1)S(1)}, bf16[2,33,16,128]{3,2,1,0:T(8,128)(2,1)S(1)}, f32[2,9216,128]{2,1,0:T(8,128)S(1)}, f32[8,128]{1,0:T(8,128)S(1)}) custom-call(f32[8,128]{1,0:T(8,128)S(1)} %get-tuple-element.82.refs_0_, bf16[2,65,16,128]{3,2,1,0:T(8,128)(2,1)S(1)} %collective-permute-done.6.refs_1_, ...), custom_call_target="tpu_custom_call" | custom-call | flops 3221225472 | bytes 8388608 | tf_op jit(solution)/shard_map/expert/pallas_call | solution.py:344
  52.5 0.1 collective-permute-done.10.refs_2_
  52.6 0.7 collective-permute-done.8.refs_1_
  53.3 1.7 %expert.9 = (bf16[1,33,16,128]{3,2,1,0:T(8,128)(2,1)S(1)}, bf16[1,33,16,128]{3,2,1,0:T(8,128)(2,1)S(1)}, f32[8,128]{1,0:T(8,128)S(1)}, bf16[1024,128]{1,0:T(8,12...) custom-call(f32[8,128]{1,0:T(8,128)S(1)} %get-tuple-element.85.refs_, ...), custom_call_target="tpu_custom_call" | custom-call | flops 1006632960 | bytes 8388608 | tf_op jit(solution)/shard_map/expert/pallas_call | solution.py:344
  54.9 0.8 weight_sums.2
  55.8 0.1 collective-permute-start.12
  55.8 1.5 %collective-permute-start.20 = (bf16[1,33,16,128]{3,2,1,0:T(8,128)(2,1)S(1)}, bf16[1,33,16,128]{3,2,1,0:T(8,128)(2,1)S(1)}, u32[]{:S(2)}, u32[]{:S(2)}) collective-permute-start(bf16[1,33,16,128]{3,2,1,0:T(8,128)(2,1)S(1)} %get-tuple-element.114), channel_id=1, source_target_pairs={{0,4},{1,5},{4,8},{5,9},{8,12},{9,13},{12,14},{13,15},{14,10},{15,... | collective-permute-start | bytes 405512 | tf_op jit(solution)/shard_map/ppermute | solution.py:298
  57.3 0.6 collective-permute-start.16
  57.9 0.8 collective-permute-done.12
  58.7 0.3 add_convert_fusion
  59.0 1.4 %collective-permute-start.13 = (bf16[96,16,128]{2,1,0:T(8,128)(2,1)S(1)}, bf16[96,16,128]{2,1,0:T(8,128)(2,1)S(1)}, u32[]{:S(2)}, u32[]{:S(2)}) collective-permute-start(bf16[96,16,128]{2,1,0:T(8,128)(2,1)S(1)} %get-tuple-element.125), channel_id=1, source_target_pairs={{0,16},{16,0},{1,17},{17,1},{2,18},{18,2},{3,19},{19,3},{4,20},{20... | collective-permute-start | bytes 1179656 | tf_op jit(solution)/shard_map/ppermute | solution.py:404
  60.4 1.5 %collective-permute-done.20 = bf16[1,33,16,128]{3,2,1,0:T(8,128)(2,1)S(1)} collective-permute-done((bf16[1,33,16,128]{3,2,1,0:T(8,128)(2,1)S(1)}, bf16[1,33,16,128]{3,2,1,0:T(8,128)(2,1)S(1)}, u32[]{:S(2)}, u32[]{:S(2)}) %collective-permute-start.20) | collective-permute-done | bytes 135200 | tf_op jit(solution)/shard_map/ppermute | solution.py:298
  61.9 1.5 %collective-permute-start.21 = (bf16[2,33,16,128]{3,2,1,0:T(8,128)(2,1)S(1)}, bf16[2,33,16,128]{3,2,1,0:T(8,128)(2,1)S(1)}, u32[]{:S(2)}, u32[]{:S(2)}) collective-permute-start(bf16[2,33,16,128]{3,2,1,0:T(8,128)(2,1)S(1)} %add_convert_fusion.5), channel_id=1, source_target_pairs={{0,4},{1,5},{4,8},{5,9},{8,12},{9,13},{12,14},{13,15},{14,10},{15,... | collective-permute-start | bytes 811016 | tf_op jit(solution)/shard_map/ppermute | solution.py:298
  63.3 0.0 collective-permute-done.16
  63.4 0.7 collective-permute-start.17
  64.1 1.3 %weight_sums.3 = (bf16[288,16,128]{2,1,0:T(8,128)(2,1)S(1)}, bf16[288,16,128]{2,1,0:T(8,128)(2,1)S(1)}, f32[8,128]{1,0:T(8,128)}) custom-call(f32[8,128]{1,0:T(8,128)S(1)} %get-tuple-element.97.turn_ref, f32[2,9216,128]{2,1,0:T(8,128)S(1)} %get-tuple-element.89.refs_0_, bf16[1024,128]{1,0:T(8,128)(2,1)S(1)} %get-tuple-element.90.refs_1_, ...), custom_call_target="tpu_custom_call" | custom-call | flops 301989888 | bytes 8388608 | tf_op jit(solution)/shard_map/weight_sums/pallas_call | solution.py:205
  65.4 1.3 %collective-permute-start.14 = (bf16[96,16,128]{2,1,0:T(8,128)(2,1)S(1)}, bf16[96,16,128]{2,1,0:T(8,128)(2,1)S(1)}, u32[]{:S(2)}, u32[]{:S(2)}) collective-permute-start(bf16[96,16,128]{2,1,0:T(8,128)(2,1)S(1)} %get-tuple-element.124), channel_id=1, source_target_pairs={{0,16},{16,0},{1,17},{17,1},{2,18},{18,2},{3,19},{19,3},{4,20},{20... | collective-permute-start | bytes 1179656 | tf_op jit(solution)/shard_map/ppermute | solution.py:404
  66.7 4.3 %collective-permute-done.13.refs_2_ = bf16[96,16,128]{2,1,0:T(8,128)(2,1)S(1)} collective-permute-done((bf16[96,16,128]{2,1,0:T(8,128)(2,1)S(1)}, bf16[96,16,128]{2,1,0:T(8,128)(2,1)S(1)}, u32[]{:S(2)}, u32[]{:S(2)}) %collective-permute-start.13) | collective-permute-done | bytes 393248 | tf_op jit(solution)/shard_map/ppermute | solution.py:404
  71.0 0.0 collective-permute-done.21
  71.0 0.1 add_convert_fusion.4
  71.1 1.5 %collective-permute-start.22 = (bf16[2,33,16,128]{3,2,1,0:T(8,128)(2,1)S(1)}, bf16[2,33,16,128]{3,2,1,0:T(8,128)(2,1)S(1)}, u32[]{:S(2)}, u32[]{:S(2)}) collective-permute-start(bf16[2,33,16,128]{3,2,1,0:T(8,128)(2,1)S(1)} %add_convert_fusion.4), channel_id=1, source_target_pairs={{0,4},{1,5},{4,8},{5,9},{8,12},{9,13},{12,14},{13,15},{14,10},{15,... | collective-permute-start | bytes 811016 | tf_op jit(solution)/shard_map/ppermute | solution.py:298
  72.6 0.1 add_convert_fusion.7
  72.6 0.7 collective-permute-start.18
  73.3 1.3 %collective-permute-start.15 = (bf16[96,16,128]{2,1,0:T(8,128)(2,1)S(1)}, bf16[96,16,128]{2,1,0:T(8,128)(2,1)S(1)}, u32[]{:S(2)}, u32[]{:S(2)}) collective-permute-start(bf16[96,16,128]{2,1,0:T(8,128)(2,1)S(1)} %get-tuple-element.123), channel_id=1, source_target_pairs={{0,16},{16,0},{1,17},{17,1},{2,18},{18,2},{3,19},{19,3},{4,20},{20... | collective-permute-start | bytes 1179656 | tf_op jit(solution)/shard_map/ppermute | solution.py:404
  74.6 4.8 %collective-permute-done.14.refs_3_ = bf16[96,16,128]{2,1,0:T(8,128)(2,1)S(1)} collective-permute-done((bf16[96,16,128]{2,1,0:T(8,128)(2,1)S(1)}, bf16[96,16,128]{2,1,0:T(8,128)(2,1)S(1)}, u32[]{:S(2)}, u32[]{:S(2)}) %collective-permute-start.14) | collective-permute-done | bytes 393248 | tf_op jit(solution)/shard_map/ppermute | solution.py:404
  79.4 0.0 collective-permute-done.22
  79.4 0.1 add_convert_fusion.3
  79.5 1.5 %collective-permute-start.23 = (bf16[2,33,16,128]{3,2,1,0:T(8,128)(2,1)S(1)}, bf16[2,33,16,128]{3,2,1,0:T(8,128)(2,1)S(1)}, u32[]{:S(2)}, u32[]{:S(2)}) collective-permute-start(bf16[2,33,16,128]{3,2,1,0:T(8,128)(2,1)S(1)} %add_convert_fusion.3), channel_id=1, source_target_pairs={{0,4},{1,5},{4,8},{5,9},{8,12},{9,13},{12,14},{13,15},{14,10},{15,... | collective-permute-start | bytes 811016 | tf_op jit(solution)/shard_map/ppermute | solution.py:298
  81.0 0.0 collective-permute-done.18
  81.0 0.1 add_convert_fusion.6
  81.1 0.7 collective-permute-start.19
  81.7 0.0 collective-permute-done.11.refs_1_
  81.7 5.3 %collective-permute-done.15.refs_4_ = bf16[96,16,128]{2,1,0:T(8,128)(2,1)S(1)} collective-permute-done((bf16[96,16,128]{2,1,0:T(8,128)(2,1)S(1)}, bf16[96,16,128]{2,1,0:T(8,128)(2,1)S(1)}, u32[]{:S(2)}, u32[]{:S(2)}) %collective-permute-start.15) | collective-permute-done | bytes 393248 | tf_op jit(solution)/shard_map/ppermute | solution.py:404
  87.1 1.4 %finish.1 = (bf16[512,384]{1,0:T(8,128)(2,1)}, bf16[512,384]{1,0:T(8,128)(2,1)}, bf16[192,1024]{1,0:T(8,128)(2,1)}, f32[8,128]{1,0:T(8,128)S(1)}) custom-call(bf16[288,16,128]{2,1,0:T(8,128)(2,1)S(1)} %get-tuple-element.98.refs_0_, bf16[288,16,128]{2,1,0:T(8,128)(2,1)S(1)} %collective-permute-done.11.refs_1_, ...), custom_call_target="tpu_custom_call" | custom-call | tf_op jit(solution)/shard_map/finish/pallas_call | solution.py:387
  88.5 0.0 collective-permute-done.23.refs_2_
  88.5 0.8 home.1
  (12 shorter events, 0.1 us)
Async XLA Ops:
  0.6 4.9 %collective-permute-start.1 = (bf16[1024,384]{1,0:T(8,128)(2,1)}, bf16[1024,384]{1,0:T(8,128)(2,1)S(1)}, u32[]{:S(2)}, u32[]{:S(2)}) collective-permute-start(bf16[1024,384]{1,0:T(8,128)(2,1)} %bitcast.9), channel_id=1, source_target_pairs={{0,1},{1,0},{2,3},{3,2},{4,5},{5,4},{6,7},{7,6},{8,9},{9,8},{10,11... | collective-permute-start | bytes 2359304 | tf_op jit(solution)/shard_map/ppermute | solution.py:300
  1.1 4.3 %collective-permute-start.2 = (bf16[1024,384]{1,0:T(8,128)(2,1)}, bf16[1024,384]{1,0:T(8,128)(2,1)S(1)}, u32[]{:S(2)}, u32[]{:S(2)}) collective-permute-start(bf16[1024,384]{1,0:T(8,128)(2,1)} %bitcast.11), channel_id=1, source_target_pairs={{0,1},{1,0},{2,3},{3,2},{4,5},{5,4},{6,7},{7,6},{8,9},{9,8},{10,11... | collective-permute-start | bytes 2359304 | tf_op jit(solution)/shard_map/ppermute | solution.py:300
  1.2 4.3 %collective-permute-start.3 = (bf16[384,1024]{1,0:T(8,128)(2,1)}, bf16[384,1024]{1,0:T(8,128)(2,1)S(1)}, u32[]{:S(2)}, u32[]{:S(2)}) collective-permute-start(bf16[384,1024]{1,0:T(8,128)(2,1)} %bitcast.13), channel_id=1, source_target_pairs={{0,1},{1,0},{2,3},{3,2},{4,5},{5,4},{6,7},{7,6},{8,9},{9,8},{10,11... | collective-permute-start | bytes 2359304 | tf_op jit(solution)/shard_map/ppermute | solution.py:300
  2.8 15.3 %collective-permute-start = (bf16[2,65,16,128]{3,2,1,0:T(8,128)(2,1)S(1)}, bf16[2,65,16,128]{3,2,1,0:T(8,128)(2,1)S(1)}, u32[]{:S(2)}, u32[]{:S(2)}) collective-permute-start(bf16[2,65,16,128]{3,2,1,0:T(8,128)(2,1)S(1)} %get-tuple-element.64.refs_1_), channel_id=1, source_target_pairs={{0,4},{1,5},{4,8},{5,9},{8,12},{9,13},{12,14},{13,15},{14,10},{15,... | collective-permute-start | bytes 1597448 | tf_op jit(solution)/shard_map/ppermute | solution.py:298
  5.5 14.5 %collective-permute-start.5 = (bf16[2,65,16,128]{3,2,1,0:T(8,128)(2,1)S(1)}, bf16[2,65,16,128]{3,2,1,0:T(8,128)(2,1)S(1)}, u32[]{:S(2)}, u32[]{:S(2)}) collective-permute-start(bf16[2,65,16,128]{3,2,1,0:T(8,128)(2,1)S(1)} %get-tuple-element.64.refs_1_), channel_id=1, source_target_pairs={{0,2},{1,3},{4,0},{5,1},{8,4},{9,5},{12,8},{13,9},{14,12},{15,13},... | collective-permute-start | bytes 1597448 | tf_op jit(solution)/shard_map/ppermute | solution.py:299
  5.5 1.1 %copy-start = (bf16[1,1024,384]{2,1,0:T(8,128)(2,1)S(1)}, bf16[1,1024,384]{2,1,0:T(8,128)(2,1)}, u32[]{:S(2)}) copy-start(bf16[1,1024,384]{2,1,0:T(8,128)(2,1)} %param.11) | copy-start | bytes 2359300
  6.7 1.1 %copy-start.1 = (bf16[1,1024,384]{2,1,0:T(8,128)(2,1)S(1)}, bf16[1,1024,384]{2,1,0:T(8,128)(2,1)}, u32[]{:S(2)}) copy-start(bf16[1,1024,384]{2,1,0:T(8,128)(2,1)} %param.12) | copy-start | bytes 2359300
  7.8 1.1 %copy-start.2 = (bf16[1,384,1024]{2,1,0:T(8,128)(2,1)S(1)}, bf16[1,384,1024]{2,1,0:T(8,128)(2,1)}, u32[]{:S(2)}) copy-start(bf16[1,384,1024]{2,1,0:T(8,128)(2,1)} %param.13) | copy-start | bytes 2359300
  18.1 13.9 %collective-permute-start.4 = (bf16[2,65,16,128]{3,2,1,0:T(8,128)(2,1)S(1)}, bf16[2,65,16,128]{3,2,1,0:T(8,128)(2,1)S(1)}, u32[]{:S(2)}, u32[]{:S(2)}) collective-permute-start(bf16[2,65,16,128]{3,2,1,0:T(8,128)(2,1)S(1)} %collective-permute-done.refs_1_), channel_id=1, source_target_pairs={{0,4},{1,5},{4,8},{5,9},{8,12},{9,13},{12,14},{13,15},{14,10},{15,... | collective-permute-start | bytes 1597448 | tf_op jit(solution)/shard_map/ppermute | solution.py:298
  19.9 13.7 %collective-permute-start.7 = (bf16[2,65,16,128]{3,2,1,0:T(8,128)(2,1)S(1)}, bf16[2,65,16,128]{3,2,1,0:T(8,128)(2,1)S(1)}, u32[]{:S(2)}, u32[]{:S(2)}) collective-permute-start(bf16[2,65,16,128]{3,2,1,0:T(8,128)(2,1)S(1)} %collective-permute-done.5.refs_2_), channel_id=1, source_target_pairs={{0,2},{1,3},{4,0},{5,1},{8,4},{9,5},{12,8},{13,9},{14,12},{15,13},... | collective-permute-start | bytes 1597448 | tf_op jit(solution)/shard_map/ppermute | solution.py:299
  32.0 13.0 %collective-permute-start.6 = (bf16[2,65,16,128]{3,2,1,0:T(8,128)(2,1)S(1)}, bf16[2,65,16,128]{3,2,1,0:T(8,128)(2,1)S(1)}, u32[]{:S(2)}, u32[]{:S(2)}) collective-permute-start(bf16[2,65,16,128]{3,2,1,0:T(8,128)(2,1)S(1)} %collective-permute-done.4.refs_1_), channel_id=1, source_target_pairs={{0,4},{1,5},{4,8},{5,9},{8,12},{9,13},{12,14},{13,15},{14,10},{15,... | collective-permute-start | bytes 1597448 | tf_op jit(solution)/shard_map/ppermute | solution.py:298
  33.6 12.5 %collective-permute-start.9 = (bf16[2,65,16,128]{3,2,1,0:T(8,128)(2,1)S(1)}, bf16[2,65,16,128]{3,2,1,0:T(8,128)(2,1)S(1)}, u32[]{:S(2)}, u32[]{:S(2)}) collective-permute-start(bf16[2,65,16,128]{3,2,1,0:T(8,128)(2,1)S(1)} %collective-permute-done.7.refs_2_), channel_id=1, source_target_pairs={{0,2},{1,3},{4,0},{5,1},{8,4},{9,5},{12,8},{13,9},{14,12},{15,13},... | collective-permute-start | bytes 1597448 | tf_op jit(solution)/shard_map/ppermute | solution.py:299
  46.1 6.5 %collective-permute-start.10 = (bf16[1,65,16,128]{3,2,1,0:T(8,128)(2,1)S(1)}, bf16[1,65,16,128]{3,2,1,0:T(8,128)(2,1)S(1)}, u32[]{:S(2)}, u32[]{:S(2)}) collective-permute-start(bf16[1,65,16,128]{3,2,1,0:T(8,128)(2,1)S(1)} %slice.25), channel_id=1, source_target_pairs={{0,2},{1,3},{4,0},{5,1},{8,4},{9,5},{12,8},{13,9},{14,12},{15,13},... | collective-permute-start | bytes 798728 | tf_op jit(solution)/shard_map/ppermute | solution.py:299
  46.8 6.5 %collective-permute-start.8 = (bf16[1,65,16,128]{3,2,1,0:T(8,128)(2,1)S(1)}, bf16[1,65,16,128]{3,2,1,0:T(8,128)(2,1)S(1)}, u32[]{:S(2)}, u32[]{:S(2)}) collective-permute-start(bf16[1,65,16,128]{3,2,1,0:T(8,128)(2,1)S(1)} %slice.24), channel_id=1, source_target_pairs={{0,4},{1,5},{4,8},{5,9},{8,12},{9,13},{12,14},{13,15},{14,10},{15,... | collective-permute-start | bytes 798728 | tf_op jit(solution)/shard_map/ppermute | solution.py:298
  55.8 2.9 %collective-permute-start.12 = (bf16[288,16,128]{2,1,0:T(8,128)(2,1)S(1)}, bf16[288,16,128]{2,1,0:T(8,128)(2,1)S(1)}, u32[]{:S(2)}, u32[]{:S(2)}) collective-permute-start(bf16[288,16,128]{2,1,0:T(8,128)(2,1)S(1)} %get-tuple-element.103), channel_id=1, source_target_pairs={{0,1},{1,0},{2,3},{3,2},{4,5},{5,4},{6,7},{7,6},{8,9},{9,8},{10,11... | collective-permute-start | bytes 3538952 | tf_op jit(solution)/shard_map/ppermute | solution.py:300
  55.8 6.0 %collective-permute-start.20 = (bf16[1,33,16,128]{3,2,1,0:T(8,128)(2,1)S(1)}, bf16[1,33,16,128]{3,2,1,0:T(8,128)(2,1)S(1)}, u32[]{:S(2)}, u32[]{:S(2)}) collective-permute-start(bf16[1,33,16,128]{3,2,1,0:T(8,128)(2,1)S(1)} %get-tuple-element.114), channel_id=1, source_target_pairs={{0,4},{1,5},{4,8},{5,9},{8,12},{9,13},{12,14},{13,15},{14,10},{15,... | collective-permute-start | bytes 405512 | tf_op jit(solution)/shard_map/ppermute | solution.py:298
  57.3 6.0 %collective-permute-start.16 = (bf16[1,33,16,128]{3,2,1,0:T(8,128)(2,1)S(1)}, bf16[1,33,16,128]{3,2,1,0:T(8,128)(2,1)S(1)}, u32[]{:S(2)}, u32[]{:S(2)}) collective-permute-start(bf16[1,33,16,128]{3,2,1,0:T(8,128)(2,1)S(1)} %get-tuple-element.110), channel_id=1, source_target_pairs={{0,2},{1,3},{4,0},{5,1},{8,4},{9,5},{12,8},{13,9},{14,12},{15,13},... | collective-permute-start | bytes 405512 | tf_op jit(solution)/shard_map/ppermute | solution.py:299
  59.0 12.0 %collective-permute-start.13 = (bf16[96,16,128]{2,1,0:T(8,128)(2,1)S(1)}, bf16[96,16,128]{2,1,0:T(8,128)(2,1)S(1)}, u32[]{:S(2)}, u32[]{:S(2)}) collective-permute-start(bf16[96,16,128]{2,1,0:T(8,128)(2,1)S(1)} %get-tuple-element.125), channel_id=1, source_target_pairs={{0,16},{16,0},{1,17},{17,1},{2,18},{18,2},{3,19},{19,3},{4,20},{20... | collective-permute-start | bytes 1179656 | tf_op jit(solution)/shard_map/ppermute | solution.py:404
  61.9 9.1 %collective-permute-start.21 = (bf16[2,33,16,128]{3,2,1,0:T(8,128)(2,1)S(1)}, bf16[2,33,16,128]{3,2,1,0:T(8,128)(2,1)S(1)}, u32[]{:S(2)}, u32[]{:S(2)}) collective-permute-start(bf16[2,33,16,128]{3,2,1,0:T(8,128)(2,1)S(1)} %add_convert_fusion.5), channel_id=1, source_target_pairs={{0,4},{1,5},{4,8},{5,9},{8,12},{9,13},{12,14},{13,15},{14,10},{15,... | collective-permute-start | bytes 811016 | tf_op jit(solution)/shard_map/ppermute | solution.py:298
  63.4 9.2 %collective-permute-start.17 = (bf16[2,33,16,128]{3,2,1,0:T(8,128)(2,1)S(1)}, bf16[2,33,16,128]{3,2,1,0:T(8,128)(2,1)S(1)}, u32[]{:S(2)}, u32[]{:S(2)}) collective-permute-start(bf16[2,33,16,128]{3,2,1,0:T(8,128)(2,1)S(1)} %add_convert_fusion.8), channel_id=1, source_target_pairs={{0,2},{1,3},{4,0},{5,1},{8,4},{9,5},{12,8},{13,9},{14,12},{15,13},... | collective-permute-start | bytes 811016 | tf_op jit(solution)/shard_map/ppermute | solution.py:299
  65.4 16.3 %collective-permute-start.11 = (bf16[288,16,128]{2,1,0:T(8,128)(2,1)S(1)}, bf16[288,16,128]{2,1,0:T(8,128)(2,1)S(1)}, u32[]{:S(2)}, u32[]{:S(2)}) collective-permute-start(bf16[288,16,128]{2,1,0:T(8,128)(2,1)S(1)} %get-tuple-element.99), channel_id=1, source_target_pairs={{0,1},{1,0},{2,3},{3,2},{4,5},{5,4},{6,7},{7,6},{8,9},{9,8},{10,11... | collective-permute-start | bytes 3538952 | tf_op jit(solution)/shard_map/ppermute | solution.py:300
  65.4 14.0 %collective-permute-start.14 = (bf16[96,16,128]{2,1,0:T(8,128)(2,1)S(1)}, bf16[96,16,128]{2,1,0:T(8,128)(2,1)S(1)}, u32[]{:S(2)}, u32[]{:S(2)}) collective-permute-start(bf16[96,16,128]{2,1,0:T(8,128)(2,1)S(1)} %get-tuple-element.124), channel_id=1, source_target_pairs={{0,16},{16,0},{1,17},{17,1},{2,18},{18,2},{3,19},{19,3},{4,20},{20... | collective-permute-start | bytes 1179656 | tf_op jit(solution)/shard_map/ppermute | solution.py:404
  71.1 8.3 %collective-permute-start.22 = (bf16[2,33,16,128]{3,2,1,0:T(8,128)(2,1)S(1)}, bf16[2,33,16,128]{3,2,1,0:T(8,128)(2,1)S(1)}, u32[]{:S(2)}, u32[]{:S(2)}) collective-permute-start(bf16[2,33,16,128]{3,2,1,0:T(8,128)(2,1)S(1)} %add_convert_fusion.4), channel_id=1, source_target_pairs={{0,4},{1,5},{4,8},{5,9},{8,12},{9,13},{12,14},{13,15},{14,10},{15,... | collective-permute-start | bytes 811016 | tf_op jit(solution)/shard_map/ppermute | solution.py:298
  72.6 8.3 %collective-permute-start.18 = (bf16[2,33,16,128]{3,2,1,0:T(8,128)(2,1)S(1)}, bf16[2,33,16,128]{3,2,1,0:T(8,128)(2,1)S(1)}, u32[]{:S(2)}, u32[]{:S(2)}) collective-permute-start(bf16[2,33,16,128]{3,2,1,0:T(8,128)(2,1)S(1)} %add_convert_fusion.7), channel_id=1, source_target_pairs={{0,2},{1,3},{4,0},{5,1},{8,4},{9,5},{12,8},{13,9},{14,12},{15,13},... | collective-permute-start | bytes 811016 | tf_op jit(solution)/shard_map/ppermute | solution.py:299
  73.3 13.8 %collective-permute-start.15 = (bf16[96,16,128]{2,1,0:T(8,128)(2,1)S(1)}, bf16[96,16,128]{2,1,0:T(8,128)(2,1)S(1)}, u32[]{:S(2)}, u32[]{:S(2)}) collective-permute-start(bf16[96,16,128]{2,1,0:T(8,128)(2,1)S(1)} %get-tuple-element.123), channel_id=1, source_target_pairs={{0,16},{16,0},{1,17},{17,1},{2,18},{18,2},{3,19},{19,3},{4,20},{20... | collective-permute-start | bytes 1179656 | tf_op jit(solution)/shard_map/ppermute | solution.py:404
  79.5 8.9 %collective-permute-start.23 = (bf16[2,33,16,128]{3,2,1,0:T(8,128)(2,1)S(1)}, bf16[2,33,16,128]{3,2,1,0:T(8,128)(2,1)S(1)}, u32[]{:S(2)}, u32[]{:S(2)}) collective-permute-start(bf16[2,33,16,128]{3,2,1,0:T(8,128)(2,1)S(1)} %add_convert_fusion.3), channel_id=1, source_target_pairs={{0,4},{1,5},{4,8},{5,9},{8,12},{9,13},{12,14},{13,15},{14,10},{15,... | collective-permute-start | bytes 811016 | tf_op jit(solution)/shard_map/ppermute | solution.py:298
  81.1 7.4 %collective-permute-start.19 = (bf16[2,33,16,128]{3,2,1,0:T(8,128)(2,1)S(1)}, bf16[2,33,16,128]{3,2,1,0:T(8,128)(2,1)S(1)}, u32[]{:S(2)}, u32[]{:S(2)}) collective-permute-start(bf16[2,33,16,128]{3,2,1,0:T(8,128)(2,1)S(1)} %add_convert_fusion.6), channel_id=1, source_target_pairs={{0,2},{1,3},{4,0},{5,1},{8,4},{9,5},{12,8},{13,9},{14,12},{15,13},... | collective-permute-start | bytes 811016 | tf_op jit(solution)/shard_map/ppermute | solution.py:299
  87.1 1.4 %copy-start.3 = (s32[128,8]{0,1:T(8,128)S(1)}, s32[128,8]{0,1:T(8,128)}, u32[]{:S(2)}) copy-start(s32[128,8]{0,1:T(8,128)} %param.9) | copy-start | bytes 12292

commit v6 on v5

--- a/solution.py
+++ b/solution.py
@@ -11,7 +11,7 @@
 ROWS, LANES = 16, 128
 VMEM = pl.BlockSpec(memory_space=pltpu.VMEM)
 ANY = pl.BlockSpec(memory_space=pl.ANY)
-PIECES = 3
+SHARES = (1, 1, 2)
 STEPS = 4
 EXPERT_VMEM = 16 * 1024 * 1024
 TOKEN = jax.ShapeDtypeStruct((8, LANES), F32)
@@ -227,10 +227,11 @@
     n = 0
 
     def total(n):
-        size = refs[count - 1].shape[0]
         terms = [ref[n] for ref in refs[:whole]]
-        if whole < count:
-            terms.append(refs[whole + n // size][n % size])
+        for ref in refs[whole:count]:
+            if 0 <= n < ref.shape[0]:
+                terms.append(ref[n])
+            n -= ref.shape[0]
         return sum(t.astype(F32) for t in terms).astype(BF16)
 
     for step in range(outs[0].shape[0] // tile_w):
@@ -275,6 +276,12 @@
     prob_ref[...] = jnp.concatenate(rows, axis=0).astype(BF16)
 
 
+def last_kernel(count, whole, sides, *refs):
+    inputs, outs = refs[: count + 1 + sides], refs[count + 1 + sides :]
+    finish_kernel(count, whole, *inputs[:count], *outs[:4])
+    home_kernel(sides, None, *inputs[count:], *outs[4:])
+
+
 def on_device(tokens, cotangent, expert_ids, gate_probs, w_gate, w_up, w_down):
     tok_dev, width = tokens.shape
     ff = w_gate.shape[2]
@@ -397,15 +404,15 @@
     if groups == 2:
         mine, other, turn = weight_sums(turn, totals, group, 1)
         came = swap(other)
-        size = mine.shape[0] // PIECES
-        cuts = [slice(i * size, (i + 1) * size) for i in range(PIECES)]
+        marks = [mine.shape[0] * sum(SHARES[:i]) // sum(SHARES) for i in range(len(SHARES) + 1)]
+        cuts = [slice(*cut) for cut in zip(marks[:-1], marks[1:])]
         send = [add(mine[cut], came[cut]) for cut in cuts]
         mine, other, turn = weight_sums(turn, totals, group, 0)
         got = [lax.ppermute(v, "dp", [(0, 1), (1, 0)]) for v in send]
-        for n in range(min(PIECES - 1, full)):
-            at = full - 1 - n if PIECES > 2 else 1
+        for n in range(len(SHARES) - 1):
+            at = full - 1 - n
             *local[at], got[n] = lax.optimization_barrier((*local[at], got[n]))
-        grads = finish(mine, swap(other), *got, rows=2, whole=2)
+        terms = mine, swap(other), *got
     else:
         mine, other, turn = weight_sums(turn, totals, group)
         grads = finish(add(mine, swap(other)), rows=1, whole=1)
@@ -413,7 +420,8 @@
             lax.psum_scatter(v, "dp", scatter_dimension=0, tiled=True) for v in grads[:-1]
         ]
         grads = (*grads, turn)
-    *grads, turn = grads
+    if groups != 2:
+        *grads, turn = grads
 
     def back(side, move):
         moving = None
@@ -432,17 +440,29 @@
         return moving
 
     parts = (home, back(0, left), back(1, right))
-    grad_tokens, grad_probs = pl.pallas_call(
-        functools.partial(home_kernel, len(parts)),
-        out_shape=(
-            jax.ShapeDtypeStruct((tok_dev, width), BF16),
-            jax.ShapeDtypeStruct(ids_t.shape, BF16),
-        ),
-        in_specs=[ANY] + [VMEM] * (1 + len(parts)),
-        out_specs=(VMEM, VMEM),
-        compiler_params=PARAMS,
-        name="home",
-    )(turn, ids_t, *parts)
+    if groups == 2:
+        shape = lambda *s: jax.ShapeDtypeStruct(s, BF16)
+        *grads, turn, grad_tokens, grad_probs = pl.pallas_call(
+            functools.partial(last_kernel, len(terms), 2, len(parts)),
+            out_shape=(shape(width // 2, ff), shape(width // 2, ff), shape(ff // 2, width), TOKEN)
+            + (shape(tok_dev, width), shape(*ids_t.shape)),
+            in_specs=[VMEM] * (len(terms) + 1 + len(parts)),
+            out_specs=(VMEM,) * 6,
+            compiler_params=PARAMS,
+            name="last",
+        )(*terms, ids_t, *parts)
+    else:
+        grad_tokens, grad_probs = pl.pallas_call(
+            functools.partial(home_kernel, len(parts)),
+            out_shape=(
+                jax.ShapeDtypeStruct((tok_dev, width), BF16),
+                jax.ShapeDtypeStruct(ids_t.shape, BF16),
+            ),
+            in_specs=[ANY] + [VMEM] * (1 + len(parts)),
+            out_specs=(VMEM, VMEM),
+            compiler_params=PARAMS,
+            name="home",
+        )(turn, ids_t, *parts)
     return (
         grad_tokens,
         grad_probs.T,

time: 89.6 us -> 89.3 us (level)
    ppermute x8, waiting for transfers between devices: 21.3 us -> 25.6 us  [on_device(): right = lambda v: lax.ppermute(v, 'expert', hop[1])]
    ppermute x3, waiting for transfers between devices: 14.4 us -> 10.5 us  [on_device(): got = [lax.ppermute(v, 'dp', [(0, 1), (1, 0)]) for v in send]]
    pallas_call x2 -> x1, Pallas kernels: 2.21 us -> 1.55 us  [on_device(): pl.pallas_call(functools.partial(last_kernel, len(terms), 2, len(parts)),...]
  transfers between devices with their start and end apart: 24 -> 24, of which waited for: 11 -> 13; matrix products, arithmetic and copies ran while one was open for 1% -> 1% of each run, Pallas kernels for 23% -> 22%
where the time goes in v6:
time: 89.3 us; the launch traced here: 89 us
  waiting for transfers between devices  38.1 us (43%)
  Pallas kernels  23.5 us (26%)
  starting transfers between devices  22.6 us (25%)
  local copies, waits for them, and re-layouts  3.44 us (4%)
    ppermute x8, waiting for transfers between devices, on_device(): right = lambda v: lax.ppermute(v, 'expert', hop[1])  25.6 us
    pallas_call x5, Pallas kernels, expert(): pl.pallas_call(functools.partial(expert_kernel, halves, half, width, ff,...  17.3 us
    ppermute x8, starting transfers between devices, on_device(): right = lambda v: lax.ppermute(v, 'expert', hop[1])  13.4 us
    ppermute x3, waiting for transfers between devices, on_device(): got = [lax.ppermute(v, 'dp', [(0, 1), (1, 0)]) for v in send]  10.5 us
    ppermute x3, starting transfers between devices, on_device(): got = [lax.ppermute(v, 'dp', [(0, 1), (1, 0)]) for v in send]  4.09 us
    ppermute x8, starting transfers between devices, on_device(): left = lambda v: lax.ppermute(v, 'expert', hop[-1])  3.95 us
    unnamed x8, local copies, waits for them, and re-layouts  3.4 us
    pallas_call x2, Pallas kernels, weight_sums(): pl.pallas_call(functools.partial(weight_kernel, STEPS // parts, away), ou...  2.16 us
  transfers between devices with their start and end apart: 24, of which 13 were waited for; matrix products, arithmetic and copies ran while one was open for 1% of the time, Pallas kernels for 22%

profile of v6, /device:TPU:0, one launch (start us, length us, event | category | flops | bytes accessed | tf_op | source)
XLA Modules:
  0.0 89.0 jit_solution(11787840770950678355)
XLA Ops:
  0.6 0.5 collective-permute-start.1
  1.1 0.1 collective-permute-start.2
  1.2 0.4 collective-permute-start.3
  1.7 1.1 %pack.1 = (bf16[2,65,16,128]{3,2,1,0:T(8,128)(2,1)S(1)}, f32[8,128]{1,0:T(8,128)S(1)}) custom-call(bf16[128,1024]{1,0:T(8,128)(2,1)} %tok_ref.1, bf16[128,1024]{1,0:T(8,128)(2,1)} %cot_ref.1, s32[8,128]{1,0:T(8,128)} %bitcast.15, bf16[8,128]{1,0:T(8,128)(2,1)} %bitcast.17), custom_call_target="tpu_custom_call" | custom-call | tf_op jit(solution)/shard_map/pack/pallas_call | solution.py:315
  2.8 2.7 %collective-permute-start = (bf16[2,65,16,128]{3,2,1,0:T(8,128)(2,1)S(1)}, bf16[2,65,16,128]{3,2,1,0:T(8,128)(2,1)S(1)}, u32[]{:S(2)}, u32[]{:S(2)}) collective-permute-start(bf16[2,65,16,128]{3,2,1,0:T(8,128)(2,1)S(1)} %get-tuple-element.63.refs_1_), channel_id=1, source_target_pairs={{0,4},{1,5},{4,8},{5,9},{8,12},{9,13},{12,14},{13,15},{14,10},{15,... | collective-permute-start | bytes 1597448 | tf_op jit(solution)/shard_map/ppermute | solution.py:305
  5.5 0.0 collective-permute-start.5
  5.5 0.0 collective-permute-done.1.refs_3_
  5.5 0.0 collective-permute-done.2.refs_4_
  5.5 0.0 collective-permute-done.3.refs_5_
  5.5 1.1 %copy-done = bf16[1,1024,384]{2,1,0:T(8,128)(2,1)S(1)} copy-done((bf16[1,1024,384]{2,1,0:T(8,128)(2,1)S(1)}, bf16[1,1024,384]{2,1,0:T(8,128)(2,1)}, u32[]{:S(2)}) %copy-start) | copy-done | bytes 786456
  6.7 1.1 %copy-done.1 = bf16[1,1024,384]{2,1,0:T(8,128)(2,1)S(1)} copy-done((bf16[1,1024,384]{2,1,0:T(8,128)(2,1)S(1)}, bf16[1,1024,384]{2,1,0:T(8,128)(2,1)}, u32[]{:S(2)}) %copy-start.1) | copy-done | bytes 786456
  7.8 1.1 %copy-done.2 = bf16[1,384,1024]{2,1,0:T(8,128)(2,1)S(1)} copy-done((bf16[1,384,1024]{2,1,0:T(8,128)(2,1)S(1)}, bf16[1,384,1024]{2,1,0:T(8,128)(2,1)}, u32[]{:S(2)}) %copy-start.2) | copy-done | bytes 786456
  8.9 1.4 %weights.1.refs_2_.refs_3_ = bf16[2,15360,128]{2,1,0:T(8,128)(2,1)S(1)} custom-call(bf16[1024,384]{1,0:T(8,128)(2,1)S(1)} %bitcast.10, bf16[1024,384]{1,0:T(8,128)(2,1)S(1)} %bitcast.12, bf16[384,1024]{1,0:T(8,128)(2,1)S(1)} %bitcast.14, bf16[1024,384]{1,0:T(8,128)(2,1)S(1)} %collective-permute-done.1.refs_3_, ...), custom_call_target="tpu_custom_call" | custom-call | bytes 9437184 | tf_op jit(solution)/shard_map/weights/pallas_call | solution.py:326
  10.3 2.9 %expert.5 = (bf16[2,33,16,128]{3,2,1,0:T(8,128)(2,1)S(1)}, f32[2,9216,128]{2,1,0:T(8,128)S(1)}, f32[8,128]{1,0:T(8,128)S(1)}) custom-call(f32[8,128]{1,0:T(8,128)S(1)} %get-tuple-element.64.refs_0_, bf16[2,65,16,128]{3,2,1,0:T(8,128)(2,1)S(1)} %get-tuple-element.63.refs_1_, bf16[2,15360,128]{2,1,0:T(8,128)(2,1)S(1)} %weights.1.refs_2_.refs_3_), custom_call_target="tpu_custom_call" | custom-call | flops 1610612736 | bytes 8388608 | tf_op jit(solution)/shard_map/expert/pallas_call | solution.py:351
  13.2 4.9 %collective-permute-done.refs_1_ = bf16[2,65,16,128]{3,2,1,0:T(8,128)(2,1)S(1)} collective-permute-done((bf16[2,65,16,128]{3,2,1,0:T(8,128)(2,1)S(1)}, bf16[2,65,16,128]{3,2,1,0:T(8,128)(2,1)S(1)}, u32[]{:S(2)}, u32[]{:S(2)}) %collective-permute-start) | collective-permute-done | bytes 532512 | tf_op jit(solution)/shard_map/ppermute | solution.py:305
  18.1 1.8 %collective-permute-start.4 = (bf16[2,65,16,128]{3,2,1,0:T(8,128)(2,1)S(1)}, bf16[2,65,16,128]{3,2,1,0:T(8,128)(2,1)S(1)}, u32[]{:S(2)}, u32[]{:S(2)}) collective-permute-start(bf16[2,65,16,128]{3,2,1,0:T(8,128)(2,1)S(1)} %collective-permute-done.refs_1_), channel_id=1, source_target_pairs={{0,4},{1,5},{4,8},{5,9},{8,12},{9,13},{12,14},{13,15},{14,10},{15,... | collective-permute-start | bytes 1597448 | tf_op jit(solution)/shard_map/ppermute | solution.py:305
  19.9 0.0 collective-permute-done.5.refs_2_
  19.9 0.2 collective-permute-start.7
  20.1 4.3 %expert.6 = (bf16[2,33,16,128]{3,2,1,0:T(8,128)(2,1)S(1)}, bf16[2,33,16,128]{3,2,1,0:T(8,128)(2,1)S(1)}, f32[2,9216,128]{2,1,0:T(8,128)S(1)}, f32[8,128]{1,0:T(8,128)S(1)}) custom-call(f32[8,128]{1,0:T(8,128)S(1)} %get-tuple-element.68.refs_0_, bf16[2,65,16,128]{3,2,1,0:T(8,128)(2,1)S(1)} %collective-permute-done.refs_1_, ...), custom_call_target="tpu_custom_call" | custom-call | flops 3221225472 | bytes 8388608 | tf_op jit(solution)/shard_map/expert/pallas_call | solution.py:351
  24.4 7.6 %collective-permute-done.4.refs_1_ = bf16[2,65,16,128]{3,2,1,0:T(8,128)(2,1)S(1)} collective-permute-done((bf16[2,65,16,128]{3,2,1,0:T(8,128)(2,1)S(1)}, bf16[2,65,16,128]{3,2,1,0:T(8,128)(2,1)S(1)}, u32[]{:S(2)}, u32[]{:S(2)}) %collective-permute-start.4) | collective-permute-done | bytes 532512 | tf_op jit(solution)/shard_map/ppermute | solution.py:305
  32.0 1.6 %collective-permute-start.6 = (bf16[2,65,16,128]{3,2,1,0:T(8,128)(2,1)S(1)}, bf16[2,65,16,128]{3,2,1,0:T(8,128)(2,1)S(1)}, u32[]{:S(2)}, u32[]{:S(2)}) collective-permute-start(bf16[2,65,16,128]{3,2,1,0:T(8,128)(2,1)S(1)} %collective-permute-done.4.refs_1_), channel_id=1, source_target_pairs={{0,4},{1,5},{4,8},{5,9},{8,12},{9,13},{12,14},{13,15},{14,10},{15,... | collective-permute-start | bytes 1597448 | tf_op jit(solution)/shard_map/ppermute | solution.py:305
  33.6 0.0 collective-permute-done.7.refs_2_
  33.6 0.4 collective-permute-start.9
  34.0 4.2 %expert.7 = (bf16[2,33,16,128]{3,2,1,0:T(8,128)(2,1)S(1)}, bf16[2,33,16,128]{3,2,1,0:T(8,128)(2,1)S(1)}, f32[2,9216,128]{2,1,0:T(8,128)S(1)}, f32[8,128]{1,0:T(8,128)S(1)}) custom-call(f32[8,128]{1,0:T(8,128)S(1)} %get-tuple-element.74.refs_0_, bf16[2,65,16,128]{3,2,1,0:T(8,128)(2,1)S(1)} %collective-permute-done.4.refs_1_, ...), custom_call_target="tpu_custom_call" | custom-call | flops 3221225472 | bytes 8388608 | tf_op jit(solution)/shard_map/expert/pallas_call | solution.py:351
  38.2 6.7 %collective-permute-done.6.refs_1_ = bf16[2,65,16,128]{3,2,1,0:T(8,128)(2,1)S(1)} collective-permute-done((bf16[2,65,16,128]{3,2,1,0:T(8,128)(2,1)S(1)}, bf16[2,65,16,128]{3,2,1,0:T(8,128)(2,1)S(1)}, u32[]{:S(2)}, u32[]{:S(2)}) %collective-permute-start.6) | collective-permute-done | bytes 532512 | tf_op jit(solution)/shard_map/ppermute | solution.py:305
  45.0 1.1 %collective-permute-done.9.refs_2_ = bf16[2,65,16,128]{3,2,1,0:T(8,128)(2,1)S(1)} collective-permute-done((bf16[2,65,16,128]{3,2,1,0:T(8,128)(2,1)S(1)}, bf16[2,65,16,128]{3,2,1,0:T(8,128)(2,1)S(1)}, u32[]{:S(2)}, u32[]{:S(2)}) %collective-permute-start.9) | collective-permute-done | bytes 532512 | tf_op jit(solution)/shard_map/ppermute | solution.py:306
  46.1 0.7 collective-permute-start.10
  46.8 1.5 %collective-permute-start.8 = (bf16[1,65,16,128]{3,2,1,0:T(8,128)(2,1)S(1)}, bf16[1,65,16,128]{3,2,1,0:T(8,128)(2,1)S(1)}, u32[]{:S(2)}, u32[]{:S(2)}) collective-permute-start(bf16[1,65,16,128]{3,2,1,0:T(8,128)(2,1)S(1)} %slice.24), channel_id=1, source_target_pairs={{0,4},{1,5},{4,8},{5,9},{8,12},{9,13},{12,14},{13,15},{14,10},{15,... | collective-permute-start | bytes 798728 | tf_op jit(solution)/shard_map/ppermute | solution.py:305
  48.3 4.2 %expert.8 = (bf16[2,33,16,128]{3,2,1,0:T(8,128)(2,1)S(1)}, bf16[2,33,16,128]{3,2,1,0:T(8,128)(2,1)S(1)}, f32[2,9216,128]{2,1,0:T(8,128)S(1)}, f32[8,128]{1,0:T(8,128)S(1)}) custom-call(f32[8,128]{1,0:T(8,128)S(1)} %get-tuple-element.81.refs_0_, bf16[2,65,16,128]{3,2,1,0:T(8,128)(2,1)S(1)} %collective-permute-done.6.refs_1_, ...), custom_call_target="tpu_custom_call" | custom-call | flops 3221225472 | bytes 8388608 | tf_op jit(solution)/shard_map/expert/pallas_call | solution.py:351
  52.5 0.1 collective-permute-done.10.refs_2_
  52.6 0.7 collective-permute-done.8.refs_1_
  53.3 1.7 %expert.9 = (bf16[1,33,16,128]{3,2,1,0:T(8,128)(2,1)S(1)}, bf16[1,33,16,128]{3,2,1,0:T(8,128)(2,1)S(1)}, f32[8,128]{1,0:T(8,128)S(1)}, bf16[1024,128]{1,0:T(8,12...) custom-call(f32[8,128]{1,0:T(8,128)S(1)} %get-tuple-element.84.refs_, ...), custom_call_target="tpu_custom_call" | custom-call | flops 1006632960 | bytes 8388608 | tf_op jit(solution)/shard_map/expert/pallas_call | solution.py:351
  54.9 0.8 weight_sums.2
  55.8 0.1 collective-permute-start.12
  55.9 1.5 %collective-permute-start.20 = (bf16[1,33,16,128]{3,2,1,0:T(8,128)(2,1)S(1)}, bf16[1,33,16,128]{3,2,1,0:T(8,128)(2,1)S(1)}, u32[]{:S(2)}, u32[]{:S(2)}) collective-permute-start(bf16[1,33,16,128]{3,2,1,0:T(8,128)(2,1)S(1)} %get-tuple-element.112), channel_id=1, source_target_pairs={{0,4},{1,5},{4,8},{5,9},{8,12},{9,13},{12,14},{13,15},{14,10},{15,... | collective-permute-start | bytes 405512 | tf_op jit(solution)/shard_map/ppermute | solution.py:305
  57.3 0.6 collective-permute-start.16
  57.9 0.8 collective-permute-done.12
  58.7 0.2 add_convert_fusion.1
  58.9 1.4 %collective-permute-start.13 = (bf16[72,16,128]{2,1,0:T(8,128)(2,1)S(1)}, bf16[72,16,128]{2,1,0:T(8,128)(2,1)S(1)}, u32[]{:S(2)}, u32[]{:S(2)}) collective-permute-start(bf16[72,16,128]{2,1,0:T(8,128)(2,1)S(1)} %get-tuple-element.122), channel_id=1, source_target_pairs={{0,16},{16,0},{1,17},{17,1},{2,18},{18,2},{3,19},{19,3},{4,20},{20... | collective-permute-start | bytes 884744 | tf_op jit(solution)/shard_map/ppermute | solution.py:411
  60.2 1.6 %collective-permute-done.20 = bf16[1,33,16,128]{3,2,1,0:T(8,128)(2,1)S(1)} collective-permute-done((bf16[1,33,16,128]{3,2,1,0:T(8,128)(2,1)S(1)}, bf16[1,33,16,128]{3,2,1,0:T(8,128)(2,1)S(1)}, u32[]{:S(2)}, u32[]{:S(2)}) %collective-permute-start.20) | collective-permute-done | bytes 135200 | tf_op jit(solution)/shard_map/ppermute | solution.py:305
  61.9 1.5 %collective-permute-start.21 = (bf16[2,33,16,128]{3,2,1,0:T(8,128)(2,1)S(1)}, bf16[2,33,16,128]{3,2,1,0:T(8,128)(2,1)S(1)}, u32[]{:S(2)}, u32[]{:S(2)}) collective-permute-start(bf16[2,33,16,128]{3,2,1,0:T(8,128)(2,1)S(1)} %add_convert_fusion.5), channel_id=1, source_target_pairs={{0,4},{1,5},{4,8},{5,9},{8,12},{9,13},{12,14},{13,15},{14,10},{15,... | collective-permute-start | bytes 811016 | tf_op jit(solution)/shard_map/ppermute | solution.py:305
  63.4 0.7 collective-permute-start.17
  64.1 1.3 %weight_sums.3 = (bf16[288,16,128]{2,1,0:T(8,128)(2,1)S(1)}, bf16[288,16,128]{2,1,0:T(8,128)(2,1)S(1)}, f32[8,128]{1,0:T(8,128)}) custom-call(f32[8,128]{1,0:T(8,128)S(1)} %get-tuple-element.96.turn_ref, f32[2,9216,128]{2,1,0:T(8,128)S(1)} %get-tuple-element.88.refs_0_, bf16[1024,128]{1,0:T(8,128)(2,1)S(1)} %get-tuple-element.89.refs_1_, ...), custom_call_target="tpu_custom_call" | custom-call | flops 301989888 | bytes 8388608 | tf_op jit(solution)/shard_map/weight_sums/pallas_call | solution.py:205
  65.4 0.0 collective-permute-start.11
  65.4 1.3 %collective-permute-start.14 = (bf16[72,16,128]{2,1,0:T(8,128)(2,1)S(1)}, bf16[72,16,128]{2,1,0:T(8,128)(2,1)S(1)}, u32[]{:S(2)}, u32[]{:S(2)}) collective-permute-start(bf16[72,16,128]{2,1,0:T(8,128)(2,1)S(1)} %get-tuple-element.121), channel_id=1, source_target_pairs={{0,16},{16,0},{1,17},{17,1},{2,18},{18,2},{3,19},{19,3},{4,20},{20... | collective-permute-start | bytes 884744 | tf_op jit(solution)/shard_map/ppermute | solution.py:411
  66.7 1.2 %collective-permute-done.13.refs_2_ = bf16[72,16,128]{2,1,0:T(8,128)(2,1)S(1)} collective-permute-done((bf16[72,16,128]{2,1,0:T(8,128)(2,1)S(1)}, bf16[72,16,128]{2,1,0:T(8,128)(2,1)S(1)}, u32[]{:S(2)}, u32[]{:S(2)}) %collective-permute-start.13) | collective-permute-done | bytes 294944 | tf_op jit(solution)/shard_map/ppermute | solution.py:411
  68.0 2.0 %collective-permute-done.21 = bf16[2,33,16,128]{3,2,1,0:T(8,128)(2,1)S(1)} collective-permute-done((bf16[2,33,16,128]{3,2,1,0:T(8,128)(2,1)S(1)}, bf16[2,33,16,128]{3,2,1,0:T(8,128)(2,1)S(1)}, u32[]{:S(2)}, u32[]{:S(2)}) %collective-permute-start.21) | collective-permute-done | bytes 270368 | tf_op jit(solution)/shard_map/ppermute | solution.py:305
  70.0 0.1 add_convert_fusion.4
  70.1 1.5 %collective-permute-start.22 = (bf16[2,33,16,128]{3,2,1,0:T(8,128)(2,1)S(1)}, bf16[2,33,16,128]{3,2,1,0:T(8,128)(2,1)S(1)}, u32[]{:S(2)}, u32[]{:S(2)}) collective-permute-start(bf16[2,33,16,128]{3,2,1,0:T(8,128)(2,1)S(1)} %add_convert_fusion.4), channel_id=1, source_target_pairs={{0,4},{1,5},{4,8},{5,9},{8,12},{9,13},{12,14},{13,15},{14,10},{15,... | collective-permute-start | bytes 811016 | tf_op jit(solution)/shard_map/ppermute | solution.py:305
  71.5 0.0 collective-permute-done.17
  71.5 0.1 add_convert_fusion.7
  71.6 0.7 collective-permute-start.18
  72.3 0.2 add_convert_fusion
  72.4 0.0 copy-start.3
  72.5 1.4 %collective-permute-start.15 = (bf16[144,16,128]{2,1,0:T(8,128)(2,1)S(1)}, bf16[144,16,128]{2,1,0:T(8,128)(2,1)S(1)}, u32[]{:S(2)}, u32[]{:S(2)}) collective-permute-start(bf16[144,16,128]{2,1,0:T(8,128)(2,1)S(1)} %add_convert_fusion), channel_id=1, source_target_pairs={{0,16},{16,0},{1,17},{17,1},{2,18},{18,2},{3,19},{19,3},{4,20},{20... | collective-permute-start | bytes 1769480 | tf_op jit(solution)/shard_map/ppermute | solution.py:411
  73.8 1.4 %collective-permute-done.14.refs_3_ = bf16[72,16,128]{2,1,0:T(8,128)(2,1)S(1)} collective-permute-done((bf16[72,16,128]{2,1,0:T(8,128)(2,1)S(1)}, bf16[72,16,128]{2,1,0:T(8,128)(2,1)S(1)}, u32[]{:S(2)}, u32[]{:S(2)}) %collective-permute-start.14) | collective-permute-done | bytes 294944 | tf_op jit(solution)/shard_map/ppermute | solution.py:411
  75.2 2.0 %collective-permute-done.22 = bf16[2,33,16,128]{3,2,1,0:T(8,128)(2,1)S(1)} collective-permute-done((bf16[2,33,16,128]{3,2,1,0:T(8,128)(2,1)S(1)}, bf16[2,33,16,128]{3,2,1,0:T(8,128)(2,1)S(1)}, u32[]{:S(2)}, u32[]{:S(2)}) %collective-permute-start.22) | collective-permute-done | bytes 270368 | tf_op jit(solution)/shard_map/ppermute | solution.py:305
  77.3 0.1 add_convert_fusion.3
  77.3 1.5 %collective-permute-start.23 = (bf16[2,33,16,128]{3,2,1,0:T(8,128)(2,1)S(1)}, bf16[2,33,16,128]{3,2,1,0:T(8,128)(2,1)S(1)}, u32[]{:S(2)}, u32[]{:S(2)}) collective-permute-start(bf16[2,33,16,128]{3,2,1,0:T(8,128)(2,1)S(1)} %add_convert_fusion.3), channel_id=1, source_target_pairs={{0,4},{1,5},{4,8},{5,9},{8,12},{9,13},{12,14},{13,15},{14,10},{15,... | collective-permute-start | bytes 811016 | tf_op jit(solution)/shard_map/ppermute | solution.py:305
  78.8 0.1 add_convert_fusion.6
  78.9 0.7 collective-permute-start.19
  79.6 0.0 collective-permute-done.11.refs_1_
  79.6 7.9 %collective-permute-done.15.refs_4_ = bf16[144,16,128]{2,1,0:T(8,128)(2,1)S(1)} collective-permute-done((bf16[144,16,128]{2,1,0:T(8,128)(2,1)S(1)}, bf16[144,16,128]{2,1,0:T(8,128)(2,1)S(1)}, u32[]{:S(2)}, u32[]{:S(2)}) %collective-permute-start.15) | collective-permute-done | bytes 589856 | tf_op jit(solution)/shard_map/ppermute | solution.py:411
  87.5 1.5 %last.1 = (bf16[512,384]{1,0:T(8,128)(2,1)}, bf16[512,384]{1,0:T(8,128)(2,1)}, bf16[192,1024]{1,0:T(8,128)(2,1)}, f32[8,128]{1,0:T(8,128)}, bf16[128,1024]{1,0:T(8,128)(2,1)}, /*index=5*/bf16[8,128]{1,0:T(8,128)(2,1)}) custom-call(bf16[288,16,128]{2,1,0:T(8,128)(2,1)S(1)} %get-tuple-element.97.refs_0_, ...), custom_call_target="tpu_custom_call" | custom-call | tf_op jit(solution)/shard_map/last/pallas_call | solution.py:445
  (12 shorter events, 0.1 us)
Async XLA Ops:
  0.6 4.9 %collective-permute-start.1 = (bf16[1024,384]{1,0:T(8,128)(2,1)}, bf16[1024,384]{1,0:T(8,128)(2,1)S(1)}, u32[]{:S(2)}, u32[]{:S(2)}) collective-permute-start(bf16[1024,384]{1,0:T(8,128)(2,1)} %bitcast.9), channel_id=1, source_target_pairs={{0,1},{1,0},{2,3},{3,2},{4,5},{5,4},{6,7},{7,6},{8,9},{9,8},{10,11... | collective-permute-start | bytes 2359304 | tf_op jit(solution)/shard_map/ppermute | solution.py:307
  1.1 4.3 %collective-permute-start.2 = (bf16[1024,384]{1,0:T(8,128)(2,1)}, bf16[1024,384]{1,0:T(8,128)(2,1)S(1)}, u32[]{:S(2)}, u32[]{:S(2)}) collective-permute-start(bf16[1024,384]{1,0:T(8,128)(2,1)} %bitcast.11), channel_id=1, source_target_pairs={{0,1},{1,0},{2,3},{3,2},{4,5},{5,4},{6,7},{7,6},{8,9},{9,8},{10,11... | collective-permute-start | bytes 2359304 | tf_op jit(solution)/shard_map/ppermute | solution.py:307
  1.2 4.3 %collective-permute-start.3 = (bf16[384,1024]{1,0:T(8,128)(2,1)}, bf16[384,1024]{1,0:T(8,128)(2,1)S(1)}, u32[]{:S(2)}, u32[]{:S(2)}) collective-permute-start(bf16[384,1024]{1,0:T(8,128)(2,1)} %bitcast.13), channel_id=1, source_target_pairs={{0,1},{1,0},{2,3},{3,2},{4,5},{5,4},{6,7},{7,6},{8,9},{9,8},{10,11... | collective-permute-start | bytes 2359304 | tf_op jit(solution)/shard_map/ppermute | solution.py:307
  2.8 15.3 %collective-permute-start = (bf16[2,65,16,128]{3,2,1,0:T(8,128)(2,1)S(1)}, bf16[2,65,16,128]{3,2,1,0:T(8,128)(2,1)S(1)}, u32[]{:S(2)}, u32[]{:S(2)}) collective-permute-start(bf16[2,65,16,128]{3,2,1,0:T(8,128)(2,1)S(1)} %get-tuple-element.63.refs_1_), channel_id=1, source_target_pairs={{0,4},{1,5},{4,8},{5,9},{8,12},{9,13},{12,14},{13,15},{14,10},{15,... | collective-permute-start | bytes 1597448 | tf_op jit(solution)/shard_map/ppermute | solution.py:305
  5.5 14.5 %collective-permute-start.5 = (bf16[2,65,16,128]{3,2,1,0:T(8,128)(2,1)S(1)}, bf16[2,65,16,128]{3,2,1,0:T(8,128)(2,1)S(1)}, u32[]{:S(2)}, u32[]{:S(2)}) collective-permute-start(bf16[2,65,16,128]{3,2,1,0:T(8,128)(2,1)S(1)} %get-tuple-element.63.refs_1_), channel_id=1, source_target_pairs={{0,2},{1,3},{4,0},{5,1},{8,4},{9,5},{12,8},{13,9},{14,12},{15,13},... | collective-permute-start | bytes 1597448 | tf_op jit(solution)/shard_map/ppermute | solution.py:306
  5.5 1.1 %copy-start = (bf16[1,1024,384]{2,1,0:T(8,128)(2,1)S(1)}, bf16[1,1024,384]{2,1,0:T(8,128)(2,1)}, u32[]{:S(2)}) copy-start(bf16[1,1024,384]{2,1,0:T(8,128)(2,1)} %param.11) | copy-start | bytes 2359300
  6.7 1.1 %copy-start.1 = (bf16[1,1024,384]{2,1,0:T(8,128)(2,1)S(1)}, bf16[1,1024,384]{2,1,0:T(8,128)(2,1)}, u32[]{:S(2)}) copy-start(bf16[1,1024,384]{2,1,0:T(8,128)(2,1)} %param.12) | copy-start | bytes 2359300
  7.8 1.1 %copy-start.2 = (bf16[1,384,1024]{2,1,0:T(8,128)(2,1)S(1)}, bf16[1,384,1024]{2,1,0:T(8,128)(2,1)}, u32[]{:S(2)}) copy-start(bf16[1,384,1024]{2,1,0:T(8,128)(2,1)} %param.13) | copy-start | bytes 2359300
  18.1 13.9 %collective-permute-start.4 = (bf16[2,65,16,128]{3,2,1,0:T(8,128)(2,1)S(1)}, bf16[2,65,16,128]{3,2,1,0:T(8,128)(2,1)S(1)}, u32[]{:S(2)}, u32[]{:S(2)}) collective-permute-start(bf16[2,65,16,128]{3,2,1,0:T(8,128)(2,1)S(1)} %collective-permute-done.refs_1_), channel_id=1, source_target_pairs={{0,4},{1,5},{4,8},{5,9},{8,12},{9,13},{12,14},{13,15},{14,10},{15,... | collective-permute-start | bytes 1597448 | tf_op jit(solution)/shard_map/ppermute | solution.py:305
  19.9 13.7 %collective-permute-start.7 = (bf16[2,65,16,128]{3,2,1,0:T(8,128)(2,1)S(1)}, bf16[2,65,16,128]{3,2,1,0:T(8,128)(2,1)S(1)}, u32[]{:S(2)}, u32[]{:S(2)}) collective-permute-start(bf16[2,65,16,128]{3,2,1,0:T(8,128)(2,1)S(1)} %collective-permute-done.5.refs_2_), channel_id=1, source_target_pairs={{0,2},{1,3},{4,0},{5,1},{8,4},{9,5},{12,8},{13,9},{14,12},{15,13},... | collective-permute-start | bytes 1597448 | tf_op jit(solution)/shard_map/ppermute | solution.py:306
  32.0 13.0 %collective-permute-start.6 = (bf16[2,65,16,128]{3,2,1,0:T(8,128)(2,1)S(1)}, bf16[2,65,16,128]{3,2,1,0:T(8,128)(2,1)S(1)}, u32[]{:S(2)}, u32[]{:S(2)}) collective-permute-start(bf16[2,65,16,128]{3,2,1,0:T(8,128)(2,1)S(1)} %collective-permute-done.4.refs_1_), channel_id=1, source_target_pairs={{0,4},{1,5},{4,8},{5,9},{8,12},{9,13},{12,14},{13,15},{14,10},{15,... | collective-permute-start | bytes 1597448 | tf_op jit(solution)/shard_map/ppermute | solution.py:305
  33.6 12.5 %collective-permute-start.9 = (bf16[2,65,16,128]{3,2,1,0:T(8,128)(2,1)S(1)}, bf16[2,65,16,128]{3,2,1,0:T(8,128)(2,1)S(1)}, u32[]{:S(2)}, u32[]{:S(2)}) collective-permute-start(bf16[2,65,16,128]{3,2,1,0:T(8,128)(2,1)S(1)} %collective-permute-done.7.refs_2_), channel_id=1, source_target_pairs={{0,2},{1,3},{4,0},{5,1},{8,4},{9,5},{12,8},{13,9},{14,12},{15,13},... | collective-permute-start | bytes 1597448 | tf_op jit(solution)/shard_map/ppermute | solution.py:306
  46.1 6.5 %collective-permute-start.10 = (bf16[1,65,16,128]{3,2,1,0:T(8,128)(2,1)S(1)}, bf16[1,65,16,128]{3,2,1,0:T(8,128)(2,1)S(1)}, u32[]{:S(2)}, u32[]{:S(2)}) collective-permute-start(bf16[1,65,16,128]{3,2,1,0:T(8,128)(2,1)S(1)} %slice.25), channel_id=1, source_target_pairs={{0,2},{1,3},{4,0},{5,1},{8,4},{9,5},{12,8},{13,9},{14,12},{15,13},... | collective-permute-start | bytes 798728 | tf_op jit(solution)/shard_map/ppermute | solution.py:306
  46.8 6.5 %collective-permute-start.8 = (bf16[1,65,16,128]{3,2,1,0:T(8,128)(2,1)S(1)}, bf16[1,65,16,128]{3,2,1,0:T(8,128)(2,1)S(1)}, u32[]{:S(2)}, u32[]{:S(2)}) collective-permute-start(bf16[1,65,16,128]{3,2,1,0:T(8,128)(2,1)S(1)} %slice.24), channel_id=1, source_target_pairs={{0,4},{1,5},{4,8},{5,9},{8,12},{9,13},{12,14},{13,15},{14,10},{15,... | collective-permute-start | bytes 798728 | tf_op jit(solution)/shard_map/ppermute | solution.py:305
  55.8 2.9 %collective-permute-start.12 = (bf16[288,16,128]{2,1,0:T(8,128)(2,1)S(1)}, bf16[288,16,128]{2,1,0:T(8,128)(2,1)S(1)}, u32[]{:S(2)}, u32[]{:S(2)}) collective-permute-start(bf16[288,16,128]{2,1,0:T(8,128)(2,1)S(1)} %get-tuple-element.102), channel_id=1, source_target_pairs={{0,1},{1,0},{2,3},{3,2},{4,5},{5,4},{6,7},{7,6},{8,9},{9,8},{10,11... | collective-permute-start | bytes 3538952 | tf_op jit(solution)/shard_map/ppermute | solution.py:307
  55.9 6.0 %collective-permute-start.20 = (bf16[1,33,16,128]{3,2,1,0:T(8,128)(2,1)S(1)}, bf16[1,33,16,128]{3,2,1,0:T(8,128)(2,1)S(1)}, u32[]{:S(2)}, u32[]{:S(2)}) collective-permute-start(bf16[1,33,16,128]{3,2,1,0:T(8,128)(2,1)S(1)} %get-tuple-element.112), channel_id=1, source_target_pairs={{0,4},{1,5},{4,8},{5,9},{8,12},{9,13},{12,14},{13,15},{14,10},{15,... | collective-permute-start | bytes 405512 | tf_op jit(solution)/shard_map/ppermute | solution.py:305
  57.3 6.0 %collective-permute-start.16 = (bf16[1,33,16,128]{3,2,1,0:T(8,128)(2,1)S(1)}, bf16[1,33,16,128]{3,2,1,0:T(8,128)(2,1)S(1)}, u32[]{:S(2)}, u32[]{:S(2)}) collective-permute-start(bf16[1,33,16,128]{3,2,1,0:T(8,128)(2,1)S(1)} %get-tuple-element.108), channel_id=1, source_target_pairs={{0,2},{1,3},{4,0},{5,1},{8,4},{9,5},{12,8},{13,9},{14,12},{15,13},... | collective-permute-start | bytes 405512 | tf_op jit(solution)/shard_map/ppermute | solution.py:306
  58.9 9.1 %collective-permute-start.13 = (bf16[72,16,128]{2,1,0:T(8,128)(2,1)S(1)}, bf16[72,16,128]{2,1,0:T(8,128)(2,1)S(1)}, u32[]{:S(2)}, u32[]{:S(2)}) collective-permute-start(bf16[72,16,128]{2,1,0:T(8,128)(2,1)S(1)} %get-tuple-element.122), channel_id=1, source_target_pairs={{0,16},{16,0},{1,17},{17,1},{2,18},{18,2},{3,19},{19,3},{4,20},{20... | collective-permute-start | bytes 884744 | tf_op jit(solution)/shard_map/ppermute | solution.py:411
  61.9 8.1 %collective-permute-start.21 = (bf16[2,33,16,128]{3,2,1,0:T(8,128)(2,1)S(1)}, bf16[2,33,16,128]{3,2,1,0:T(8,128)(2,1)S(1)}, u32[]{:S(2)}, u32[]{:S(2)}) collective-permute-start(bf16[2,33,16,128]{3,2,1,0:T(8,128)(2,1)S(1)} %add_convert_fusion.5), channel_id=1, source_target_pairs={{0,4},{1,5},{4,8},{5,9},{8,12},{9,13},{12,14},{13,15},{14,10},{15,... | collective-permute-start | bytes 811016 | tf_op jit(solution)/shard_map/ppermute | solution.py:305
  63.4 8.1 %collective-permute-start.17 = (bf16[2,33,16,128]{3,2,1,0:T(8,128)(2,1)S(1)}, bf16[2,33,16,128]{3,2,1,0:T(8,128)(2,1)S(1)}, u32[]{:S(2)}, u32[]{:S(2)}) collective-permute-start(bf16[2,33,16,128]{3,2,1,0:T(8,128)(2,1)S(1)} %add_convert_fusion.8), channel_id=1, source_target_pairs={{0,2},{1,3},{4,0},{5,1},{8,4},{9,5},{12,8},{13,9},{14,12},{15,13},... | collective-permute-start | bytes 811016 | tf_op jit(solution)/shard_map/ppermute | solution.py:306
  65.4 14.2 %collective-permute-start.11 = (bf16[288,16,128]{2,1,0:T(8,128)(2,1)S(1)}, bf16[288,16,128]{2,1,0:T(8,128)(2,1)S(1)}, u32[]{:S(2)}, u32[]{:S(2)}) collective-permute-start(bf16[288,16,128]{2,1,0:T(8,128)(2,1)S(1)} %get-tuple-element.98), channel_id=1, source_target_pairs={{0,1},{1,0},{2,3},{3,2},{4,5},{5,4},{6,7},{7,6},{8,9},{9,8},{10,11... | collective-permute-start | bytes 3538952 | tf_op jit(solution)/shard_map/ppermute | solution.py:307
  65.4 9.8 %collective-permute-start.14 = (bf16[72,16,128]{2,1,0:T(8,128)(2,1)S(1)}, bf16[72,16,128]{2,1,0:T(8,128)(2,1)S(1)}, u32[]{:S(2)}, u32[]{:S(2)}) collective-permute-start(bf16[72,16,128]{2,1,0:T(8,128)(2,1)S(1)} %get-tuple-element.121), channel_id=1, source_target_pairs={{0,16},{16,0},{1,17},{17,1},{2,18},{18,2},{3,19},{19,3},{4,20},{20... | collective-permute-start | bytes 884744 | tf_op jit(solution)/shard_map/ppermute | solution.py:411
  70.1 7.2 %collective-permute-start.22 = (bf16[2,33,16,128]{3,2,1,0:T(8,128)(2,1)S(1)}, bf16[2,33,16,128]{3,2,1,0:T(8,128)(2,1)S(1)}, u32[]{:S(2)}, u32[]{:S(2)}) collective-permute-start(bf16[2,33,16,128]{3,2,1,0:T(8,128)(2,1)S(1)} %add_convert_fusion.4), channel_id=1, source_target_pairs={{0,4},{1,5},{4,8},{5,9},{8,12},{9,13},{12,14},{13,15},{14,10},{15,... | collective-permute-start | bytes 811016 | tf_op jit(solution)/shard_map/ppermute | solution.py:305
  71.6 7.2 %collective-permute-start.18 = (bf16[2,33,16,128]{3,2,1,0:T(8,128)(2,1)S(1)}, bf16[2,33,16,128]{3,2,1,0:T(8,128)(2,1)S(1)}, u32[]{:S(2)}, u32[]{:S(2)}) collective-permute-start(bf16[2,33,16,128]{3,2,1,0:T(8,128)(2,1)S(1)} %add_convert_fusion.7), channel_id=1, source_target_pairs={{0,2},{1,3},{4,0},{5,1},{8,4},{9,5},{12,8},{13,9},{14,12},{15,13},... | collective-permute-start | bytes 811016 | tf_op jit(solution)/shard_map/ppermute | solution.py:306
  72.4 15.0 %copy-start.3 = (s32[128,8]{0,1:T(8,128)S(1)}, s32[128,8]{0,1:T(8,128)}, u32[]{:S(2)}) copy-start(s32[128,8]{0,1:T(8,128)} %param.9) | copy-start | bytes 12292
  72.5 15.0 %collective-permute-start.15 = (bf16[144,16,128]{2,1,0:T(8,128)(2,1)S(1)}, bf16[144,16,128]{2,1,0:T(8,128)(2,1)S(1)}, u32[]{:S(2)}, u32[]{:S(2)}) collective-permute-start(bf16[144,16,128]{2,1,0:T(8,128)(2,1)S(1)} %add_convert_fusion), channel_id=1, source_target_pairs={{0,16},{16,0},{1,17},{17,1},{2,18},{18,2},{3,19},{19,3},{4,20},{20... | collective-permute-start | bytes 1769480 | tf_op jit(solution)/shard_map/ppermute | solution.py:411
  77.3 10.1 %collective-permute-start.23 = (bf16[2,33,16,128]{3,2,1,0:T(8,128)(2,1)S(1)}, bf16[2,33,16,128]{3,2,1,0:T(8,128)(2,1)S(1)}, u32[]{:S(2)}, u32[]{:S(2)}) collective-permute-start(bf16[2,33,16,128]{3,2,1,0:T(8,128)(2,1)S(1)} %add_convert_fusion.3), channel_id=1, source_target_pairs={{0,4},{1,5},{4,8},{5,9},{8,12},{9,13},{12,14},{13,15},{14,10},{15,... | collective-permute-start | bytes 811016 | tf_op jit(solution)/shard_map/ppermute | solution.py:305
  78.9 8.6 %collective-permute-start.19 = (bf16[2,33,16,128]{3,2,1,0:T(8,128)(2,1)S(1)}, bf16[2,33,16,128]{3,2,1,0:T(8,128)(2,1)S(1)}, u32[]{:S(2)}, u32[]{:S(2)}) collective-permute-start(bf16[2,33,16,128]{3,2,1,0:T(8,128)(2,1)S(1)} %add_convert_fusion.6), channel_id=1, source_target_pairs={{0,2},{1,3},{4,0},{5,1},{8,4},{9,5},{12,8},{13,9},{14,12},{15,13},... | collective-permute-start | bytes 811016 | tf_op jit(solution)/shard_map/ppermute | solution.py:306
